TPU v7x, 32 devices: a whole 2x2x4 slice. The times are simulated.
32 devices in a mesh: fsdp: 4 (over z), rep: 8 (over y, x, core).
Axes of the slice: x: 2, y: 2, z: 4, core: 2. Of those that a mesh axis runs over, the one named last changes fastest.
Arguments:
- gradients: bfloat16 [8, 8, 360, 3584], P('rep', None, 'fsdp'), may hold values from -6 to 6
- momentum: float32 [8, 360, 3584], P('rep', 'fsdp')
- offsets: int32 [8, 5], P('rep'), may hold values from 0 to 288, as said below
Outputs:
- kept_state: float32 [8, 360, 3584], P('rep', 'fsdp')
- update: bfloat16 [8, 360, 3584], P('rep', 'fsdp')
Inputs may be any that keep to these rules, and one draw needn't show every extreme that they name: offsets[k, 0] = 0 and offsets[k, 4] = 288; offsets never fall; every index of fsdp holds between 54 and 90 rows of each matrix, and in every matrix some index holds exactly 90.
All inputs are finite; a program needn't handle non-finite values.
Results may differ from a plain program's by a relative error of at most 0.024.
Values may be sent and summed in bfloat16 or wider, within the bound.
No kernel may reach another device: no remote copies, remote signals or barrier semaphores. Data moves between devices by JAX's collectives and lax.ppermute only.
A program may use at most 64 MiB of HBM per device.

v0:
```python
import math

import jax
import jax.numpy as jnp
from jax import lax
from jax.sharding import PartitionSpec as P

D = 3584
ROWS = 288
ITERS = 3


momentum_rate = 0.95
coef_a = 3.4445
coef_b = -4.775
coef_c = 2.0315


def orthogonalize(matrix):
    values = matrix.astype(jnp.float32)
    frob_norm = jnp.sqrt(jnp.sum(values * values))
    iterate = (values / (frob_norm + 1e-07)).astype(jnp.bfloat16)
    for iteration in range(ITERS):
        gram_matrix = lax.dot_general(
            iterate, iterate, (((1,), (1,)), ((), ())), preferred_element_type=jnp.float32
        ).astype(jnp.bfloat16)
        gram_square = jnp.dot(gram_matrix, gram_matrix, preferred_element_type=jnp.float32)
        polynomial = (coef_b * gram_matrix.astype(jnp.float32) + coef_c * gram_square).astype(
            jnp.bfloat16
        )
        iterate = (
            coef_a * iterate.astype(jnp.float32)
            + jnp.dot(polynomial, iterate, preferred_element_type=jnp.float32)
        ).astype(jnp.bfloat16)
    return iterate


def per_device(gradients, momentum, offsets):
    groups = lax.axis_size("fsdp")
    capacity = momentum.shape[1]
    summed = lax.psum_scatter(
        gradients[0].astype(jnp.float32).astype(jnp.bfloat16),
        "rep",
        scatter_dimension=0,
        tiled=True,
    ).astype(jnp.float32)
    mean_grad = summed[0] / lax.axis_size("rep")
    bounds = offsets[0]
    device = lax.axis_index("fsdp")
    first_row = lax.dynamic_index_in_dim(bounds, device, 0, keepdims=False)
    row_count = lax.dynamic_index_in_dim(bounds, device + 1, 0, keepdims=False) - first_row
    slot_index = jnp.arange(capacity, dtype=jnp.int32)
    live_slot = slot_index < row_count
    buffer_new = momentum_rate * momentum[0] + mean_grad
    kept_state = jnp.where(live_slot[:, None], buffer_new, 0.0)
    nesterov = (mean_grad + momentum_rate * buffer_new).astype(jnp.bfloat16)
    shards = lax.all_gather(nesterov, "fsdp", axis=0, tiled=True)
    position = jnp.arange(ROWS, dtype=jnp.int32)
    holder = jnp.sum((bounds[None, 1:groups] <= position[:, None]).astype(jnp.int32), axis=1)
    full_matrix = jnp.take(shards, holder * capacity + position - jnp.take(bounds, holder), axis=0)
    owner_index = lax.axis_index("rep") % groups
    all_slots = jnp.arange(groups * capacity, dtype=jnp.int32)
    slot_holder = all_slots // capacity
    slot_within = all_slots % capacity
    slot_counts = jnp.take(bounds, slot_holder + 1) - jnp.take(bounds, slot_holder)
    slot_live = slot_within < slot_counts
    slot_source = jnp.clip(jnp.take(bounds, slot_holder) + slot_within, 0, ROWS - 1)

    def solve_and_place(matrix):
        orthogonal = orthogonalize(matrix)
        packed = jnp.take(orthogonal, slot_source, axis=0)
        return jnp.where(slot_live[:, None], packed, jnp.zeros_like(packed))

    def empty_slots(matrix):
        return jnp.zeros((groups * capacity, matrix.shape[1]), jnp.bfloat16)

    packed_rows = lax.cond(device == owner_index, solve_and_place, empty_slots, full_matrix)
    own_rows = lax.psum_scatter(
        packed_rows.astype(jnp.float32).astype(jnp.bfloat16),
        "fsdp",
        scatter_dimension=0,
        tiled=True,
    )
    placed = own_rows.astype(jnp.float32) * math.sqrt(D)
    update = jnp.where(live_slot[:, None], placed, 0.0).astype(jnp.bfloat16)
    return (kept_state[None], update[None])


def solution(mesh):
    placed = (P("rep", None, "fsdp", None), P("rep", "fsdp", None), P("rep", None))
    return jax.shard_map(
        per_device,
        mesh=mesh,
        in_specs=placed,
        out_specs=(P("rep", "fsdp", None), P("rep", "fsdp", None)),
        check_vma=False,
    )
```

profile of v0, /device:TPU:0, one launch (start us, length us, event | category | flops | bytes accessed | tf_op | source)
XLA Modules:
  0.0 239.8 jit_solution(1668010575932960031)
XLA Ops:
  7.2 6.4 %copy.23 = bf16[1,8,90,3584]{3,2,1,0:T(8,128)(2,1)} copy(bf16[1,8,90,3584]{3,1,2,0:T(8,128)(2,1)} %param.7) | data formatting | bytes 10321920 | tf_op args[0]
  13.7 60.6 %reduce-scatter.4.cloned.1.call-done = bf16[1,90,3584]{2,1,0:T(8,128)(2,1)} async-done(((bf16[8,90,3584]{2,1,0:T(8,128)(2,1)}), bf16[1,90,3584]{2,1,0:T(8,128)(2,1)}) %reduce-scatter.4.cloned.1.call-update) | async-done | bytes 645136 | tf_op jit(solution)/shard_map/reduce_scatter | solution.py:41
  74.3 2.2 fusion.47
  80.8 52.9 %all-gather.3.cloned.1.call-done = bf16[4,90,3584]{2,1,0:T(8,128)(2,1)} async-done(((bf16[1,90,3584]{2,1,0:T(8,128)(2,1)}), bf16[4,90,3584]{2,1,0:T(8,128)(2,1)}) %all-gather.3.cloned.1.call-update) | async-done | bytes 2580496 | tf_op jit(solution)/shard_map/all_gather | solution.py:57
  137.0 38.4 %conditional.1 = (bf16[360,3584]{1,0:T(8,128)(2,1)S(1)}) conditional(s32[]{:T(128)} %convert_element_type.142, () %tuple.71, (s32[360]{0:T(512)S(1)}, s32[360]{0:T(512)S(1)}, s32[360]{0:T(512)S(1)}, pred[360]{0:T(512)(128)(4,1)S(1)}, pred[360]{0:T(512)(128)(4,1)S(1)}, /*index=5*/s32[360]{0:T(512)S(1)}, s32[360]{0:T(512)S(1)}, ...), branch_computations={%region_2.4_spmd, %region_3.6_spmd.clone.clone} | conditional | flops 3735328000 | bytes 61962488 | solution.py:77
  137.9 3.3 %fusion.42 = (s32[288]{0:T(512)S(1)}, s32[288]{0:T(512)S(1)}) fusion(s32[]{:T(128)} %bitcast.28, s32[]{:T(128)} %bitcast.27, s32[]{:T(128)} %bitcast.26, s32[]{:T(128)} %bitcast.25, s32[]{:T(128)} %bitcast.24, s32[]{:T(128)} %get-tuple-element.451, s32[]{:T(128)} %get-tuple-element.455, s32[288]{0:T(512)S(1)} %get-tuple-element.454, ...), kind=kLoop, calls=%fused_computation.76 | loop fusion | flops 6048 | bytes 4636 | tf_op jit(solution)/shard_map/jit(_take)/gather | solution.py:60
  141.2 2.5 %reshape.174 = bf16[360,3584]{1,0:T(8,128)(2,1)S(1)} reshape(bf16[4,90,3584]{2,1,0:T(8,128)(2,1)} %get-tuple-element.456) | data formatting | bytes 5160960 | tf_op jit(solution)/shard_map/cond
  143.6 3.6 %gather_fusion = bf16[288,3584]{1,0:T(8,128)(2,1)} fusion(bf16[360,3584]{1,0:T(8,128)(2,1)S(1)} %reshape.174, s32[1024]{0:T(1024)S(1)} %pad_clamp_fusion.1), kind=kCustom, calls=%fused_computation.clone | custom fusion | bytes 4129920 | tf_op jit(solution)/shard_map/jit(_take)/gather | solution.py:60
  147.3 3.5 %fusion.4 = f32[]{:T(128)} fusion(bf16[288,3584]{1,0:T(8,128)(2,1)} %gather_fusion, pred[288]{0:T(512)(128)(4,1)S(1)} %compare_and_fusion.2), kind=kLoop, calls=%fused_computation.10 | loop fusion | flops 4128767 | bytes 2064676 | tf_op jit(solution)/shard_map/cond/branch_1_fun/reduce_sum | solution.py:21
  152.1 1.3 copy-done.2
  153.4 1.2 convolution_convert_fusion.2
  154.7 3.6 %fusion.1 = bf16[288,3584]{1,0:T(8,128)(2,1)S(1)} fusion(bf16[288,3584]{1,0:T(8,128)(2,1)} %copy-done.2, bf16[288,288]{1,0:T(8,128)(2,1)S(1)} %convolution_convert_fusion.2), kind=kOutput, calls=%fused_computation.5 | convolution fusion | flops 646861824 | bytes 4294656 | tf_op jit(solution)/shard_map/cond/branch_1_fun/dot_general | solution.py:33
  158.3 1.2 convolution_convert_fusion.1
  159.6 2.8 %fusion.2 = bf16[288,3584]{1,0:T(8,128)(2,1)} fusion(bf16[288,3584]{1,0:T(8,128)(2,1)S(1)} %fusion.1, bf16[288,288]{1,0:T(8,128)(2,1)S(1)} %convolution_convert_fusion.1), kind=kOutput, calls=%fused_computation.6 | convolution fusion | flops 646861824 | bytes 4294656 | tf_op jit(solution)/shard_map/cond/branch_1_fun/dot_general | solution.py:33
  162.4 3.4 %convolution_convert_fusion = bf16[288,288]{1,0:T(8,128)(2,1)S(1)} fusion(bf16[288,3584]{1,0:T(8,128)(2,1)} %fusion.2), kind=kOutput, calls=%fused_computation.23 | convolution fusion | flops 594625536 | bytes 2230272 | tf_op jit(solution)/shard_map/cond/branch_1_fun/dot_general | solution.py:24
  165.8 3.6 %fusion.3 = bf16[288,3584]{1,0:T(8,128)(2,1)S(1)} fusion(bf16[288,3584]{1,0:T(8,128)(2,1)} %fusion.2, bf16[288,288]{1,0:T(8,128)(2,1)S(1)} %convolution_convert_fusion), kind=kOutput, calls=%fused_computation.7 | convolution fusion | flops 646861824 | bytes 4294656 | tf_op jit(solution)/shard_map/cond/branch_1_fun/dot_general | solution.py:33
  169.5 3.8 %gather_fusion.1 = bf16[360,3584]{1,0:T(8,128)(2,1)} fusion(bf16[288,3584]{1,0:T(8,128)(2,1)S(1)} %fusion.3, s32[1024]{0:T(1024)S(1)} %pad_clamp_fusion), kind=kCustom, calls=%fused_computation.1.clone | custom fusion | bytes 5162400 | tf_op jit(solution)/shard_map/cond/branch_1_fun/jit(_take)/gather | solution.py:71
  173.3 2.1 select_select_fusion
  175.5 45.8 %fusion = bf16[96,3584]{1,0:T(8,128)(2,1)S(1)} fusion(bf16[360,3584]{1,0:T(8,128)(2,1)S(1)} %get-tuple-element.547), kind=kCustom, calls=%all-reduce-scatter | all-reduce-scatter fusion | flops 1376257 | bytes 3269120
  221.4 4.4 %collective-permute-start = (bf16[18,3584]{1,0:T(8,128)(2,1)S(1)}, bf16[18,3584]{1,0:T(8,128)(2,1)S(1)}, u32[]{:S(2)}, u32[]{:S(2)}) collective-permute-start(bf16[18,3584]{1,0:T(8,128)(2,1)S(1)} %slice.42), channel_id=1, source_target_pairs={{0,8},{8,16},{16,24},{1,9},{9,17},{17,25},{2,10},{10,18},{18,26},{... | collective-permute-start | bytes 387080
  225.8 1.8 add_select_fusion.2
  227.6 2.4 copy.14
  229.9 1.9 concatenate
  231.8 1.1 fusion.46
  (44 shorter events, 7.0 us)
Async XLA Ops:
  7.2 67.1 %reduce-scatter.4.cloned.1.call-start = ((), (), s32[]{:S(2)}) async-start(), calls=%async_computation.1 | async-start | bytes 6193152 | tf_op jit(solution)/shard_map/reduce_scatter | solution.py:41
  13.6 60.7 %copy-start.1 = (f32[1,90,3584]{2,0,1:T(1,128)S(1)}, f32[1,90,3584]{2,0,1:T(1,128)}, u32[]{:S(2)}) copy-start(f32[1,90,3584]{2,0,1:T(1,128)} %param.8) | copy-start | bytes 3870724
  13.6 63.0 %copy-start.3 = (s32[1,5]{1,0:T(1,128)S(1)}, s32[1,5]{1,0:T(1,128)}, u32[]{:S(2)}) copy-start(s32[1,5]{1,0:T(1,128)} %param.9) | copy-start | bytes 64
  13.6 65.0 %copy-start.4 = (u32[32]{0:T(128)S(1)}, u32[32]{0:T(128)}, u32[]{:S(2)}) copy-start(u32[32]{0:T(128)} %constant.215) | copy-start | bytes 388
  13.6 120.1 %all-gather.3.cloned.1.call-start = ((), (), s32[]{:S(2)}) async-start(), calls=%async_computation.2 | async-start | bytes 3440640 | tf_op jit(solution)/shard_map/all_gather | solution.py:57
  147.3 4.2 %copy-start = (bf16[288,3584]{1,0:T(8,128)(2,1)S(1)}, bf16[288,3584]{1,0:T(8,128)(2,1)}, u32[]{:S(2)}) copy-start(bf16[288,3584]{1,0:T(8,128)(2,1)} %gather_fusion) | copy-start | bytes 6193156 | tf_op jit(solution)/shard_map/cond
  152.1 1.3 copy-start.2
  221.4 8.6 %collective-permute-start = (bf16[18,3584]{1,0:T(8,128)(2,1)S(1)}, bf16[18,3584]{1,0:T(8,128)(2,1)S(1)}, u32[]{:S(2)}, u32[]{:S(2)}) collective-permute-start(bf16[18,3584]{1,0:T(8,128)(2,1)S(1)} %slice.42), channel_id=1, source_target_pairs={{0,8},{8,16},{16,24},{1,9},{9,17},{17,25},{2,10},{10,18},{18,26},{... | collective-permute-start | bytes 387080
Sparse Core Ops, SparseCore 0:
  13.7 60.5 reduce-scatter.3
  76.7 56.9 all-gather.2
where the time goes:
time: 240 us
  waiting for transfers between devices  114 us (48%)
  blocking collectives  45.8 us (19%)
  local copies, waits for them, and re-layouts  27.8 us (12%)
  between operations  16.3 us (7%)
  matrix products  16 us (7%)
  other arithmetic  14.8 us (6%)
  starting transfers between devices  4.47 us (2%)
    reduce_scatter x1, waiting for transfers between devices, per_device(): lax.psum_scatter(gradients[0].astype(jnp.float32).astype(jnp.bfloat16), '...  60.6 us
    all_gather x1, waiting for transfers between devices, per_device(): shards = lax.all_gather(nesterov, 'fsdp', axis=0, tiled=True)  52.9 us
    unnamed x1, blocking collectives  45.8 us
    unnamed x11, local copies, waits for them, and re-layouts  11.3 us
    dot_general x3, matrix products, orthogonalize(): jnp.dot(polynomial, iterate, preferred_element_type=jnp.float32)  10.1 us
    dot_general x3, matrix products, orthogonalize(): lax.dot_general(iterate, iterate, (((1,), (1,)), ((), ())), preferred_ele...  5.92 us
  transfers between devices with their start and end apart: 3, of which 2 were waited for; matrix products, arithmetic and copies ran while one was open for 3% of the time, Pallas kernels for 0%

commit v1 on v0

v1 whole, which is shorter than its diff:
```python
import functools
import math

import jax
import jax.numpy as jnp
from jax import lax
from jax.experimental import pallas as pl
from jax.experimental.pallas import tpu as pltpu
from jax.sharding import PartitionSpec as P

ITERS = 3
CHUNKS = 2

momentum_rate = 0.95
coef_a = 3.4445
coef_b = -4.775
coef_c = 2.0315

AXES = ("fsdp", "rep")
VMEM_LIMIT = 32 * 1024 * 1024
bf16 = jnp.bfloat16
f32 = jnp.float32


def split_kernel(mats, cap, me_ref, x_ref, keep_ref, send_ref):
    me = me_ref[0]
    rows = min(256 // mats, cap)
    half = mats // 2
    padded = keep_ref.shape[1]
    size = rows * mats
    out_row = lax.broadcasted_iota(jnp.int32, (size, size), 0)
    in_row = lax.broadcasted_iota(jnp.int32, (size, size), 1)
    place = out_row // rows
    within = out_row - place * rows
    j = jnp.where(place < half, 2 * place, 2 * (place - half) + 1)
    matrix = jnp.bitwise_xor(j, me)
    blocks = -(-cap // rows)
    for block in range(blocks):
        first = block * rows
        start = min(first, cap - rows)
        source = (within + (first - start)) * mats + matrix
        chosen = (in_row == source) & (within < cap - first)
        moved = jnp.dot(
            chosen.astype(f32).astype(bf16),
            x_ref[start * mats : start * mats + size, :],
            preferred_element_type=f32,
        )
        moved = moved.reshape(mats, rows, moved.shape[1])
        here = min(rows, padded - first)
        keep_ref[:, first : first + here, :] = moved[:half, :here].astype(bf16)
        send_ref[:, first : first + here, :] = moved[half:, :here].astype(bf16)
    done = blocks * rows
    if done < padded:
        zeros = jnp.zeros((half, padded - done, keep_ref.shape[2]), bf16)
        keep_ref[:, done:, :] = zeros
        send_ref[:, done:, :] = zeros


def split(me, flat, mats, cap, padded, first, width):
    half = mats // 2
    out = jax.ShapeDtypeStruct((half, padded, width), bf16)
    tile = 128
    while tile * 2 <= 512 and width % (tile * 2) == 0:
        tile *= 2
    offset = first // tile
    return pl.pallas_call(
        functools.partial(split_kernel, mats, cap),
        grid=(width // tile,),
        out_shape=(out, out),
        in_specs=[
            pl.BlockSpec(memory_space=pltpu.SMEM),
            pl.BlockSpec((flat.shape[0], tile), lambda i: (0, i + offset)),
        ],
        out_specs=[pl.BlockSpec((half, padded, tile), lambda i: (0, 0, i))] * 2,
        compiler_params=pltpu.CompilerParams(vmem_limit_bytes=VMEM_LIMIT),
        cost_estimate=pl.CostEstimate(
            flops=2 * flat.shape[0] * 256 * width,
            bytes_accessed=4 * flat.shape[0] * width,
            transcendentals=0,
        ),
    )(me, flat)


def dot(left, right):
    return jnp.dot(left, right, preferred_element_type=f32)


def gram_of(parts, stack_ref):
    rows = parts[0].shape[0]
    for i, part in enumerate(parts):
        stack_ref[i * rows : (i + 1) * rows, :] = part[...]
    return lax.dot_general(
        stack_ref[...], stack_ref[...], (((1,), (1,)), ((), ())), preferred_element_type=f32
    )


def gram_kernel(*refs):
    *parts, out_ref, stack_ref = refs
    out_ref[...] = gram_of(parts, stack_ref)


def two(value):
    high = value.astype(bf16)
    return high, (value - high.astype(f32)).astype(bf16)


def chain_kernel(width, earlier, *refs):
    sums, parts = refs[:earlier], refs[earlier:-4]
    high_ref, low_ref, alpha_ref, stack_ref = refs[-4:]
    gram = gram_of(parts, stack_ref)
    for earlier_ref in sums:
        gram = gram + earlier_ref[...]
    size = gram.shape[0]
    diagonal = lax.broadcasted_iota(jnp.int32, (size, size), 0) == lax.broadcasted_iota(
        jnp.int32, (size, size), 1
    )
    trace = jnp.sum(jnp.where(diagonal, gram, 0.0), keepdims=True)
    scale = 1.0 / (jnp.sqrt(trace) + 1e-07)
    gram = (gram * scale) * scale
    rest = None
    power = 1.0
    for iteration in range(ITERS):
        rounded = gram.astype(bf16)
        square = dot(rounded, rounded)
        poly = (coef_b * rounded.astype(f32) + coef_c * square).astype(bf16)
        if rest is None:
            rest = poly.astype(f32)
        else:
            rest_high, rest_low = two(rest)
            rest = (
                coef_a * rest
                + power * poly.astype(f32)
                + (dot(poly, rest_high) + dot(poly, rest_low))
            )
        power = power * coef_a
        if iteration < ITERS - 1:
            gram_high, gram_low = two(gram)
            left = coef_a * gram + (dot(poly, gram_high) + dot(poly, gram_low))
            left_high, left_low = two(left)
            gram = coef_a * left + (dot(left_high, poly) + dot(left_low, poly))
    scale = scale * math.sqrt(width)
    high, low = two(rest * scale)
    high_ref[...] = high
    low_ref[...] = low
    alpha_ref[...] = jnp.broadcast_to(scale * power, alpha_ref.shape)


def apply_kernel(groups, *refs):
    high_ref, low_ref, alpha_ref = refs[:3]
    parts, outs, stack_ref = refs[3 : 3 + groups], refs[3 + groups : -1], refs[-1]
    rows = parts[0].shape[0]
    for i, part in enumerate(parts):
        stack_ref[i * rows : (i + 1) * rows, :] = part[...]
    alpha = alpha_ref[0:1, 0:1]
    stack = stack_ref[...]
    result = dot(high_ref[...], stack) + dot(low_ref[...], stack)
    result = result + alpha * stack.astype(f32)
    for i, out in enumerate(outs):
        out[...] = result[i * rows : (i + 1) * rows, :].astype(bf16)


def whole(count):
    return [pl.BlockSpec(memory_space=pltpu.VMEM)] * count


def gram_call(parts):
    size = len(parts) * parts[0].shape[0]
    width = parts[0].shape[1]
    return pl.pallas_call(
        gram_kernel,
        out_shape=jax.ShapeDtypeStruct((size, size), f32),
        in_specs=whole(len(parts)),
        out_specs=pl.BlockSpec(memory_space=pltpu.VMEM),
        scratch_shapes=[pltpu.VMEM((size, width), bf16)],
        compiler_params=pltpu.CompilerParams(vmem_limit_bytes=VMEM_LIMIT),
        cost_estimate=pl.CostEstimate(
            flops=2 * size * size * width, bytes_accessed=2 * size * width, transcendentals=0
        ),
    )(*parts)


def chain_call(full_width, sums, parts):
    size = len(parts) * parts[0].shape[0]
    width = parts[0].shape[1]
    return pl.pallas_call(
        functools.partial(chain_kernel, full_width, len(sums)),
        out_shape=(
            jax.ShapeDtypeStruct((size, size), bf16),
            jax.ShapeDtypeStruct((size, size), bf16),
            jax.ShapeDtypeStruct((8, 128), f32),
        ),
        in_specs=whole(len(sums) + len(parts)),
        out_specs=whole(3),
        scratch_shapes=[pltpu.VMEM((size, width), bf16)],
        compiler_params=pltpu.CompilerParams(vmem_limit_bytes=VMEM_LIMIT),
        cost_estimate=pl.CostEstimate(
            flops=2 * size * size * (width + 14 * size),
            bytes_accessed=2 * size * width,
            transcendentals=0,
        ),
    )(*sums, *parts)


def apply_call(factors, parts):
    groups = len(parts)
    rows, width = parts[0].shape
    size = groups * rows
    return pl.pallas_call(
        functools.partial(apply_kernel, groups),
        out_shape=tuple(jax.ShapeDtypeStruct((rows, width), bf16) for _ in range(groups)),
        in_specs=whole(3 + groups),
        out_specs=whole(groups),
        scratch_shapes=[pltpu.VMEM((size, width), bf16)],
        compiler_params=pltpu.CompilerParams(vmem_limit_bytes=VMEM_LIMIT),
        cost_estimate=pl.CostEstimate(
            flops=4 * size * size * width, bytes_accessed=4 * size * width, transcendentals=0
        ),
    )(*factors, *parts)


def per_device(groups, replicas, gradients, momentum, offsets):
    _, mats, cap, width = gradients.shape
    padded = -(-cap // 16) * 16
    fsdp = lax.axis_index("fsdp")
    me = lax.axis_index("rep")
    bits = [1 << i for i in range(replicas.bit_length() - 1)]

    def swap(value, bit):
        pairs = [(f * replicas + r, f * replicas + (r ^ bit)) for f in range(groups) for r in range(replicas)]
        return lax.ppermute(value, AXES, pairs)

    def owner(r):
        return (groups - 1) // 2 + (r & 1)

    def sources(r):
        return [f for f in range(groups) if f != owner(r)]

    def to_owner(value, k):
        pairs = [(sources(r)[k] * replicas + r, owner(r) * replicas + r) for r in range(replicas)]
        return lax.ppermute(value, AXES, pairs)

    def from_owner(value, k):
        pairs = [(owner(r) * replicas + r, sources(r)[k] * replicas + r) for r in range(replicas)]
        return lax.ppermute(value, AXES, pairs)

    flat = jnp.transpose(gradients[0], (1, 0, 2)).reshape(cap * mats, width)
    me_array = me.astype(jnp.int32).reshape(1)

    def total(terms, places):
        return sum(jnp.stack([term[p] for p in places]).astype(f32) for term in terms)

    part = width // (2 * CHUNKS)
    orders = [bits[1:], bits[1:][::-1]]
    state = {}
    for chunk in range(CHUNKS):
        for side in range(2):
            first = (chunk * 2 + side) * part
            keep, send = split(me_array, flat, mats, cap, padded, first, part)
            state[chunk, side] = ([2 * i for i in range(mats // 2)], [keep, swap(send, 1)])
    for level in range(len(bits) - 1):
        for chunk in range(CHUNKS):
            for side in range(2):
                js, terms = state[chunk, side]
                bit = orders[side][level]
                away = [p for p, j in enumerate(js) if j & bit]
                stay = [p for p, j in enumerate(js) if not j & bit]
                got = swap(total(terms, away).astype(bf16), bit)
                terms = [jnp.stack([term[p] for p in stay]) for term in terms] + [got]
                state[chunk, side] = ([js[p] for p in stay], terms)

    bounds = offsets[0]
    count = lax.dynamic_index_in_dim(bounds, fsdp + 1, 0, keepdims=False) - lax.dynamic_index_in_dim(
        bounds, fsdp, 0, keepdims=False
    )
    live = (jnp.arange(padded, dtype=jnp.int32) < count)[:, None]
    old = jnp.pad(momentum[0], ((0, padded - cap), (0, 0)))
    kept, nests = [], []
    for chunk in range(CHUNKS):
        for side in range(2):
            first = (chunk * 2 + side) * part
            _, terms = state[chunk, side]
            mean_grad = total(terms, [0])[0] / replicas
            buffer_new = momentum_rate * old[:, first : first + part] + mean_grad
            kept.append(jnp.where(live, buffer_new, 0.0)[:cap])
            nests.append(jnp.where(live, mean_grad + momentum_rate * buffer_new, 0.0).astype(bf16))
    kept_state = jnp.concatenate(kept, axis=1)

    held = []
    for chunk in range(CHUNKS):
        own = jnp.concatenate(nests[2 * chunk : 2 * chunk + 2], axis=1)
        held.append([own] + [to_owner(own, k) for k in range(groups - 1)])
    sums = [gram_call(parts) for parts in held[:-1]]
    factors = chain_call(width, sums, held[-1])
    is_owner = fsdp == (groups - 1) // 2 + (me & 1)
    rows = []
    for parts in held:
        own, *others = apply_call(factors, parts)
        back = [from_owner(other, k) for k, other in enumerate(others)]
        rows.append(jnp.where(is_owner, own, sum(back[1:], back[0]))[:cap])
    update = jnp.concatenate(rows, axis=1)
    return (kept_state[None], update[None])


def solution(mesh):
    placed = (P("rep", None, "fsdp", None), P("rep", "fsdp", None), P("rep", None))
    return jax.shard_map(
        functools.partial(per_device, mesh.shape["fsdp"], mesh.shape["rep"]),
        mesh=mesh,
        in_specs=placed,
        out_specs=(P("rep", "fsdp", None), P("rep", "fsdp", None)),
        check_vma=False,
    )
```

time: 240 us -> 108 us (0.45)
  waiting for transfers between devices: 114 us -> 31.2 us
  blocking collectives: 45.8 us -> 0 us
  starting transfers between devices: 4.47 us -> 28.1 us
  Pallas kernels: 0 us -> 22.7 us
  local copies, waits for them, and re-layouts: 27.8 us -> 10.1 us
  matrix products: 16 us -> 0 us
  between operations: 16.3 us -> 2.26 us
    reduce_scatter x1 -> x0, waiting for transfers between devices: 60.6 us -> none  [per_device(): lax.psum_scatter(gradients[0].astype(jnp.float32).astype(jnp.bfloat16), '...]
    all_gather x1 -> x0, waiting for transfers between devices: 52.9 us -> none  [per_device(): shards = lax.all_gather(nesterov, 'fsdp', axis=0, tiled=True)]
    unnamed x1 -> x0, blocking collectives: 45.8 us -> none
    ppermute x0 -> x24, waiting for transfers between devices: none -> 31.2 us  [the longest x6 16.2 us: from_owner(): return lax.ppermute(value, AXES, pairs)]
    ppermute x0 -> x24, starting transfers between devices: none -> 28.1 us  [the longest x12 13.7 us: swap(): return lax.ppermute(value, AXES, pairs)]
    pallas_call x0 -> x8, Pallas kernels: none -> 22.7 us  [the longest x4 14 us: split(): pl.pallas_call(functools.partial(split_kernel, mats, cap), grid=(width //...]
    dot_general x6 -> x0, matrix products: 16 us -> none  [the longest x3 10.1 us: orthogonalize(): jnp.dot(polynomial, iterate, preferred_element_type=jnp.float32)]
    gather x9 -> x0, local copies, waits for them, and re-layouts: 12 us -> none  [the longest x6 3.88 us: per_device(): jnp.take(bounds, slot_holder + 1) - jnp.take(bounds, slot_holder)]
  transfers between devices with their start and end apart: 3 -> 24, of which waited for: 2 -> 8; matrix products, arithmetic and copies ran while one was open for 3% -> 18% of each run, Pallas kernels for 0% -> 12%
where the time goes in v1:
time: 108 us; the launch traced here: 107 us
  waiting for transfers between devices  31.2 us (29%)
  starting transfers between devices  28.1 us (26%)
  Pallas kernels  22.7 us (21%)
  other arithmetic  12.9 us (12%)
  local copies, waits for them, and re-layouts  10.1 us (9%)
  between operations  2.26 us (2%)
    ppermute x6, waiting for transfers between devices, from_owner(): return lax.ppermute(value, AXES, pairs)  16.2 us
    pallas_call x4, Pallas kernels, split(): pl.pallas_call(functools.partial(split_kernel, mats, cap), grid=(width //...  14 us
    ppermute x12, starting transfers between devices, swap(): return lax.ppermute(value, AXES, pairs)  13.7 us
    ppermute x12, waiting for transfers between devices, swap(): return lax.ppermute(value, AXES, pairs)  9.98 us
    ppermute x6, starting transfers between devices, to_owner(): return lax.ppermute(value, AXES, pairs)  8.95 us
    unnamed x8, local copies, waits for them, and re-layouts  7.38 us
    convert_element_type x8, other arithmetic, per_device(): got = swap(total(terms, away).astype(bf16), bit)  6.26 us
    ppermute x6, starting transfers between devices, from_owner(): return lax.ppermute(value, AXES, pairs)  5.5 us
  transfers between devices with their start and end apart: 24, of which 8 were waited for; matrix products, arithmetic and copies ran while one was open for 18% of the time, Pallas kernels for 12%

profile of v1, /device:TPU:0, one launch (start us, length us, event | category | flops | bytes accessed | tf_op | source)
XLA Modules:
  0.0 107.3 jit_solution(14887427786047321128)
XLA Ops:
  0.6 2.5 %copy-done = bf16[1,8,90,3584]{3,1,2,0:T(8,128)(2,1)S(1)} copy-done((bf16[1,8,90,3584]{3,1,2,0:T(8,128)(2,1)S(1)}, bf16[1,8,90,3584]{3,1,2,0:T(8,128)(2,1)}, u32[]{:S(2)}) %copy-start) | copy-done | bytes 5160984
  3.1 3.8 %shard_map.50 = (bf16[4,96,896]{2,1,0:T(8,128)(2,1)S(1)}, bf16[4,96,896]{2,1,0:T(8,128)(2,1)}) custom-call(s32[1]{0:T(128)} %bitcast.1.me_ref, bf16[720,3584]{1,0:T(8,128)(2,1)S(1)} %bitcast.47), custom_call_target="tpu_custom_call" | custom-call | flops 330301440 | bytes 2580480 | tf_op jit(solution)/shard_map/pallas_call | solution.py:66
  7.4 3.8 %shard_map.52 = (bf16[4,96,896]{2,1,0:T(8,128)(2,1)S(1)}, bf16[4,96,896]{2,1,0:T(8,128)(2,1)}) custom-call(s32[1]{0:T(128)} %bitcast.1.me_ref, bf16[720,3584]{1,0:T(8,128)(2,1)S(1)} %bitcast.48), custom_call_target="tpu_custom_call" | custom-call | flops 330301440 | bytes 2580480 | tf_op jit(solution)/shard_map/pallas_call | solution.py:66
  11.3 3.9 %shard_map.51 = (bf16[4,96,896]{2,1,0:T(8,128)(2,1)S(1)}, bf16[4,96,896]{2,1,0:T(8,128)(2,1)}) custom-call(s32[1]{0:T(128)} %bitcast.1.me_ref, bf16[720,3584]{1,0:T(8,128)(2,1)S(1)} %bitcast.49), custom_call_target="tpu_custom_call" | custom-call | flops 330301440 | bytes 2580480 | tf_op jit(solution)/shard_map/pallas_call | solution.py:66
  15.6 2.4 %shard_map.53 = (bf16[4,96,896]{2,1,0:T(8,128)(2,1)S(1)}, bf16[4,96,896]{2,1,0:T(8,128)(2,1)S(1)}) custom-call(s32[1]{0:T(128)} %bitcast.1.me_ref, bf16[720,3584]{1,0:T(8,128)(2,1)S(1)} %bitcast.50), custom_call_target="tpu_custom_call" | custom-call | flops 330301440 | bytes 2580480 | tf_op jit(solution)/shard_map/pallas_call | solution.py:66
  18.2 2.5 %copy.8 = f32[1,90,3584]{2,1,0:T(8,128)} copy(f32[1,90,3584]{2,0,1:T(1,128)} %param.4) | data formatting | bytes 2580480
  23.9 3.0 %collective-permute-start.1 = (bf16[2,96,896]{2,1,0:T(8,128)(2,1)S(1)}, bf16[2,96,896]{2,1,0:T(8,128)(2,1)S(1)}, u32[]{:S(2)}, u32[]{:S(2)}) collective-permute-start(bf16[2,96,896]{2,1,0:T(8,128)(2,1)S(1)} %add_convert_fusion.3), channel_id=1, source_target_pairs={{0,2},{1,3},{2,0},{3,1},{4,6},{5,7},{6,4},{7,5},{8,10},{9,11},{10,... | collective-permute-start | bytes 1032200 | tf_op jit(solution)/shard_map/ppermute | solution.py:230
  29.2 2.1 %collective-permute-start.4 = (bf16[2,96,896]{2,1,0:T(8,128)(2,1)S(1)}, bf16[2,96,896]{2,1,0:T(8,128)(2,1)S(1)}, u32[]{:S(2)}, u32[]{:S(2)}) collective-permute-start(bf16[2,96,896]{2,1,0:T(8,128)(2,1)S(1)} %add_convert_fusion.2), channel_id=1, source_target_pairs={{0,4},{1,5},{2,6},{3,7},{4,0},{5,1},{6,2},{7,3},{8,12},{9,13},{10,... | collective-permute-start | bytes 1032200 | tf_op jit(solution)/shard_map/ppermute | solution.py:230
  32.4 3.3 %collective-permute-done.1 = bf16[2,96,896]{2,1,0:T(8,128)(2,1)S(1)} collective-permute-done((bf16[2,96,896]{2,1,0:T(8,128)(2,1)S(1)}, bf16[2,96,896]{2,1,0:T(8,128)(2,1)S(1)}, u32[]{:S(2)}, u32[]{:S(2)}) %collective-permute-start.1) | collective-permute-done | bytes 344096 | tf_op jit(solution)/shard_map/ppermute | solution.py:230
  36.7 2.2 %collective-permute-start.2 = (bf16[1,96,896]{2,1,0:T(8,128)(2,1)S(1)}, bf16[1,96,896]{2,1,0:T(8,128)(2,1)S(1)}, u32[]{:S(2)}, u32[]{:S(2)}) collective-permute-start(bf16[1,96,896]{2,1,0:T(8,128)(2,1)S(1)} %add_convert_fusion.7), channel_id=1, source_target_pairs={{0,4},{1,5},{2,6},{3,7},{4,0},{5,1},{6,2},{7,3},{8,12},{9,13},{10,... | collective-permute-start | bytes 516104 | tf_op jit(solution)/shard_map/ppermute | solution.py:230
  38.9 3.6 %collective-permute-done.7 = bf16[2,96,896]{2,1,0:T(8,128)(2,1)S(1)} collective-permute-done((bf16[2,96,896]{2,1,0:T(8,128)(2,1)S(1)}, bf16[2,96,896]{2,1,0:T(8,128)(2,1)S(1)}, u32[]{:S(2)}, u32[]{:S(2)}) %collective-permute-start.7) | collective-permute-done | bytes 344096 | tf_op jit(solution)/shard_map/ppermute | solution.py:230
  43.5 1.8 %collective-permute-start.8 = (bf16[1,96,896]{2,1,0:T(8,128)(2,1)S(1)}, bf16[1,96,896]{2,1,0:T(8,128)(2,1)S(1)}, u32[]{:S(2)}, u32[]{:S(2)}) collective-permute-start(bf16[1,96,896]{2,1,0:T(8,128)(2,1)S(1)} %add_convert_fusion.5), channel_id=1, source_target_pairs={{0,4},{1,5},{2,6},{3,7},{4,0},{5,1},{6,2},{7,3},{8,12},{9,13},{10,... | collective-permute-start | bytes 516104 | tf_op jit(solution)/shard_map/ppermute | solution.py:230
  48.9 1.8 %collective-permute-start.11 = (bf16[1,96,896]{2,1,0:T(8,128)(2,1)S(1)}, bf16[1,96,896]{2,1,0:T(8,128)(2,1)S(1)}, u32[]{:S(2)}, u32[]{:S(2)}) collective-permute-start(bf16[1,96,896]{2,1,0:T(8,128)(2,1)S(1)} %add_convert_fusion.4), channel_id=1, source_target_pairs={{0,2},{1,3},{2,0},{3,1},{4,6},{5,7},{6,4},{7,5},{8,10},{9,11},{10,... | collective-permute-start | bytes 516104 | tf_op jit(solution)/shard_map/ppermute | solution.py:230
  51.3 2.4 %collective-permute-done.8 = bf16[1,96,896]{2,1,0:T(8,128)(2,1)S(1)} collective-permute-done((bf16[1,96,896]{2,1,0:T(8,128)(2,1)S(1)}, bf16[1,96,896]{2,1,0:T(8,128)(2,1)S(1)}, u32[]{:S(2)}, u32[]{:S(2)}) %collective-permute-start.8) | collective-permute-done | bytes 172064 | tf_op jit(solution)/shard_map/ppermute | solution.py:230
  53.7 2.3 %fusion.15 = (bf16[96,896]{1,0:T(8,128)(2,1)S(1)}, f32[96,896]{1,0:T(8,128)S(1)}, bf16[96,896]{1,0:T(8,128)(2,1)S(1)}, f32[96,896]{1,0:T(8,128)S(1)}, bf16[96,896]{1,0:T(8,128)(2,1)S(1)}, /*index=5*/f32[96,896]{1,0:T(8,128)}) fusion(pred[96]{0:T(512)(128)(4,1)S(1)} %iota_compare_fusion, bf16[1,96,896]{2,1,0:T(8,128)(2,1)S(1)} %collective-permute-done.2, ...), kind=kLoop, calls=%fused_computation.42 | loop fusion | flops 3612672 | bytes 4903008 | tf_op jit(solution)/shard_map/convert_element_type | solution.py:285
  56.0 3.7 %collective-permute-start.12 = (bf16[96,1792]{1,0:T(8,128)(2,1)S(1)}, bf16[96,1792]{1,0:T(8,128)(2,1)S(1)}, u32[]{:S(2)}, u32[]{:S(2)}) collective-permute-start(bf16[96,1792]{1,0:T(8,128)(2,1)S(1)} %pad_maximum_fusion.refs_0_.refs_3_), channel_id=1, source_target_pairs={{0,8},{1,17},{2,10},{3,19},{4,12},{5,21},{6,14},{7,23}} | collective-permute-start | bytes 1032200 | tf_op jit(solution)/shard_map/ppermute | solution.py:240
  61.2 1.8 %fusion.9 = (bf16[96,896]{1,0:T(8,128)(2,1)S(1)}, f32[96,896]{1,0:T(8,128)}) fusion(pred[96]{0:T(512)(128)(4,1)S(1)} %iota_compare_fusion, bf16[1,96,896]{2,1,0:T(8,128)(2,1)S(1)} %collective-permute-done.11, bf16[2,96,896]{2,1,0:T(8,128)(2,1)S(1)} %collective-permute-done.10, bf16[4,96,896]{2,1,0:T(8,128)(2,1)} %collective-permute-done.9, ...), kind=kLoop, calls=%fused_computation.33 | loop fusion | flops 1204224 | bytes 2494560 | tf_op jit(solution)/shard_map/convert_element_type | solution.py:285
  63.0 2.5 %collective-permute-start.15 = (bf16[96,1792]{1,0:T(8,128)(2,1)S(1)}, bf16[96,1792]{1,0:T(8,128)(2,1)S(1)}, u32[]{:S(2)}, u32[]{:S(2)}) collective-permute-start(bf16[96,1792]{1,0:T(8,128)(2,1)S(1)} %pad_maximum_fusion.1.refs_1_.refs_3_), channel_id=1, source_target_pairs={{0,8},{1,17},{2,10},{3,19},{4,12},{5,21},{6,14},{7,23}} | collective-permute-start | bytes 1032200 | tf_op jit(solution)/shard_map/ppermute | solution.py:240
  66.2 2.0 %collective-permute-done.12.refs_1_.refs_4_ = bf16[96,1792]{1,0:T(8,128)(2,1)S(1)} collective-permute-done((bf16[96,1792]{1,0:T(8,128)(2,1)S(1)}, bf16[96,1792]{1,0:T(8,128)(2,1)S(1)}, u32[]{:S(2)}, u32[]{:S(2)}) %collective-permute-start.12) | collective-permute-done | bytes 344096 | tf_op jit(solution)/shard_map/ppermute | solution.py:240
  71.1 3.0 %collective-permute-done.15.refs_2_.refs_4_ = bf16[96,1792]{1,0:T(8,128)(2,1)S(1)} collective-permute-done((bf16[96,1792]{1,0:T(8,128)(2,1)S(1)}, bf16[96,1792]{1,0:T(8,128)(2,1)S(1)}, u32[]{:S(2)}, u32[]{:S(2)}) %collective-permute-start.15) | collective-permute-done | bytes 344096 | tf_op jit(solution)/shard_map/ppermute | solution.py:240
  74.1 4.6 %shard_map.55 = (bf16[384,384]{1,0:T(8,128)(2,1)S(1)}, bf16[384,384]{1,0:T(8,128)(2,1)S(1)}, f32[8,128]{1,0:T(8,128)S(1)}) custom-call(f32[384,384]{1,0:T(8,128)S(1)} %shard_map.54.refs_0_, bf16[96,1792]{1,0:T(8,128)(2,1)S(1)} %pad_maximum_fusion.1.refs_1_.refs_3_, bf16[96,1792]{1,0:T(8,128)(2,1)S(1)} %collective-permute-done.15.refs_2_.refs_4_, ...), custom_call_target="tpu_custom_call" | custom-call | flops 2113929216 | bytes 1376256 | tf_op jit(solution)/shard_map/pallas_call | solution.py:185
  83.4 2.4 %copy.5 = f32[1,90,3584]{2,0,1:T(1,128)} copy(f32[1,90,3584]{2,1,0:T(8,128)S(1)} %maximum_bitcast_fusion) | data formatting | bytes 2580480
  90.1 8.0 %collective-permute-done.21 = bf16[96,1792]{1,0:T(8,128)(2,1)S(1)} collective-permute-done((bf16[96,1792]{1,0:T(8,128)(2,1)S(1)}, bf16[96,1792]{1,0:T(8,128)(2,1)S(1)}, u32[]{:S(2)}, u32[]{:S(2)}) %collective-permute-start.21) | collective-permute-done | bytes 344096 | tf_op jit(solution)/shard_map/ppermute | solution.py:244
  98.2 8.1 %collective-permute-done.18 = bf16[96,1792]{1,0:T(8,128)(2,1)S(1)} collective-permute-done((bf16[96,1792]{1,0:T(8,128)(2,1)S(1)}, bf16[96,1792]{1,0:T(8,128)(2,1)S(1)}, u32[]{:S(2)}, u32[]{:S(2)}) %collective-permute-start.18) | collective-permute-done | bytes 344096 | tf_op jit(solution)/shard_map/ppermute | solution.py:244
  (63 shorter events, 27.3 us)
Async XLA Ops:
  6.9 15.8 %collective-permute-start = (bf16[4,96,896]{2,1,0:T(8,128)(2,1)}, bf16[4,96,896]{2,1,0:T(8,128)(2,1)}, u32[]{:S(2)}, u32[]{:S(2)}) collective-permute-start(bf16[4,96,896]{2,1,0:T(8,128)(2,1)} %get-tuple-element.22), channel_id=1, source_target_pairs={{0,1},{1,0},{2,3},{3,2},{4,5},{5,4},{6,7},{7,6},{8,9},{9,8},{10,11... | collective-permute-start | bytes 2064392 | tf_op jit(solution)/shard_map/ppermute | solution.py:230
  11.2 15.7 %collective-permute-start.6 = (bf16[4,96,896]{2,1,0:T(8,128)(2,1)}, bf16[4,96,896]{2,1,0:T(8,128)(2,1)}, u32[]{:S(2)}, u32[]{:S(2)}) collective-permute-start(bf16[4,96,896]{2,1,0:T(8,128)(2,1)} %get-tuple-element.26), channel_id=1, source_target_pairs={{0,1},{1,0},{2,3},{3,2},{4,5},{5,4},{6,7},{7,6},{8,9},{9,8},{10,11... | collective-permute-start | bytes 2064392 | tf_op jit(solution)/shard_map/ppermute | solution.py:230
  15.1 13.0 %collective-permute-start.3 = (bf16[4,96,896]{2,1,0:T(8,128)(2,1)}, bf16[4,96,896]{2,1,0:T(8,128)(2,1)}, u32[]{:S(2)}, u32[]{:S(2)}) collective-permute-start(bf16[4,96,896]{2,1,0:T(8,128)(2,1)} %get-tuple-element.24), channel_id=1, source_target_pairs={{0,1},{1,0},{2,3},{3,2},{4,5},{5,4},{6,7},{7,6},{8,9},{9,8},{10,11... | collective-permute-start | bytes 2064392 | tf_op jit(solution)/shard_map/ppermute | solution.py:230
  18.0 13.2 %collective-permute-start.9 = (bf16[4,96,896]{2,1,0:T(8,128)(2,1)S(1)}, bf16[4,96,896]{2,1,0:T(8,128)(2,1)}, u32[]{:S(2)}, u32[]{:S(2)}) collective-permute-start(bf16[4,96,896]{2,1,0:T(8,128)(2,1)S(1)} %get-tuple-element.28), channel_id=1, source_target_pairs={{0,1},{1,0},{2,3},{3,2},{4,5},{5,4},{6,7},{7,6},{8,9},{9,8},{10,11... | collective-permute-start | bytes 2064392 | tf_op jit(solution)/shard_map/ppermute | solution.py:230
  23.9 11.9 %collective-permute-start.1 = (bf16[2,96,896]{2,1,0:T(8,128)(2,1)S(1)}, bf16[2,96,896]{2,1,0:T(8,128)(2,1)S(1)}, u32[]{:S(2)}, u32[]{:S(2)}) collective-permute-start(bf16[2,96,896]{2,1,0:T(8,128)(2,1)S(1)} %add_convert_fusion.3), channel_id=1, source_target_pairs={{0,2},{1,3},{2,0},{3,1},{4,6},{5,7},{6,4},{7,5},{8,10},{9,11},{10,... | collective-permute-start | bytes 1032200 | tf_op jit(solution)/shard_map/ppermute | solution.py:230
  28.0 14.5 %collective-permute-start.7 = (bf16[2,96,896]{2,1,0:T(8,128)(2,1)S(1)}, bf16[2,96,896]{2,1,0:T(8,128)(2,1)S(1)}, u32[]{:S(2)}, u32[]{:S(2)}) collective-permute-start(bf16[2,96,896]{2,1,0:T(8,128)(2,1)S(1)} %add_convert_fusion.1), channel_id=1, source_target_pairs={{0,2},{1,3},{2,0},{3,1},{4,6},{5,7},{6,4},{7,5},{8,10},{9,11},{10,... | collective-permute-start | bytes 1032200 | tf_op jit(solution)/shard_map/ppermute | solution.py:230
  29.2 16.2 %collective-permute-start.4 = (bf16[2,96,896]{2,1,0:T(8,128)(2,1)S(1)}, bf16[2,96,896]{2,1,0:T(8,128)(2,1)S(1)}, u32[]{:S(2)}, u32[]{:S(2)}) collective-permute-start(bf16[2,96,896]{2,1,0:T(8,128)(2,1)S(1)} %add_convert_fusion.2), channel_id=1, source_target_pairs={{0,4},{1,5},{2,6},{3,7},{4,0},{5,1},{6,2},{7,3},{8,12},{9,13},{10,... | collective-permute-start | bytes 1032200 | tf_op jit(solution)/shard_map/ppermute | solution.py:230
  32.3 15.5 %collective-permute-start.10 = (bf16[2,96,896]{2,1,0:T(8,128)(2,1)S(1)}, bf16[2,96,896]{2,1,0:T(8,128)(2,1)S(1)}, u32[]{:S(2)}, u32[]{:S(2)}) collective-permute-start(bf16[2,96,896]{2,1,0:T(8,128)(2,1)S(1)} %add_convert_fusion), channel_id=1, source_target_pairs={{0,4},{1,5},{2,6},{3,7},{4,0},{5,1},{6,2},{7,3},{8,12},{9,13},{10,... | collective-permute-start | bytes 1032200 | tf_op jit(solution)/shard_map/ppermute | solution.py:230
  36.7 14.5 %collective-permute-start.2 = (bf16[1,96,896]{2,1,0:T(8,128)(2,1)S(1)}, bf16[1,96,896]{2,1,0:T(8,128)(2,1)S(1)}, u32[]{:S(2)}, u32[]{:S(2)}) collective-permute-start(bf16[1,96,896]{2,1,0:T(8,128)(2,1)S(1)} %add_convert_fusion.7), channel_id=1, source_target_pairs={{0,4},{1,5},{2,6},{3,7},{4,0},{5,1},{6,2},{7,3},{8,12},{9,13},{10,... | collective-permute-start | bytes 516104 | tf_op jit(solution)/shard_map/ppermute | solution.py:230
  43.5 10.2 %collective-permute-start.8 = (bf16[1,96,896]{2,1,0:T(8,128)(2,1)S(1)}, bf16[1,96,896]{2,1,0:T(8,128)(2,1)S(1)}, u32[]{:S(2)}, u32[]{:S(2)}) collective-permute-start(bf16[1,96,896]{2,1,0:T(8,128)(2,1)S(1)} %add_convert_fusion.5), channel_id=1, source_target_pairs={{0,4},{1,5},{2,6},{3,7},{4,0},{5,1},{6,2},{7,3},{8,12},{9,13},{10,... | collective-permute-start | bytes 516104 | tf_op jit(solution)/shard_map/ppermute | solution.py:230
  46.3 7.4 %collective-permute-start.5 = (bf16[1,96,896]{2,1,0:T(8,128)(2,1)S(1)}, bf16[1,96,896]{2,1,0:T(8,128)(2,1)S(1)}, u32[]{:S(2)}, u32[]{:S(2)}) collective-permute-start(bf16[1,96,896]{2,1,0:T(8,128)(2,1)S(1)} %add_convert_fusion.6), channel_id=1, source_target_pairs={{0,2},{1,3},{2,0},{3,1},{4,6},{5,7},{6,4},{7,5},{8,10},{9,11},{10,... | collective-permute-start | bytes 516104 | tf_op jit(solution)/shard_map/ppermute | solution.py:230
  48.9 12.3 %collective-permute-start.11 = (bf16[1,96,896]{2,1,0:T(8,128)(2,1)S(1)}, bf16[1,96,896]{2,1,0:T(8,128)(2,1)S(1)}, u32[]{:S(2)}, u32[]{:S(2)}) collective-permute-start(bf16[1,96,896]{2,1,0:T(8,128)(2,1)S(1)} %add_convert_fusion.4), channel_id=1, source_target_pairs={{0,2},{1,3},{2,0},{3,1},{4,6},{5,7},{6,4},{7,5},{8,10},{9,11},{10,... | collective-permute-start | bytes 516104 | tf_op jit(solution)/shard_map/ppermute | solution.py:230
  56.0 12.2 %collective-permute-start.12 = (bf16[96,1792]{1,0:T(8,128)(2,1)S(1)}, bf16[96,1792]{1,0:T(8,128)(2,1)S(1)}, u32[]{:S(2)}, u32[]{:S(2)}) collective-permute-start(bf16[96,1792]{1,0:T(8,128)(2,1)S(1)} %pad_maximum_fusion.refs_0_.refs_3_), channel_id=1, source_target_pairs={{0,8},{1,17},{2,10},{3,19},{4,12},{5,21},{6,14},{7,23}} | collective-permute-start | bytes 1032200 | tf_op jit(solution)/shard_map/ppermute | solution.py:240
  59.8 10.4 %collective-permute-start.13 = (bf16[96,1792]{1,0:T(8,128)(2,1)S(1)}, bf16[96,1792]{1,0:T(8,128)(2,1)S(1)}, u32[]{:S(2)}, u32[]{:S(2)}) collective-permute-start(bf16[96,1792]{1,0:T(8,128)(2,1)S(1)} %pad_maximum_fusion.refs_0_.refs_3_), channel_id=1, source_target_pairs={{16,8},{9,17},{18,10},{11,19},{20,12},{13,21},{22,14},{15,23}} | collective-permute-start | bytes 1032200 | tf_op jit(solution)/shard_map/ppermute | solution.py:240
  60.5 9.7 %collective-permute-start.14 = (bf16[96,1792]{1,0:T(8,128)(2,1)S(1)}, bf16[96,1792]{1,0:T(8,128)(2,1)S(1)}, u32[]{:S(2)}, u32[]{:S(2)}) collective-permute-start(bf16[96,1792]{1,0:T(8,128)(2,1)S(1)} %pad_maximum_fusion.refs_0_.refs_3_), channel_id=1, source_target_pairs={{24,8},{25,17},{26,10},{27,19},{28,12},{29,21},{30,14},{31,23}} | collective-permute-start | bytes 1032200 | tf_op jit(solution)/shard_map/ppermute | solution.py:240
  63.0 11.1 %collective-permute-start.15 = (bf16[96,1792]{1,0:T(8,128)(2,1)S(1)}, bf16[96,1792]{1,0:T(8,128)(2,1)S(1)}, u32[]{:S(2)}, u32[]{:S(2)}) collective-permute-start(bf16[96,1792]{1,0:T(8,128)(2,1)S(1)} %pad_maximum_fusion.1.refs_1_.refs_3_), channel_id=1, source_target_pairs={{0,8},{1,17},{2,10},{3,19},{4,12},{5,21},{6,14},{7,23}} | collective-permute-start | bytes 1032200 | tf_op jit(solution)/shard_map/ppermute | solution.py:240
  65.5 8.6 %collective-permute-start.16 = (bf16[96,1792]{1,0:T(8,128)(2,1)S(1)}, bf16[96,1792]{1,0:T(8,128)(2,1)S(1)}, u32[]{:S(2)}, u32[]{:S(2)}) collective-permute-start(bf16[96,1792]{1,0:T(8,128)(2,1)S(1)} %pad_maximum_fusion.1.refs_1_.refs_3_), channel_id=1, source_target_pairs={{16,8},{9,17},{18,10},{11,19},{20,12},{13,21},{22,14},{15,23}} | collective-permute-start | bytes 1032200 | tf_op jit(solution)/shard_map/ppermute | solution.py:240
  68.2 5.9 %collective-permute-start.17 = (bf16[96,1792]{1,0:T(8,128)(2,1)S(1)}, bf16[96,1792]{1,0:T(8,128)(2,1)S(1)}, u32[]{:S(2)}, u32[]{:S(2)}) collective-permute-start(bf16[96,1792]{1,0:T(8,128)(2,1)S(1)} %pad_maximum_fusion.1.refs_1_.refs_3_), channel_id=1, source_target_pairs={{24,8},{25,17},{26,10},{27,19},{28,12},{29,21},{30,14},{31,23}} | collective-permute-start | bytes 1032200 | tf_op jit(solution)/shard_map/ppermute | solution.py:240
  80.4 8.4 %collective-permute-start.23 = (bf16[96,1792]{1,0:T(8,128)(2,1)S(1)}, bf16[96,1792]{1,0:T(8,128)(2,1)S(1)}, u32[]{:S(2)}, u32[]{:S(2)}) collective-permute-start(bf16[96,1792]{1,0:T(8,128)(2,1)S(1)} %get-tuple-element.39), channel_id=1, source_target_pairs={{8,24},{17,25},{10,26},{19,27},{12,28},{21,29},{14,30},{23,31}} | collective-permute-start | bytes 1032200 | tf_op jit(solution)/shard_map/ppermute | solution.py:244
  81.1 9.0 %collective-permute-start.22 = (bf16[96,1792]{1,0:T(8,128)(2,1)S(1)}, bf16[96,1792]{1,0:T(8,128)(2,1)S(1)}, u32[]{:S(2)}, u32[]{:S(2)}) collective-permute-start(bf16[96,1792]{1,0:T(8,128)(2,1)S(1)} %get-tuple-element.38), channel_id=1, source_target_pairs={{8,16},{17,9},{10,18},{19,11},{12,20},{21,13},{14,22},{23,15}} | collective-permute-start | bytes 1032200 | tf_op jit(solution)/shard_map/ppermute | solution.py:244
  81.8 16.3 %collective-permute-start.21 = (bf16[96,1792]{1,0:T(8,128)(2,1)S(1)}, bf16[96,1792]{1,0:T(8,128)(2,1)S(1)}, u32[]{:S(2)}, u32[]{:S(2)}) collective-permute-start(bf16[96,1792]{1,0:T(8,128)(2,1)S(1)} %get-tuple-element.37), channel_id=1, source_target_pairs={{8,0},{17,1},{10,2},{19,3},{12,4},{21,5},{14,6},{23,7}} | collective-permute-start | bytes 1032200 | tf_op jit(solution)/shard_map/ppermute | solution.py:244
  87.4 10.8 %collective-permute-start.20 = (bf16[96,1792]{1,0:T(8,128)(2,1)S(1)}, bf16[96,1792]{1,0:T(8,128)(2,1)S(1)}, u32[]{:S(2)}, u32[]{:S(2)}) collective-permute-start(bf16[96,1792]{1,0:T(8,128)(2,1)S(1)} %get-tuple-element.35), channel_id=1, source_target_pairs={{8,24},{17,25},{10,26},{19,27},{12,28},{21,29},{14,30},{23,31}} | collective-permute-start | bytes 1032200 | tf_op jit(solution)/shard_map/ppermute | solution.py:244
  88.1 10.1 %collective-permute-start.19 = (bf16[96,1792]{1,0:T(8,128)(2,1)S(1)}, bf16[96,1792]{1,0:T(8,128)(2,1)S(1)}, u32[]{:S(2)}, u32[]{:S(2)}) collective-permute-start(bf16[96,1792]{1,0:T(8,128)(2,1)S(1)} %get-tuple-element.34), channel_id=1, source_target_pairs={{8,16},{17,9},{10,18},{19,11},{12,20},{21,13},{14,22},{23,15}} | collective-permute-start | bytes 1032200 | tf_op jit(solution)/shard_map/ppermute | solution.py:244
  88.8 17.6 %collective-permute-start.18 = (bf16[96,1792]{1,0:T(8,128)(2,1)S(1)}, bf16[96,1792]{1,0:T(8,128)(2,1)S(1)}, u32[]{:S(2)}, u32[]{:S(2)}) collective-permute-start(bf16[96,1792]{1,0:T(8,128)(2,1)S(1)} %get-tuple-element.33), channel_id=1, source_target_pairs={{8,0},{17,1},{10,2},{19,3},{12,4},{21,5},{14,6},{23,7}} | collective-permute-start | bytes 1032200 | tf_op jit(solution)/shard_map/ppermute | solution.py:244
  (3 other events, 26.5 us)

commit v2 on v0

v2 whole, which is shorter than its diff:
```python
import functools
import math

import jax
import jax.numpy as jnp
from jax import lax
from jax.experimental import pallas as pl
from jax.experimental.pallas import tpu as pltpu
from jax.sharding import PartitionSpec as P

ITERS = 3
FIRST_SHARE = 7 / 14

momentum_rate = 0.95
coef_a = 3.4445
coef_b = -4.775
coef_c = 2.0315

AXES = ("fsdp", "rep")
VMEM_LIMIT = 24 * 1024 * 1024
LANES = 128
TILE = 256
NEST_COST = 5_000_000
bf16 = jnp.bfloat16
f32 = jnp.float32


def dot(left, right):
    return jnp.dot(left, right, preferred_element_type=f32)


def two(value):
    high = value.astype(bf16)
    return high, (value - high.astype(f32)).astype(bf16)


def in_vmem(count):
    return [pl.BlockSpec(memory_space=pltpu.VMEM)] * count


def in_smem(count):
    return [pl.BlockSpec(memory_space=pltpu.SMEM)] * count


def call(body, outs, inputs, specs, after=(), scratch=(), hold=True, cost=1):
    count = len(inputs)

    def kernel(*refs):
        body(*refs[:count], *refs[count + len(after) :])

    return pl.pallas_call(
        kernel,
        out_shape=tuple(pltpu.VMEM(o.shape, o.dtype) if hold else o for o in outs),
        in_specs=list(specs) + [pl.BlockSpec(memory_space=pl.ANY)] * len(after),
        out_specs=tuple(in_vmem(len(outs))),
        scratch_shapes=list(scratch),
        compiler_params=pltpu.CompilerParams(vmem_limit_bytes=VMEM_LIMIT),
        cost_estimate=pl.CostEstimate(flops=1, bytes_accessed=cost, transcendentals=0),
    )(*inputs, *after)


def split(flat, mats, cap, padded, first, width, after):
    half = mats // 2
    rows = min(TILE // mats, cap)
    size = rows * mats
    blocks = -(-cap // rows)
    tiles = [(at, min(TILE, width - at)) for at in range(0, width, TILE)]

    def body(x_ref, keep_ref, send_ref, held_ref, sems):
        copies = [
            pltpu.make_async_copy(
                x_ref.at[:, first + at : first + at + wide], held_ref.at[:, at : at + wide], sems.at[i]
            )
            for i, (at, wide) in enumerate(tiles)
        ]
        for copy in copies:
            copy.start()
        me = lax.axis_index("rep")
        out_row = lax.broadcasted_iota(jnp.int32, (size, 1), 0)
        in_row = lax.broadcasted_iota(jnp.int32, (size, size), 1)
        place = out_row // rows
        within = out_row - place * rows
        j = jnp.where(place < half, 2 * place, 2 * (place - half) + 1)
        matrix = jnp.bitwise_xor(j, me)
        chosen = {}
        for block in range(blocks):
            start = min(block * rows, cap - rows)
            shift = block * rows - start
            if shift not in chosen:
                source = jnp.where(within < rows - shift, (within + shift) * mats + matrix, -1)
                chosen[shift] = jnp.where(in_row == source, 1.0, 0.0).astype(bf16)
        for copy, (at, wide) in zip(copies, tiles):
            copy.wait()
            for block in range(blocks):
                start = min(block * rows, cap - rows)
                moved = dot(
                    chosen[block * rows - start],
                    held_ref[start * mats : start * mats + size, at : at + wide],
                ).reshape(mats, rows, wide)
                here = min(rows, padded - block * rows)
                to = slice(block * rows, block * rows + here)
                keep_ref[:, to, at : at + wide] = moved[:half, :here].astype(bf16)
                send_ref[:, to, at : at + wide] = moved[half:, :here].astype(bf16)
        if blocks * rows < padded:
            rest = padded - blocks * rows
            keep_ref[:, blocks * rows :, :] = jnp.zeros((half, rest, width), bf16)
            send_ref[:, blocks * rows :, :] = jnp.zeros((half, rest, width), bf16)

    out = jax.ShapeDtypeStruct((half, padded, width), bf16)
    return call(
        body,
        [out, out],
        [pltpu.with_memory_space_constraint(flat, pltpu.HBM)],
        [pl.BlockSpec(memory_space=pltpu.HBM)],
        after,
        [pltpu.VMEM((flat.shape[0], width), bf16), pltpu.SemaphoreType.DMA((len(tiles),))],
    )


def fold(terms, plans, part, padded):
    def body(*refs):
        inputs, outs = refs[: len(terms)], refs[len(terms) :]
        for out, plan in zip(outs, plans):
            for row in range(0, padded, 16):
                to = slice(row, row + 16)
                for i, parts in enumerate(plan):
                    added = None
                    for term, place, at in parts:
                        value = inputs[term][place, to, at : at + part].astype(f32)
                        added = value if added is None else added + value
                    out[i, to, :] = added.astype(bf16)

    outs = [jax.ShapeDtypeStruct((len(plan), padded, part), bf16) for plan in plans]
    return call(body, outs, terms, in_vmem(len(terms)))


def linear_rows(ref, row, cap, blocks, block):
    here = max(0, min(8, cap - row))
    found = []
    if here:
        found.append(ref[pl.ds(row * blocks + block, here, stride=blocks), :])
    if here < 8:
        found.append(jnp.zeros((8 - here, LANES), f32))
    return found[0] if len(found) == 1 else jnp.concatenate(found, axis=0)


def live_count(offsets_ref):
    device = lax.axis_index("fsdp")
    return offsets_ref[0, device + 1] - offsets_ref[0, device]


def nesterov(offsets, linear, terms, plans, part, first, cap, padded, replicas, after):
    blocks = linear.shape[0] // cap
    width = part * len(plans)

    def body(*refs):
        offsets_ref, linear_ref, *inputs = refs[: 2 + len(terms)]
        out_ref, mean_ref = refs[2 + len(terms) :]
        count = live_count(offsets_ref)
        for row in range(0, padded, 16):
            slot = lax.broadcasted_iota(jnp.int32, (16, LANES), 0) + row
            to = slice(row, row + 16)
            for side, plan in enumerate(plans):
                for column in range(0, part, LANES):
                    added = None
                    for term, place, at in plan:
                        value = inputs[term][place, to, at + column : at + column + LANES].astype(f32)
                        added = value if added is None else added + value
                    mean = added * (1.0 / replicas)
                    here = side * part + column
                    block = (first + here) // LANES
                    old = jnp.concatenate(
                        [linear_rows(linear_ref, row + i, cap, blocks, block) for i in (0, 8)], axis=0
                    )
                    new = momentum_rate * old + mean
                    value = jnp.where(slot < count, mean + momentum_rate * new, 0.0)
                    out_ref[to, here : here + LANES] = value.astype(bf16)
                    mean_ref[to, here : here + LANES] = mean

    outs = [jax.ShapeDtypeStruct((padded, width), bf16), jax.ShapeDtypeStruct((padded, width), f32)]
    specs = in_smem(1) + in_vmem(1 + len(terms))
    return call(body, outs, [offsets, linear, *terms], specs, after, cost=NEST_COST)


def keep_state(offsets, linear, means, cap, after):
    blocks = linear.shape[0] // cap

    def body(offsets_ref, linear_ref, *refs):
        inputs, out_ref = refs[:-1], refs[-1]
        count = live_count(offsets_ref)
        for row in range(0, cap, 8):
            here = min(8, cap - row)
            slot = lax.broadcasted_iota(jnp.int32, (here, LANES), 0) + row
            first = 0
            for mean_ref in inputs:
                for column in range(0, mean_ref.shape[1], LANES):
                    at = pl.ds(row * blocks + (first + column) // LANES, here, stride=blocks)
                    new = momentum_rate * linear_ref[at, :] + mean_ref[
                        row : row + here, column : column + LANES
                    ]
                    out_ref[at, :] = jnp.where(slot < count, new, 0.0)
                first += mean_ref.shape[1]

    outs = [jax.ShapeDtypeStruct(linear.shape, f32)]
    specs = in_smem(1) + in_vmem(1 + len(means))
    return call(body, outs, [offsets, linear, *means], specs, after, hold=False)[0]


def gram_of(parts, stack_ref):
    rows = parts[0].shape[0]
    for i, part in enumerate(parts):
        stack_ref[i * rows : (i + 1) * rows, :] = part[...]
    return lax.dot_general(
        stack_ref[...], stack_ref[...], (((1,), (1,)), ((), ())), preferred_element_type=f32
    )


def gram(parts, after):
    size, width = len(parts) * parts[0].shape[0], parts[0].shape[1]

    def body(*refs):
        *inputs, stack_ref, out_ref = refs
        out_ref[...] = gram_of(inputs, stack_ref)

    outs = [jax.ShapeDtypeStruct((size, width), bf16), jax.ShapeDtypeStruct((size, size), f32)]
    return call(body, outs, parts, in_vmem(len(parts)), after)


def chain(full_width, sums, parts, after):
    groups = len(parts)
    rows, width = parts[0].shape
    size = groups * rows

    def body(*refs):
        earlier, inputs = refs[: len(sums)], refs[len(sums) : -3]
        stack_ref, factor_ref, alpha_ref = refs[-3:]
        gram = gram_of(inputs, stack_ref)
        for earlier_ref in earlier:
            gram = gram + earlier_ref[...]
        diagonal = lax.broadcasted_iota(jnp.int32, (size, size), 0) == lax.broadcasted_iota(
            jnp.int32, (size, size), 1
        )
        trace = jnp.sum(jnp.where(diagonal, gram, 0.0), keepdims=True)
        scale = 1.0 / (jnp.sqrt(trace) + 1e-07)
        gram = (gram * scale) * scale
        rest = None
        power = 1.0
        for iteration in range(ITERS):
            rounded = gram.astype(bf16)
            square = dot(rounded, rounded)
            poly = (coef_b * rounded.astype(f32) + coef_c * square).astype(bf16)
            if rest is None:
                rest = poly.astype(f32)
            else:
                rest_high, rest_low = two(rest)
                rest = (
                    coef_a * rest
                    + power * poly.astype(f32)
                    + (dot(poly, rest_high) + dot(poly, rest_low))
                )
            power = power * coef_a
            if iteration < ITERS - 1:
                gram_high, gram_low = two(gram)
                left = coef_a * gram + (dot(poly, gram_high) + dot(poly, gram_low))
                left_high, left_low = two(left)
                gram = coef_a * left + (dot(left_high, poly) + dot(left_low, poly))
        scale = scale * math.sqrt(full_width)
        high, low = two(rest * scale)
        for i in range(groups):
            factor_ref[i, :rows, :] = high[i * rows : (i + 1) * rows]
            factor_ref[i, rows:, :] = low[i * rows : (i + 1) * rows]
        alpha_ref[...] = jnp.broadcast_to(scale * power, alpha_ref.shape)

    outs = [
        jax.ShapeDtypeStruct((size, width), bf16),
        jax.ShapeDtypeStruct((groups, 2 * rows, size), bf16),
        jax.ShapeDtypeStruct((8, LANES), f32),
    ]
    return call(body, outs, [*sums, *parts], in_vmem(len(sums) + groups), after)


def apply_rows(index, factor_ref, alpha_ref, stacks, out_ref):
    rows = factor_ref.shape[1] // 2
    height = out_ref.shape[0]
    left = factor_ref[index]
    own = slice(index * rows, (index + 1) * rows)
    first = 0
    for stack_ref in stacks:
        for at in range(0, stack_ref.shape[1], TILE):
            to = slice(at, min(at + TILE, stack_ref.shape[1]))
            both = dot(left, stack_ref[:, to])
            result = both[:rows] + both[rows:] + alpha_ref[0:1, 0:1] * stack_ref[own, to].astype(f32)
            out_ref[:, first + to.start : first + to.stop] = result[:height].astype(bf16)
        first += stack_ref.shape[1]


def rows_of(factor, alpha, stacks, index, after):
    def body(factor_ref, alpha_ref, *refs):
        apply_rows(index, factor_ref, alpha_ref, refs[:-1], refs[-1])

    outs = [jax.ShapeDtypeStruct((factor.shape[1] // 2, sum(s.shape[1] for s in stacks)), bf16)]
    return call(body, outs, [factor, alpha, *stacks], in_vmem(2 + len(stacks)), after)[0]


def own_or_received(owners, factor, alpha, stacks, received, cap):
    def body(factor_ref, alpha_ref, *refs):
        *inputs, out_ref = refs
        mine = lax.axis_index("fsdp") == owners + lax.rem(lax.axis_index("rep"), 2)

        @pl.when(mine)
        def _():
            apply_rows(0, factor_ref, alpha_ref, inputs[: len(stacks)], out_ref)

        @pl.when(jnp.logical_not(mine))
        def _():
            for row in range(0, cap, 16):
                to = slice(row, min(row + 16, cap))
                added = None
                for came in inputs[len(stacks) :]:
                    value = came[to, :]
                    added = value if added is None else added + value
                out_ref[to, :] = added

    outs = [jax.ShapeDtypeStruct((cap, received[0].shape[1]), bf16)]
    specs = in_vmem(2 + len(stacks) + len(received))
    return call(body, outs, [factor, alpha, *stacks, *received], specs, hold=False)[0]


def per_device(groups, replicas, gradients, momentum, offsets):
    _, mats, cap, width = gradients.shape
    padded = -(-cap // 16) * 16
    bits = [1 << i for i in range(replicas.bit_length() - 1)]

    def swap(value, bit):
        pairs = [(f * replicas + r, f * replicas + (r ^ bit)) for f in range(groups) for r in range(replicas)]
        return lax.ppermute(value, AXES, pairs)

    def owner(r):
        return (groups - 1) // 2 + r % 2

    def others(r):
        return sorted((f for f in range(groups) if f != owner(r)), key=lambda f: -abs(f - owner(r)))

    def to_owner(value, k):
        pairs = [(others(r)[k] * replicas + r, owner(r) * replicas + r) for r in range(replicas)]
        return lax.ppermute(value, AXES, pairs)

    def from_owner(value, k):
        pairs = [(owner(r) * replicas + r, others(r)[k] * replicas + r) for r in range(replicas)]
        return lax.ppermute(value, AXES, pairs)

    flat = jnp.transpose(gradients[0], (1, 0, 2)).reshape(cap * mats, width)
    linear = momentum[0].reshape(cap * (width // LANES), LANES)

    unit = 2 * LANES
    head = max(1, round(width // unit * FIRST_SHARE)) * unit
    chunks = [(0, head), (head, width - head)]
    orders = [bits[1:], bits[1:][::-1]]
    terms, plans = [], []
    last = ()
    for first, wide in chunks:
        keep, send = split(flat, mats, cap, padded, first, wide, last)
        last = (keep,)
        terms.append([keep, swap(send, bits[0])])
        plans.append(
            [{2 * i: [(t, i, side * (wide // 2)) for t in range(2)] for i in range(mats // 2)} for side in range(2)]
        )
    for level in range(len(bits) - 1):
        for chunk, (_, wide) in enumerate(chunks):
            moving = [[j for j in plan if j & order[level]] for plan, order in zip(plans[chunk], orders)]
            wanted = [[plan[j] for j in away] for plan, away in zip(plans[chunk], moving)]
            sends = fold(terms[chunk], wanted, wide // 2, padded)
            last = (sends[0],)
            for side, away in enumerate(moving):
                bit = orders[side][level]
                terms[chunk].append(swap(sends[side], bit))
                for place, j in enumerate(away):
                    plans[chunk][side][j ^ bit].append((len(terms[chunk]) - 1, place, 0))
                    del plans[chunk][side][j]

    means, held = [], []
    for chunk, (first, wide) in enumerate(chunks):
        sources = [plan[0] for plan in plans[chunk]]
        own, mean = nesterov(
            offsets, linear, terms[chunk], sources, wide // 2, first, cap, padded, replicas, last
        )
        last = (own,)
        means.append(mean)
        held.append([own] + [to_owner(own, k) for k in range(groups - 1)])
    kept_state = keep_state(offsets, linear, means, cap, last)
    stacks, sums = [], []
    for parts in held[:-1]:
        stack, partial = gram(parts, (kept_state,))
        stacks.append(stack)
        sums.append(partial)
    stack, factor, alpha = chain(width, sums, held[-1], ())
    stacks.append(stack)
    back = []
    last = ()
    for k in range(groups - 1):
        result = rows_of(factor, alpha, stacks, k + 1, last)
        last = (result,)
        back.append(from_owner(result, k))
    update = own_or_received((groups - 1) // 2, factor, alpha, stacks, back, cap)
    return (kept_state.reshape(1, cap, width), update[None])


def solution(mesh):
    placed = (P("rep", None, "fsdp", None), P("rep", "fsdp", None), P("rep", None))
    return jax.shard_map(
        functools.partial(per_device, mesh.shape["fsdp"], mesh.shape["rep"]),
        mesh=mesh,
        in_specs=placed,
        out_specs=(P("rep", "fsdp", None), P("rep", "fsdp", None)),
        check_vma=False,
    )
```

time: 240 us -> 84.9 us (0.35)
  waiting for transfers between devices: 114 us -> 37.2 us
  blocking collectives: 45.8 us -> 0 us
  local copies, waits for them, and re-layouts: 27.8 us -> 1.32 us
  starting transfers between devices: 4.47 us -> 25.5 us
  Pallas kernels: 0 us -> 19.7 us
  matrix products: 16 us -> 0 us
  between operations: 16.3 us -> 0.83 us
  other arithmetic: 14.8 us -> 0 us
    reduce_scatter x1 -> x0, waiting for transfers between devices: 60.6 us -> none  [per_device(): lax.psum_scatter(gradients[0].astype(jnp.float32).astype(jnp.bfloat16), '...]
    all_gather x1 -> x0, waiting for transfers between devices: 52.9 us -> none  [per_device(): shards = lax.all_gather(nesterov, 'fsdp', axis=0, tiled=True)]
    unnamed x1 -> x0, blocking collectives: 45.8 us -> none
    ppermute x0 -> x19, waiting for transfers between devices: none -> 37.2 us  [the longest x3 18.7 us: from_owner(): return lax.ppermute(value, AXES, pairs)]
    ppermute x0 -> x19, starting transfers between devices: none -> 25.5 us  [the longest x10 12 us: swap(): return lax.ppermute(value, AXES, pairs)]
    pallas_call x0 -> x15, Pallas kernels: none -> 19.7 us  [call(): pl.pallas_call(kernel, out_shape=tuple((pltpu.VMEM(o.shape, o.dtype) if h...]
    dot_general x6 -> x0, matrix products: 16 us -> none  [the longest x3 10.1 us: orthogonalize(): jnp.dot(polynomial, iterate, preferred_element_type=jnp.float32)]
    gather x9 -> x0, local copies, waits for them, and re-layouts: 12 us -> none  [the longest x6 3.88 us: per_device(): jnp.take(bounds, slot_holder + 1) - jnp.take(bounds, slot_holder)]
  transfers between devices with their start and end apart: 3 -> 19, of which waited for: 2 -> 7; matrix products, arithmetic and copies ran while one was open for 3% -> 0% of each run, Pallas kernels for 0% -> 9%
where the time goes in v2:
time: 84.9 us; the launch traced here: 84.6 us
  waiting for transfers between devices  37.2 us (44%)
  starting transfers between devices  25.5 us (30%)
  Pallas kernels  19.7 us (23%)
  local copies, waits for them, and re-layouts  1.32 us (2%)
    pallas_call x15, Pallas kernels, call(): pl.pallas_call(kernel, out_shape=tuple((pltpu.VMEM(o.shape, o.dtype) if h...  19.7 us
    ppermute x3, waiting for transfers between devices, from_owner(): return lax.ppermute(value, AXES, pairs)  18.7 us
    ppermute x10, waiting for transfers between devices, swap(): return lax.ppermute(value, AXES, pairs)  14.1 us
    ppermute x10, starting transfers between devices, swap(): return lax.ppermute(value, AXES, pairs)  12 us
    ppermute x6, starting transfers between devices, to_owner(): return lax.ppermute(value, AXES, pairs)  10.8 us
    ppermute x6, waiting for transfers between devices, to_owner(): return lax.ppermute(value, AXES, pairs)  4.48 us
    ppermute x3, starting transfers between devices, from_owner(): return lax.ppermute(value, AXES, pairs)  2.7 us
  transfers between devices with their start and end apart: 19, of which 7 were waited for; matrix products, arithmetic and copies ran while one was open for 0% of the time, Pallas kernels for 9%

profile of v2, /device:TPU:0, one launch (start us, length us, event | category | flops | bytes accessed | tf_op | source)
XLA Modules:
  0.0 84.6 jit_solution(215185410828022778)
XLA Ops:
  0.6 3.1 %shard_map.50 = (bf16[4,96,1792]{2,1,0:T(8,128)(2,1)S(1)}, bf16[4,96,1792]{2,1,0:T(8,128)(2,1)S(1)}) custom-call(bf16[720,3584]{1,0:T(8,128)(2,1)} %bitcast.12), custom_call_target="tpu_custom_call" | custom-call | flops 1 | bytes 1 | tf_op jit(solution)/shard_map/pallas_call | solution.py:51
  4.3 3.1 %shard_map.53 = (bf16[4,96,1792]{2,1,0:T(8,128)(2,1)S(1)}, bf16[4,96,1792]{2,1,0:T(8,128)(2,1)S(1)}) custom-call(bf16[720,3584]{1,0:T(8,128)(2,1)} %bitcast.13, bf16[4,96,1792]{2,1,0:T(8,128)(2,1)S(1)} %get-tuple-element.23.refs_0_.refs_1_.refs_2_), custom_call_target="tpu_custom_call" | custom-call | flops 1 | bytes 1 | tf_op jit(solution)/shard_map/pallas_call | solution.py:51
  7.6 3.0 %collective-permute-start.1 = (bf16[2,96,896]{2,1,0:T(8,128)(2,1)S(1)}, bf16[2,96,896]{2,1,0:T(8,128)(2,1)S(1)}, u32[]{:S(2)}, u32[]{:S(2)}) collective-permute-start(bf16[2,96,896]{2,1,0:T(8,128)(2,1)S(1)} %get-tuple-element.25), channel_id=1, source_target_pairs={{0,2},{1,3},{2,0},{3,1},{4,6},{5,7},{6,4},{7,5},{8,10},{9,11},{10,... | collective-permute-start | bytes 1032200 | tf_op jit(solution)/shard_map/ppermute | solution.py:336
  10.7 1.5 %collective-permute-start.2 = (bf16[2,96,896]{2,1,0:T(8,128)(2,1)S(1)}, bf16[2,96,896]{2,1,0:T(8,128)(2,1)S(1)}, u32[]{:S(2)}, u32[]{:S(2)}) collective-permute-start(bf16[2,96,896]{2,1,0:T(8,128)(2,1)S(1)} %get-tuple-element.26), channel_id=1, source_target_pairs={{0,4},{1,5},{2,6},{3,7},{4,0},{5,1},{6,2},{7,3},{8,12},{9,13},{10,... | collective-permute-start | bytes 1032200 | tf_op jit(solution)/shard_map/ppermute | solution.py:336
  12.3 1.1 %collective-permute-start.6 = (bf16[2,96,896]{2,1,0:T(8,128)(2,1)S(1)}, bf16[2,96,896]{2,1,0:T(8,128)(2,1)S(1)}, u32[]{:S(2)}, u32[]{:S(2)}) collective-permute-start(bf16[2,96,896]{2,1,0:T(8,128)(2,1)S(1)} %get-tuple-element.31), channel_id=1, source_target_pairs={{0,2},{1,3},{2,0},{3,1},{4,6},{5,7},{6,4},{7,5},{8,10},{9,11},{10,... | collective-permute-start | bytes 1032200 | tf_op jit(solution)/shard_map/ppermute | solution.py:336
  13.4 1.5 %collective-permute-start.7 = (bf16[2,96,896]{2,1,0:T(8,128)(2,1)S(1)}, bf16[2,96,896]{2,1,0:T(8,128)(2,1)S(1)}, u32[]{:S(2)}, u32[]{:S(2)}) collective-permute-start(bf16[2,96,896]{2,1,0:T(8,128)(2,1)S(1)} %get-tuple-element.32), channel_id=1, source_target_pairs={{0,4},{1,5},{2,6},{3,7},{4,0},{5,1},{6,2},{7,3},{8,12},{9,13},{10,... | collective-permute-start | bytes 1032200 | tf_op jit(solution)/shard_map/ppermute | solution.py:336
  14.9 4.6 %collective-permute-done.1.refs_2_.refs_4_ = bf16[2,96,896]{2,1,0:T(8,128)(2,1)S(1)} collective-permute-done((bf16[2,96,896]{2,1,0:T(8,128)(2,1)S(1)}, bf16[2,96,896]{2,1,0:T(8,128)(2,1)S(1)}, u32[]{:S(2)}, u32[]{:S(2)}) %collective-permute-start.1) | collective-permute-done | bytes 344096 | tf_op jit(solution)/shard_map/ppermute | solution.py:336
  19.5 2.1 %collective-permute-done.2.refs_3_.refs_5_ = bf16[2,96,896]{2,1,0:T(8,128)(2,1)S(1)} collective-permute-done((bf16[2,96,896]{2,1,0:T(8,128)(2,1)S(1)}, bf16[2,96,896]{2,1,0:T(8,128)(2,1)S(1)}, u32[]{:S(2)}, u32[]{:S(2)}) %collective-permute-start.2) | collective-permute-done | bytes 344096 | tf_op jit(solution)/shard_map/ppermute | solution.py:336
  21.8 1.6 %collective-permute-start.3 = (bf16[1,96,896]{2,1,0:T(8,128)(2,1)S(1)}, bf16[1,96,896]{2,1,0:T(8,128)(2,1)S(1)}, u32[]{:S(2)}, u32[]{:S(2)}) collective-permute-start(bf16[1,96,896]{2,1,0:T(8,128)(2,1)S(1)} %get-tuple-element.27), channel_id=1, source_target_pairs={{0,4},{1,5},{2,6},{3,7},{4,0},{5,1},{6,2},{7,3},{8,12},{9,13},{10,... | collective-permute-start | bytes 516104 | tf_op jit(solution)/shard_map/ppermute | solution.py:336
  23.9 3.0 %collective-permute-done.6.refs_2_.refs_4_ = bf16[2,96,896]{2,1,0:T(8,128)(2,1)S(1)} collective-permute-done((bf16[2,96,896]{2,1,0:T(8,128)(2,1)S(1)}, bf16[2,96,896]{2,1,0:T(8,128)(2,1)S(1)}, u32[]{:S(2)}, u32[]{:S(2)}) %collective-permute-start.6) | collective-permute-done | bytes 344096 | tf_op jit(solution)/shard_map/ppermute | solution.py:336
  26.9 2.1 %collective-permute-done.7.refs_3_.refs_5_ = bf16[2,96,896]{2,1,0:T(8,128)(2,1)S(1)} collective-permute-done((bf16[2,96,896]{2,1,0:T(8,128)(2,1)S(1)}, bf16[2,96,896]{2,1,0:T(8,128)(2,1)S(1)}, u32[]{:S(2)}, u32[]{:S(2)}) %collective-permute-start.7) | collective-permute-done | bytes 344096 | tf_op jit(solution)/shard_map/ppermute | solution.py:336
  29.1 2.3 %collective-permute-done.3.refs_6_ = bf16[1,96,896]{2,1,0:T(8,128)(2,1)S(1)} collective-permute-done((bf16[1,96,896]{2,1,0:T(8,128)(2,1)S(1)}, bf16[1,96,896]{2,1,0:T(8,128)(2,1)S(1)}, u32[]{:S(2)}, u32[]{:S(2)}) %collective-permute-start.3) | collective-permute-done | bytes 172064 | tf_op jit(solution)/shard_map/ppermute | solution.py:336
  33.4 1.7 %collective-permute-start.8 = (bf16[1,96,896]{2,1,0:T(8,128)(2,1)S(1)}, bf16[1,96,896]{2,1,0:T(8,128)(2,1)S(1)}, u32[]{:S(2)}, u32[]{:S(2)}) collective-permute-start(bf16[1,96,896]{2,1,0:T(8,128)(2,1)S(1)} %get-tuple-element.33.refs_8_), channel_id=1, source_target_pairs={{0,4},{1,5},{2,6},{3,7},{4,0},{5,1},{6,2},{7,3},{8,12},{9,13},{10,... | collective-permute-start | bytes 516104 | tf_op jit(solution)/shard_map/ppermute | solution.py:336
  35.1 4.1 %collective-permute-start.11 = (bf16[96,1792]{1,0:T(8,128)(2,1)S(1)}, bf16[96,1792]{1,0:T(8,128)(2,1)S(1)}, u32[]{:S(2)}, u32[]{:S(2)}) collective-permute-start(bf16[96,1792]{1,0:T(8,128)(2,1)S(1)} %get-tuple-element.36.refs_8_.refs_0_), channel_id=1, source_target_pairs={{0,8},{9,17},{2,10},{11,19},{4,12},{13,21},{6,14},{15,23}} | collective-permute-start | bytes 1032200 | tf_op jit(solution)/shard_map/ppermute | solution.py:346
  41.5 3.8 %collective-permute-start.14 = (bf16[96,1792]{1,0:T(8,128)(2,1)S(1)}, bf16[96,1792]{1,0:T(8,128)(2,1)S(1)}, u32[]{:S(2)}, u32[]{:S(2)}) collective-permute-start(bf16[96,1792]{1,0:T(8,128)(2,1)S(1)} %get-tuple-element.38.refs_4_.refs_1_), channel_id=1, source_target_pairs={{0,8},{9,17},{2,10},{11,19},{4,12},{13,21},{6,14},{15,23}} | collective-permute-start | bytes 1032200 | tf_op jit(solution)/shard_map/ppermute | solution.py:346
  46.2 1.8 %shard_map.58.refs_4_ = f32[2520,128]{1,0:T(8,128)} custom-call(s32[1,5]{1,0:T(1,128)S(1)} %copy-done.2, f32[2520,128]{1,0:T(8,128)S(1)} %bitcast.10, f32[96,1792]{1,0:T(8,128)S(1)} %get-tuple-element.34.refs_2_, f32[96,1792]{1,0:T(8,128)S(1)} %get-tuple-element.37.refs_3_, bf16[96,1792]{1,0:T(8,128)(2,1)S(1)} %get-tuple-element.38.refs_4_.refs_1_), custom_call_target="tpu_custom_call" | custom-call | flops 1 | bytes 1 | tf_op jit(solution)/shard_map/pallas_call | solution.py:51
  48.0 1.3 %copy-done.1 = f32[2520,128]{1,0:T(8,128)S(1)} copy-done((f32[2520,128]{1,0:T(8,128)S(1)}, f32[2520,128]{1,0:T(8,128)}, u32[]{:S(2)}) %copy-start.1) | copy-done | bytes 1290264
  50.2 4.5 %collective-permute-done.14.refs_3_ = bf16[96,1792]{1,0:T(8,128)(2,1)S(1)} collective-permute-done((bf16[96,1792]{1,0:T(8,128)(2,1)S(1)}, bf16[96,1792]{1,0:T(8,128)(2,1)S(1)}, u32[]{:S(2)}, u32[]{:S(2)}) %collective-permute-start.14) | collective-permute-done | bytes 344096 | tf_op jit(solution)/shard_map/ppermute | solution.py:346
  54.7 4.6 %shard_map.60 = (bf16[384,1792]{1,0:T(8,128)(2,1)S(1)}, bf16[4,192,384]{2,1,0:T(8,128)(2,1)S(1)}, f32[8,128]{1,0:T(8,128)S(1)}) custom-call(f32[384,384]{1,0:T(8,128)S(1)} %get-tuple-element.39.refs_0_, bf16[96,1792]{1,0:T(8,128)(2,1)S(1)} %get-tuple-element.38.refs_4_.refs_1_, bf16[96,1792]{1,0:T(8,128)(2,1)S(1)} %collective-permute-done.13.refs_2_, ...), custom_call_target="tpu_custom_call" | custom-call | flops 1 | bytes 1 | tf_op jit(solution)/shard_map/pallas_call | solution.py:51
  59.4 1.0 %shard_map.61.refs_4_ = bf16[96,3584]{1,0:T(8,128)(2,1)S(1)} custom-call(bf16[4,192,384]{2,1,0:T(8,128)(2,1)S(1)} %get-tuple-element.40.refs_0_, f32[8,128]{1,0:T(8,128)S(1)} %get-tuple-element.41.refs_1_, bf16[384,1792]{1,0:T(8,128)(2,1)S(1)} %get-tuple-element.42.refs_2_, bf16[384,1792]{1,0:T(8,128)(2,1)S(1)} %get-tuple-element.43.refs_3_), custom_call_target="tpu_custom_call" | custom-call | flops 1 | bytes 1 | tf_op jit(solution)/shard_map/pallas_call | solution.py:51
  60.3 1.0 %shard_map.62.refs_4_ = bf16[96,3584]{1,0:T(8,128)(2,1)S(1)} custom-call(bf16[4,192,384]{2,1,0:T(8,128)(2,1)S(1)} %get-tuple-element.40.refs_0_, f32[8,128]{1,0:T(8,128)S(1)} %get-tuple-element.41.refs_1_, bf16[384,1792]{1,0:T(8,128)(2,1)S(1)} %get-tuple-element.42.refs_2_, bf16[384,1792]{1,0:T(8,128)(2,1)S(1)} %get-tuple-element.43.refs_3_, ...), custom_call_target="tpu_custom_call" | custom-call | flops 1 | bytes 1 | tf_op jit(solution)/shard_map/pallas_call | solution.py:51
  63.0 1.3 %collective-permute-start.17 = (bf16[96,3584]{1,0:T(8,128)(2,1)S(1)}, bf16[96,3584]{1,0:T(8,128)(2,1)S(1)}, u32[]{:S(2)}, u32[]{:S(2)}) collective-permute-start(bf16[96,3584]{1,0:T(8,128)(2,1)S(1)} %shard_map.62.refs_4_), channel_id=1, source_target_pairs={{8,0},{17,9},{10,2},{19,11},{12,4},{21,13},{14,6},{23,15}} | collective-permute-start | bytes 2064392 | tf_op jit(solution)/shard_map/ppermute | solution.py:350
  65.0 18.7 %collective-permute-done.17.refs_5_ = bf16[96,3584]{1,0:T(8,128)(2,1)S(1)} collective-permute-done((bf16[96,3584]{1,0:T(8,128)(2,1)S(1)}, bf16[96,3584]{1,0:T(8,128)(2,1)S(1)}, u32[]{:S(2)}, u32[]{:S(2)}) %collective-permute-start.17) | collective-permute-done | bytes 688160 | tf_op jit(solution)/shard_map/ppermute | solution.py:350
  83.6 0.9 %shard_map.64 = bf16[90,3584]{1,0:T(8,128)(2,1)} custom-call(bf16[4,192,384]{2,1,0:T(8,128)(2,1)S(1)} %get-tuple-element.40.refs_0_, f32[8,128]{1,0:T(8,128)S(1)} %get-tuple-element.41.refs_1_, bf16[384,1792]{1,0:T(8,128)(2,1)S(1)} %get-tuple-element.42.refs_2_, bf16[384,1792]{1,0:T(8,128)(2,1)S(1)} %get-tuple-element.43.refs_3_, ...), custom_call_target="tpu_custom_call" | custom-call | flops 1 | bytes 1 | tf_op jit(solution)/shard_map/pallas_call | solution.py:51
  (35 shorter events, 10.1 us)
Async XLA Ops:
  3.7 3.7 %collective-permute-start = (bf16[4,96,1792]{2,1,0:T(8,128)(2,1)S(1)}, bf16[4,96,1792]{2,1,0:T(8,128)(2,1)S(1)}, u32[]{:S(2)}, u32[]{:S(2)}) collective-permute-start(bf16[4,96,1792]{2,1,0:T(8,128)(2,1)S(1)} %get-tuple-element.24), channel_id=1, source_target_pairs={{0,1},{1,0},{2,3},{3,2},{4,5},{5,4},{6,7},{7,6},{8,9},{9,8},{10,11... | collective-permute-start | bytes 4128776 | tf_op jit(solution)/shard_map/ppermute | solution.py:336
  7.4 4.8 %collective-permute-start.5 = (bf16[4,96,1792]{2,1,0:T(8,128)(2,1)S(1)}, bf16[4,96,1792]{2,1,0:T(8,128)(2,1)S(1)}, u32[]{:S(2)}, u32[]{:S(2)}) collective-permute-start(bf16[4,96,1792]{2,1,0:T(8,128)(2,1)S(1)} %get-tuple-element.30), channel_id=1, source_target_pairs={{0,1},{1,0},{2,3},{3,2},{4,5},{5,4},{6,7},{7,6},{8,9},{9,8},{10,11... | collective-permute-start | bytes 4128776 | tf_op jit(solution)/shard_map/ppermute | solution.py:336
  7.6 11.9 %collective-permute-start.1 = (bf16[2,96,896]{2,1,0:T(8,128)(2,1)S(1)}, bf16[2,96,896]{2,1,0:T(8,128)(2,1)S(1)}, u32[]{:S(2)}, u32[]{:S(2)}) collective-permute-start(bf16[2,96,896]{2,1,0:T(8,128)(2,1)S(1)} %get-tuple-element.25), channel_id=1, source_target_pairs={{0,2},{1,3},{2,0},{3,1},{4,6},{5,7},{6,4},{7,5},{8,10},{9,11},{10,... | collective-permute-start | bytes 1032200 | tf_op jit(solution)/shard_map/ppermute | solution.py:336
  10.7 11.0 %collective-permute-start.2 = (bf16[2,96,896]{2,1,0:T(8,128)(2,1)S(1)}, bf16[2,96,896]{2,1,0:T(8,128)(2,1)S(1)}, u32[]{:S(2)}, u32[]{:S(2)}) collective-permute-start(bf16[2,96,896]{2,1,0:T(8,128)(2,1)S(1)} %get-tuple-element.26), channel_id=1, source_target_pairs={{0,4},{1,5},{2,6},{3,7},{4,0},{5,1},{6,2},{7,3},{8,12},{9,13},{10,... | collective-permute-start | bytes 1032200 | tf_op jit(solution)/shard_map/ppermute | solution.py:336
  12.3 14.6 %collective-permute-start.6 = (bf16[2,96,896]{2,1,0:T(8,128)(2,1)S(1)}, bf16[2,96,896]{2,1,0:T(8,128)(2,1)S(1)}, u32[]{:S(2)}, u32[]{:S(2)}) collective-permute-start(bf16[2,96,896]{2,1,0:T(8,128)(2,1)S(1)} %get-tuple-element.31), channel_id=1, source_target_pairs={{0,2},{1,3},{2,0},{3,1},{4,6},{5,7},{6,4},{7,5},{8,10},{9,11},{10,... | collective-permute-start | bytes 1032200 | tf_op jit(solution)/shard_map/ppermute | solution.py:336
  13.4 15.6 %collective-permute-start.7 = (bf16[2,96,896]{2,1,0:T(8,128)(2,1)S(1)}, bf16[2,96,896]{2,1,0:T(8,128)(2,1)S(1)}, u32[]{:S(2)}, u32[]{:S(2)}) collective-permute-start(bf16[2,96,896]{2,1,0:T(8,128)(2,1)S(1)} %get-tuple-element.32), channel_id=1, source_target_pairs={{0,4},{1,5},{2,6},{3,7},{4,0},{5,1},{6,2},{7,3},{8,12},{9,13},{10,... | collective-permute-start | bytes 1032200 | tf_op jit(solution)/shard_map/ppermute | solution.py:336
  21.8 9.7 %collective-permute-start.3 = (bf16[1,96,896]{2,1,0:T(8,128)(2,1)S(1)}, bf16[1,96,896]{2,1,0:T(8,128)(2,1)S(1)}, u32[]{:S(2)}, u32[]{:S(2)}) collective-permute-start(bf16[1,96,896]{2,1,0:T(8,128)(2,1)S(1)} %get-tuple-element.27), channel_id=1, source_target_pairs={{0,4},{1,5},{2,6},{3,7},{4,0},{5,1},{6,2},{7,3},{8,12},{9,13},{10,... | collective-permute-start | bytes 516104 | tf_op jit(solution)/shard_map/ppermute | solution.py:336
  23.3 8.1 %copy-start = (f32[1,90,3584]{2,0,1:T(1,128)S(1)}, f32[1,90,3584]{2,0,1:T(1,128)}, u32[]{:S(2)}) copy-start(f32[1,90,3584]{2,0,1:T(1,128)} %param.4) | copy-start | bytes 3870724
  23.3 8.1 %copy-start.2 = (s32[1,5]{1,0:T(1,128)S(1)}, s32[1,5]{1,0:T(1,128)}, u32[]{:S(2)}) copy-start(s32[1,5]{1,0:T(1,128)} %refs_0_.5) | copy-start | bytes 64
  23.3 8.1 %collective-permute-start.4 = (bf16[1,96,896]{2,1,0:T(8,128)(2,1)S(1)}, bf16[1,96,896]{2,1,0:T(8,128)(2,1)S(1)}, u32[]{:S(2)}, u32[]{:S(2)}) collective-permute-start(bf16[1,96,896]{2,1,0:T(8,128)(2,1)S(1)} %get-tuple-element.28), channel_id=1, source_target_pairs={{0,2},{1,3},{2,0},{3,1},{4,6},{5,7},{6,4},{7,5},{8,10},{9,11},{10,... | collective-permute-start | bytes 516104 | tf_op jit(solution)/shard_map/ppermute | solution.py:336
  32.3 13.0 %collective-permute-start.12 = (bf16[96,1792]{1,0:T(8,128)(2,1)S(1)}, bf16[96,1792]{1,0:T(8,128)(2,1)S(1)}, u32[]{:S(2)}, u32[]{:S(2)}) collective-permute-start(bf16[96,1792]{1,0:T(8,128)(2,1)S(1)} %get-tuple-element.36.refs_8_.refs_0_), channel_id=1, source_target_pairs={{16,8},{25,17},{18,10},{27,19},{20,12},{29,21},{22,14},{31,23}} | collective-permute-start | bytes 1032200 | tf_op jit(solution)/shard_map/ppermute | solution.py:346
  33.0 6.9 %collective-permute-start.9 = (bf16[1,96,896]{2,1,0:T(8,128)(2,1)S(1)}, bf16[1,96,896]{2,1,0:T(8,128)(2,1)S(1)}, u32[]{:S(2)}, u32[]{:S(2)}) collective-permute-start(bf16[1,96,896]{2,1,0:T(8,128)(2,1)S(1)} %get-tuple-element.35), channel_id=1, source_target_pairs={{0,2},{1,3},{2,0},{3,1},{4,6},{5,7},{6,4},{7,5},{8,10},{9,11},{10,... | collective-permute-start | bytes 516104 | tf_op jit(solution)/shard_map/ppermute | solution.py:336
  33.4 6.5 %collective-permute-start.8 = (bf16[1,96,896]{2,1,0:T(8,128)(2,1)S(1)}, bf16[1,96,896]{2,1,0:T(8,128)(2,1)S(1)}, u32[]{:S(2)}, u32[]{:S(2)}) collective-permute-start(bf16[1,96,896]{2,1,0:T(8,128)(2,1)S(1)} %get-tuple-element.33.refs_8_), channel_id=1, source_target_pairs={{0,4},{1,5},{2,6},{3,7},{4,0},{5,1},{6,2},{7,3},{8,12},{9,13},{10,... | collective-permute-start | bytes 516104 | tf_op jit(solution)/shard_map/ppermute | solution.py:336
  35.1 12.9 %collective-permute-start.11 = (bf16[96,1792]{1,0:T(8,128)(2,1)S(1)}, bf16[96,1792]{1,0:T(8,128)(2,1)S(1)}, u32[]{:S(2)}, u32[]{:S(2)}) collective-permute-start(bf16[96,1792]{1,0:T(8,128)(2,1)S(1)} %get-tuple-element.36.refs_8_.refs_0_), channel_id=1, source_target_pairs={{0,8},{9,17},{2,10},{11,19},{4,12},{13,21},{6,14},{15,23}} | collective-permute-start | bytes 1032200 | tf_op jit(solution)/shard_map/ppermute | solution.py:346
  39.2 8.8 %collective-permute-start.10 = (bf16[96,1792]{1,0:T(8,128)(2,1)S(1)}, bf16[96,1792]{1,0:T(8,128)(2,1)S(1)}, u32[]{:S(2)}, u32[]{:S(2)}) collective-permute-start(bf16[96,1792]{1,0:T(8,128)(2,1)S(1)} %get-tuple-element.36.refs_8_.refs_0_), channel_id=1, source_target_pairs={{24,8},{1,17},{26,10},{3,19},{28,12},{5,21},{30,14},{7,23}} | collective-permute-start | bytes 1032200 | tf_op jit(solution)/shard_map/ppermute | solution.py:346
  40.8 9.4 %collective-permute-start.15 = (bf16[96,1792]{1,0:T(8,128)(2,1)S(1)}, bf16[96,1792]{1,0:T(8,128)(2,1)S(1)}, u32[]{:S(2)}, u32[]{:S(2)}) collective-permute-start(bf16[96,1792]{1,0:T(8,128)(2,1)S(1)} %get-tuple-element.38.refs_4_.refs_1_), channel_id=1, source_target_pairs={{16,8},{25,17},{18,10},{27,19},{20,12},{29,21},{22,14},{31,23}} | collective-permute-start | bytes 1032200 | tf_op jit(solution)/shard_map/ppermute | solution.py:346
  41.5 13.2 %collective-permute-start.14 = (bf16[96,1792]{1,0:T(8,128)(2,1)S(1)}, bf16[96,1792]{1,0:T(8,128)(2,1)S(1)}, u32[]{:S(2)}, u32[]{:S(2)}) collective-permute-start(bf16[96,1792]{1,0:T(8,128)(2,1)S(1)} %get-tuple-element.38.refs_4_.refs_1_), channel_id=1, source_target_pairs={{0,8},{9,17},{2,10},{11,19},{4,12},{13,21},{6,14},{15,23}} | collective-permute-start | bytes 1032200 | tf_op jit(solution)/shard_map/ppermute | solution.py:346
  45.3 9.4 %collective-permute-start.13 = (bf16[96,1792]{1,0:T(8,128)(2,1)S(1)}, bf16[96,1792]{1,0:T(8,128)(2,1)S(1)}, u32[]{:S(2)}, u32[]{:S(2)}) collective-permute-start(bf16[96,1792]{1,0:T(8,128)(2,1)S(1)} %get-tuple-element.38.refs_4_.refs_1_), channel_id=1, source_target_pairs={{24,8},{1,17},{26,10},{3,19},{28,12},{5,21},{30,14},{7,23}} | collective-permute-start | bytes 1032200 | tf_op jit(solution)/shard_map/ppermute | solution.py:346
  48.0 1.3 %copy-start.1 = (f32[2520,128]{1,0:T(8,128)S(1)}, f32[2520,128]{1,0:T(8,128)}, u32[]{:S(2)}) copy-start(f32[2520,128]{1,0:T(8,128)} %shard_map.58.refs_4_) | copy-start | bytes 3870724
  62.2 2.7 %collective-permute-start.18 = (bf16[96,3584]{1,0:T(8,128)(2,1)S(1)}, bf16[96,3584]{1,0:T(8,128)(2,1)S(1)}, u32[]{:S(2)}, u32[]{:S(2)}) collective-permute-start(bf16[96,3584]{1,0:T(8,128)(2,1)S(1)} %shard_map.63), channel_id=1, source_target_pairs={{8,16},{17,25},{10,18},{19,27},{12,20},{21,29},{14,22},{23,31}} | collective-permute-start | bytes 2064392 | tf_op jit(solution)/shard_map/ppermute | solution.py:350
  63.0 20.7 %collective-permute-start.17 = (bf16[96,3584]{1,0:T(8,128)(2,1)S(1)}, bf16[96,3584]{1,0:T(8,128)(2,1)S(1)}, u32[]{:S(2)}, u32[]{:S(2)}) collective-permute-start(bf16[96,3584]{1,0:T(8,128)(2,1)S(1)} %shard_map.62.refs_4_), channel_id=1, source_target_pairs={{8,0},{17,9},{10,2},{19,11},{12,4},{21,13},{14,6},{23,15}} | collective-permute-start | bytes 2064392 | tf_op jit(solution)/shard_map/ppermute | solution.py:350
  64.2 19.4 %collective-permute-start.16 = (bf16[96,3584]{1,0:T(8,128)(2,1)S(1)}, bf16[96,3584]{1,0:T(8,128)(2,1)S(1)}, u32[]{:S(2)}, u32[]{:S(2)}) collective-permute-start(bf16[96,3584]{1,0:T(8,128)(2,1)S(1)} %shard_map.61.refs_4_), channel_id=1, source_target_pairs={{8,24},{17,1},{10,26},{19,3},{12,28},{21,5},{14,30},{23,7}} | collective-permute-start | bytes 2064392 | tf_op jit(solution)/shard_map/ppermute | solution.py:350

commit v3 on v2

--- a/solution.py
+++ b/solution.py
@@ -9,7 +9,8 @@
 from jax.sharding import PartitionSpec as P
 
 ITERS = 3
-FIRST_SHARE = 7 / 14
+SHARES = (7, 7)
+STEPS = (('S', 0), ('S', 1), ('H', 0, 0), ('H', 1, 0), ('H', 0, 1), ('H', 1, 1), ('N', 0), ('N', 1))
 
 momentum_rate = 0.95
 coef_a = 3.4445
@@ -20,7 +21,7 @@
 VMEM_LIMIT = 24 * 1024 * 1024
 LANES = 128
 TILE = 256
-NEST_COST = 5_000_000
+BESIDE = {'gate0': 1, 'gate1': 1, 'nest0': 8.7, 'nest1792': 8.7}
 bf16 = jnp.bfloat16
 f32 = jnp.float32
 
@@ -42,7 +43,7 @@
     return [pl.BlockSpec(memory_space=pltpu.SMEM)] * count
 
 
-def call(body, outs, inputs, specs, after=(), scratch=(), hold=True, cost=1):
+def call(body, outs, inputs, specs, after=(), scratch=(), hold=True, name="step"):
     count = len(inputs)
 
     def kernel(*refs):
@@ -54,8 +55,9 @@
         in_specs=list(specs) + [pl.BlockSpec(memory_space=pl.ANY)] * len(after),
         out_specs=tuple(in_vmem(len(outs))),
         scratch_shapes=list(scratch),
+        name=name,
         compiler_params=pltpu.CompilerParams(vmem_limit_bytes=VMEM_LIMIT),
-        cost_estimate=pl.CostEstimate(flops=1, bytes_accessed=cost, transcendentals=0),
+        cost_estimate=pl.CostEstimate(flops=max(1, int(BESIDE.get(name, 0) * 1.15e9)), bytes_accessed=1, transcendentals=0),
     )(*inputs, *after)
 
 
@@ -64,14 +66,14 @@
     rows = min(TILE // mats, cap)
     size = rows * mats
     blocks = -(-cap // rows)
-    tiles = [(at, min(TILE, width - at)) for at in range(0, width, TILE)]
+    starts = [min(block * rows, cap - rows) for block in range(blocks)]
 
     def body(x_ref, keep_ref, send_ref, held_ref, sems):
         copies = [
             pltpu.make_async_copy(
-                x_ref.at[:, first + at : first + at + wide], held_ref.at[:, at : at + wide], sems.at[i]
+                x_ref.at[start * mats : start * mats + size, first : first + width], held_ref.at[i], sems.at[i]
             )
-            for i, (at, wide) in enumerate(tiles)
+            for i, start in enumerate(starts)
         ]
         for copy in copies:
             copy.start()
@@ -83,20 +85,17 @@
         j = jnp.where(place < half, 2 * place, 2 * (place - half) + 1)
         matrix = jnp.bitwise_xor(j, me)
         chosen = {}
-        for block in range(blocks):
-            start = min(block * rows, cap - rows)
+        for block, start in enumerate(starts):
             shift = block * rows - start
             if shift not in chosen:
                 source = jnp.where(within < rows - shift, (within + shift) * mats + matrix, -1)
                 chosen[shift] = jnp.where(in_row == source, 1.0, 0.0).astype(bf16)
-        for copy, (at, wide) in zip(copies, tiles):
-            copy.wait()
-            for block in range(blocks):
-                start = min(block * rows, cap - rows)
-                moved = dot(
-                    chosen[block * rows - start],
-                    held_ref[start * mats : start * mats + size, at : at + wide],
-                ).reshape(mats, rows, wide)
+        for block, start in enumerate(starts):
+            copies[block].wait()
+            for at in range(0, width, TILE):
+                wide = min(TILE, width - at)
+                moved = dot(chosen[block * rows - start], held_ref[block, :, at : at + wide])
+                moved = moved.reshape(mats, rows, wide)
                 here = min(rows, padded - block * rows)
                 to = slice(block * rows, block * rows + here)
                 keep_ref[:, to, at : at + wide] = moved[:half, :here].astype(bf16)
@@ -113,25 +112,33 @@
         [pltpu.with_memory_space_constraint(flat, pltpu.HBM)],
         [pl.BlockSpec(memory_space=pltpu.HBM)],
         after,
-        [pltpu.VMEM((flat.shape[0], width), bf16), pltpu.SemaphoreType.DMA((len(tiles),))],
+        [pltpu.VMEM((blocks, size, width), bf16), pltpu.SemaphoreType.DMA((blocks,))],
+        name=f"split{first}",
     )
 
 
-def fold(terms, plans, part, padded):
+def added(inputs, parts, rows, width):
+    total = None
+    for term, place, at in parts:
+        value = inputs[term][place, rows, at : at + width].astype(f32)
+        total = value if total is None else total + value
+    return total
+
+
+def fold(terms, plans, padded, after, name):
     def body(*refs):
         inputs, outs = refs[: len(terms)], refs[len(terms) :]
         for out, plan in zip(outs, plans):
             for row in range(0, padded, 16):
                 to = slice(row, row + 16)
-                for i, parts in enumerate(plan):
-                    added = None
-                    for term, place, at in parts:
-                        value = inputs[term][place, to, at : at + part].astype(f32)
-                        added = value if added is None else added + value
-                    out[i, to, :] = added.astype(bf16)
-
-    outs = [jax.ShapeDtypeStruct((len(plan), padded, part), bf16) for plan in plans]
-    return call(body, outs, terms, in_vmem(len(terms)))
+                for i, segments in enumerate(plan):
+                    at = 0
+                    for width, parts in segments:
+                        out[i, to, at : at + width] = added(inputs, parts, to, width).astype(bf16)
+                        at += width
+
+    outs = [jax.ShapeDtypeStruct((len(plan), padded, sum(w for w, _ in plan[0])), bf16) for plan in plans]
+    return call(body, outs, terms, in_vmem(len(terms)), after, name=name)
 
 
 def linear_rows(ref, row, cap, blocks, block):
@@ -149,9 +156,8 @@
     return offsets_ref[0, device + 1] - offsets_ref[0, device]
 
 
-def nesterov(offsets, linear, terms, plans, part, first, cap, padded, replicas, after):
+def nesterov(offsets, linear, terms, segments, first, wide, cap, padded, replicas, after):
     blocks = linear.shape[0] // cap
-    width = part * len(plans)
 
     def body(*refs):
         offsets_ref, linear_ref, *inputs = refs[: 2 + len(terms)]
@@ -160,26 +166,23 @@
         for row in range(0, padded, 16):
             slot = lax.broadcasted_iota(jnp.int32, (16, LANES), 0) + row
             to = slice(row, row + 16)
-            for side, plan in enumerate(plans):
-                for column in range(0, part, LANES):
-                    added = None
-                    for term, place, at in plan:
-                        value = inputs[term][place, to, at + column : at + column + LANES].astype(f32)
-                        added = value if added is None else added + value
-                    mean = added * (1.0 / replicas)
-                    here = side * part + column
-                    block = (first + here) // LANES
+            for start, width, parts in segments:
+                for column in range(0, width, LANES):
+                    here = [(term, place, at + column) for term, place, at in parts]
+                    mean = added(inputs, here, to, LANES) * (1.0 / replicas)
+                    block = (start + column) // LANES
                     old = jnp.concatenate(
                         [linear_rows(linear_ref, row + i, cap, blocks, block) for i in (0, 8)], axis=0
                     )
                     new = momentum_rate * old + mean
                     value = jnp.where(slot < count, mean + momentum_rate * new, 0.0)
-                    out_ref[to, here : here + LANES] = value.astype(bf16)
-                    mean_ref[to, here : here + LANES] = mean
-
-    outs = [jax.ShapeDtypeStruct((padded, width), bf16), jax.ShapeDtypeStruct((padded, width), f32)]
+                    at = start + column - first
+                    out_ref[to, at : at + LANES] = value.astype(bf16)
+                    mean_ref[to, at : at + LANES] = mean
+
+    outs = [jax.ShapeDtypeStruct((padded, wide), bf16), jax.ShapeDtypeStruct((padded, wide), f32)]
     specs = in_smem(1) + in_vmem(1 + len(terms))
-    return call(body, outs, [offsets, linear, *terms], specs, after, cost=NEST_COST)
+    return call(body, outs, [offsets, linear, *terms], specs, after, name=f"nest{first}")
 
 
 def keep_state(offsets, linear, means, cap, after):
@@ -203,7 +206,7 @@
 
     outs = [jax.ShapeDtypeStruct(linear.shape, f32)]
     specs = in_smem(1) + in_vmem(1 + len(means))
-    return call(body, outs, [offsets, linear, *means], specs, after, hold=False)[0]
+    return call(body, outs, [offsets, linear, *means], specs, after, hold=False, name="keep")[0]
 
 
 def gram_of(parts, stack_ref):
@@ -215,7 +218,7 @@
     )
 
 
-def gram(parts, after):
+def gram(parts, after, name):
     size, width = len(parts) * parts[0].shape[0], parts[0].shape[1]
 
     def body(*refs):
@@ -223,7 +226,7 @@
         out_ref[...] = gram_of(inputs, stack_ref)
 
     outs = [jax.ShapeDtypeStruct((size, width), bf16), jax.ShapeDtypeStruct((size, size), f32)]
-    return call(body, outs, parts, in_vmem(len(parts)), after)
+    return call(body, outs, parts, in_vmem(len(parts)), after, name=name)
 
 
 def chain(full_width, sums, parts, after):
@@ -276,7 +279,7 @@
         jax.ShapeDtypeStruct((groups, 2 * rows, size), bf16),
         jax.ShapeDtypeStruct((8, LANES), f32),
     ]
-    return call(body, outs, [*sums, *parts], in_vmem(len(sums) + groups), after)
+    return call(body, outs, [*sums, *parts], in_vmem(len(sums) + groups), after, name="chain")
 
 
 def apply_rows(index, factor_ref, alpha_ref, stacks, out_ref):
@@ -299,10 +302,17 @@
         apply_rows(index, factor_ref, alpha_ref, refs[:-1], refs[-1])
 
     outs = [jax.ShapeDtypeStruct((factor.shape[1] // 2, sum(s.shape[1] for s in stacks)), bf16)]
-    return call(body, outs, [factor, alpha, *stacks], in_vmem(2 + len(stacks)), after)[0]
-
-
-def own_or_received(owners, factor, alpha, stacks, received, cap):
+    return call(body, outs, [factor, alpha, *stacks], in_vmem(2 + len(stacks)), after, name=f"rows{index}")[0]
+
+
+def gate(after, name):
+    def body(out_ref):
+        out_ref[...] = jnp.zeros_like(out_ref)
+
+    return call(body, [jax.ShapeDtypeStruct((8, LANES), f32)], [], [], after, name=name)[0]
+
+
+def own_or_received(owners, factor, alpha, stacks, received, cap, after):
     def body(factor_ref, alpha_ref, *refs):
         *inputs, out_ref = refs
         mine = lax.axis_index("fsdp") == owners + lax.rem(lax.axis_index("rep"), 2)
@@ -323,7 +333,7 @@
 
     outs = [jax.ShapeDtypeStruct((cap, received[0].shape[1]), bf16)]
     specs = in_vmem(2 + len(stacks) + len(received))
-    return call(body, outs, [factor, alpha, *stacks, *received], specs, hold=False)[0]
+    return call(body, outs, [factor, alpha, *stacks, *received], specs, after, hold=False, name="last")[0]
 
 
 def per_device(groups, replicas, gradients, momentum, offsets):
@@ -352,45 +362,77 @@
     flat = jnp.transpose(gradients[0], (1, 0, 2)).reshape(cap * mats, width)
     linear = momentum[0].reshape(cap * (width // LANES), LANES)
 
-    unit = 2 * LANES
-    head = max(1, round(width // unit * FIRST_SHARE)) * unit
-    chunks = [(0, head), (head, width - head)]
+    chunks, first = [], 0
+    for share in SHARES:
+        wide = width // sum(SHARES) * share
+        chunks.append((first, wide))
+        first += wide
     orders = [bits[1:], bits[1:][::-1]]
-    terms, plans = [], []
     last = ()
-    for first, wide in chunks:
+
+    def split_piece(first, wide):
+        nonlocal last
         keep, send = split(flat, mats, cap, padded, first, wide, last)
         last = (keep,)
-        terms.append([keep, swap(send, bits[0])])
-        plans.append(
-            [{2 * i: [(t, i, side * (wide // 2)) for t in range(2)] for i in range(mats // 2)} for side in range(2)]
-        )
-    for level in range(len(bits) - 1):
-        for chunk, (_, wide) in enumerate(chunks):
-            moving = [[j for j in plan if j & order[level]] for plan, order in zip(plans[chunk], orders)]
-            wanted = [[plan[j] for j in away] for plan, away in zip(plans[chunk], moving)]
-            sends = fold(terms[chunk], wanted, wide // 2, padded)
-            last = (sends[0],)
-            for side, away in enumerate(moving):
-                bit = orders[side][level]
-                terms[chunk].append(swap(sends[side], bit))
-                for place, j in enumerate(away):
-                    plans[chunk][side][j ^ bit].append((len(terms[chunk]) - 1, place, 0))
-                    del plans[chunk][side][j]
+        half = wide // 2
+        plans = [
+            {2 * i: [(first + side * half, half, [(t, i, side * half) for t in range(2)])] for i in range(mats // 2)}
+            for side in range(2)
+        ]
+        return [keep, swap(send, bits[0])], plans
+
+    def halve(level, terms, plans):
+        nonlocal last
+        moving = [[j for j in plan if j & order[level]] for plan, order in zip(plans, orders)]
+        wanted = [[[(w, parts) for _, w, parts in plan[j]] for j in away] for plan, away in zip(plans, moving)]
+        name = f"fold{level}_{plans[0][0][0][0]}"
+        sends = fold(terms, wanted, padded, last, name)
+        last = (sends[0],)
+        for side, away in enumerate(moving):
+            bit = orders[side][level]
+            terms.append(swap(sends[side], bit))
+            for place, j in enumerate(away):
+                at = 0
+                for _, segment, parts in plans[side][j ^ bit]:
+                    parts.append((len(terms) - 1, place, at))
+                    at += segment
+                del plans[side][j]
 
     means, held = [], []
-    for chunk, (first, wide) in enumerate(chunks):
-        sources = [plan[0] for plan in plans[chunk]]
-        own, mean = nesterov(
-            offsets, linear, terms[chunk], sources, wide // 2, first, cap, padded, replicas, last
-        )
+
+    def finish(chunk, terms, plans):
+        nonlocal last
+        segments = [segment for plan in plans for segment in plan[0]]
+        own, mean = nesterov(offsets, linear, terms, segments, *chunk, cap, padded, replicas, last)
         last = (own,)
         means.append(mean)
         held.append([own] + [to_owner(own, k) for k in range(groups - 1)])
+
+    levels = len(bits) - 1
+    work, arrived, reached = {}, {}, [0] * len(chunks)
+
+    def halve_next(chunk):
+        level = reached[chunk]
+        halve(level, *work[chunk])
+        arrived[chunk, level] = tuple(work[chunk][0][-2:])
+        reached[chunk] += 1
+
+    for kind, chunk, *more in STEPS:
+        if more and isinstance(more[-1], tuple):
+            last += arrived.get(more[-1], ())
+        if kind == "S":
+            work[chunk] = split_piece(*chunks[chunk])
+        elif kind == "H" and more[0] < levels:
+            halve_next(chunk)
+        elif kind == "N":
+            while reached[chunk] < levels:
+                halve_next(chunk)
+            finish(chunks[chunk], *work[chunk])
     kept_state = keep_state(offsets, linear, means, cap, last)
+    kept_there = pltpu.with_memory_space_constraint(kept_state, pltpu.HBM)
     stacks, sums = [], []
     for parts in held[:-1]:
-        stack, partial = gram(parts, (kept_state,))
+        stack, partial = gram(parts, (kept_there,), f"gram{len(sums)}")
         stacks.append(stack)
         sums.append(partial)
     stack, factor, alpha = chain(width, sums, held[-1], ())
@@ -401,7 +443,10 @@
         result = rows_of(factor, alpha, stacks, k + 1, last)
         last = (result,)
         back.append(from_owner(result, k))
-    update = own_or_received((groups - 1) // 2, factor, alpha, stacks, back, cap)
+    last = ()
+    for k, came in enumerate(back[:-1]):
+        last = (gate((came, *last), f"gate{k}"),)
+    update = own_or_received((groups - 1) // 2, factor, alpha, stacks, back, cap, last)
     return (kept_state.reshape(1, cap, width), update[None])
 
 

time: 84.9 us -> 78.6 us (0.926)
  waiting for transfers between devices: 37.2 us -> 35.1 us
  starting transfers between devices: 25.5 us -> 23.8 us
  local copies, waits for them, and re-layouts: 1.32 us -> 0.01 us
  Pallas kernels: 19.7 us -> 18.5 us
    ppermute x3, waiting for transfers between devices: 18.7 us -> 14.8 us  [from_owner(): return lax.ppermute(value, AXES, pairs)]
    ppermute x6, waiting for transfers between devices: 4.48 us -> 6.75 us  [to_owner(): return lax.ppermute(value, AXES, pairs)]
    ppermute x6, starting transfers between devices: 10.8 us -> 9.35 us  [to_owner(): return lax.ppermute(value, AXES, pairs)]
    unnamed x6 -> x4, local copies, waits for them, and re-layouts: 1.32 us -> 0.01 us
    pallas_call x15 -> x17, Pallas kernels: 19.7 us -> 18.5 us  [call(): pl.pallas_call(kernel, out_shape=tuple((pltpu.VMEM(o.shape, o.dtype) if h...]
  transfers between devices with their start and end apart: 19 -> 19, of which waited for: 7 -> 9; matrix products, arithmetic and copies ran while one was open for 0% -> 0% of each run, Pallas kernels for 9% -> 12%
where the time goes in v3:
time: 78.6 us; the launch traced here: 78.3 us
  waiting for transfers between devices  35.1 us (45%)
  starting transfers between devices  23.8 us (30%)
  Pallas kernels  18.5 us (24%)
  between operations  0.84 us (1%)
    pallas_call x17, Pallas kernels, call(): pl.pallas_call(kernel, out_shape=tuple((pltpu.VMEM(o.shape, o.dtype) if h...  18.5 us
    ppermute x3, waiting for transfers between devices, from_owner(): return lax.ppermute(value, AXES, pairs)  14.8 us
    ppermute x10, waiting for transfers between devices, swap(): return lax.ppermute(value, AXES, pairs)  13.5 us
    ppermute x10, starting transfers between devices, swap(): return lax.ppermute(value, AXES, pairs)  11.8 us
    ppermute x6, starting transfers between devices, to_owner(): return lax.ppermute(value, AXES, pairs)  9.35 us
    ppermute x6, waiting for transfers between devices, to_owner(): return lax.ppermute(value, AXES, pairs)  6.75 us
    ppermute x3, starting transfers between devices, from_owner(): return lax.ppermute(value, AXES, pairs)  2.7 us
  transfers between devices with their start and end apart: 19, of which 9 were waited for; matrix products, arithmetic and copies ran while one was open for 0% of the time, Pallas kernels for 12%

profile of v3, /device:TPU:0, one launch (start us, length us, event | category | flops | bytes accessed | tf_op | source)
XLA Modules:
  0.0 78.3 jit_solution(8489735810526604697)
XLA Ops:
  0.6 2.5 %split0.1 = (bf16[4,96,1792]{2,1,0:T(8,128)(2,1)S(1)}, bf16[4,96,1792]{2,1,0:T(8,128)(2,1)S(1)}) custom-call(bf16[720,3584]{1,0:T(8,128)(2,1)} %bitcast.11), custom_call_target="tpu_custom_call" | custom-call | flops 1 | bytes 1 | tf_op jit(solution)/shard_map/split0/pallas_call | solution.py:52
  3.7 2.5 %split1792.1 = (bf16[4,96,1792]{2,1,0:T(8,128)(2,1)S(1)}, bf16[4,96,1792]{2,1,0:T(8,128)(2,1)S(1)}) custom-call(bf16[720,3584]{1,0:T(8,128)(2,1)} %bitcast.12, bf16[4,96,1792]{2,1,0:T(8,128)(2,1)S(1)} %get-tuple-element.23.refs_1_.refs_0_.refs_2_), custom_call_target="tpu_custom_call" | custom-call | flops 1 | bytes 1 | tf_op jit(solution)/shard_map/split1792/pallas_call | solution.py:52
  6.6 3.0 %collective-permute-start.2 = (bf16[2,96,896]{2,1,0:T(8,128)(2,1)S(1)}, bf16[2,96,896]{2,1,0:T(8,128)(2,1)S(1)}, u32[]{:S(2)}, u32[]{:S(2)}) collective-permute-start(bf16[2,96,896]{2,1,0:T(8,128)(2,1)S(1)} %get-tuple-element.27), channel_id=1, source_target_pairs={{0,4},{1,5},{2,6},{3,7},{4,0},{5,1},{6,2},{7,3},{8,12},{9,13},{10,... | collective-permute-start | bytes 1032200 | tf_op jit(solution)/shard_map/ppermute | solution.py:346
  9.5 1.5 %collective-permute-start.1 = (bf16[2,96,896]{2,1,0:T(8,128)(2,1)S(1)}, bf16[2,96,896]{2,1,0:T(8,128)(2,1)S(1)}, u32[]{:S(2)}, u32[]{:S(2)}) collective-permute-start(bf16[2,96,896]{2,1,0:T(8,128)(2,1)S(1)} %get-tuple-element.26.refs_2_), channel_id=1, source_target_pairs={{0,2},{1,3},{2,0},{3,1},{4,6},{5,7},{6,4},{7,5},{8,10},{9,11},{10,... | collective-permute-start | bytes 1032200 | tf_op jit(solution)/shard_map/ppermute | solution.py:346
  11.2 1.1 %collective-permute-start.7 = (bf16[2,96,896]{2,1,0:T(8,128)(2,1)S(1)}, bf16[2,96,896]{2,1,0:T(8,128)(2,1)S(1)}, u32[]{:S(2)}, u32[]{:S(2)}) collective-permute-start(bf16[2,96,896]{2,1,0:T(8,128)(2,1)S(1)} %get-tuple-element.32), channel_id=1, source_target_pairs={{0,4},{1,5},{2,6},{3,7},{4,0},{5,1},{6,2},{7,3},{8,12},{9,13},{10,... | collective-permute-start | bytes 1032200 | tf_op jit(solution)/shard_map/ppermute | solution.py:346
  12.3 1.5 %collective-permute-start.6 = (bf16[2,96,896]{2,1,0:T(8,128)(2,1)S(1)}, bf16[2,96,896]{2,1,0:T(8,128)(2,1)S(1)}, u32[]{:S(2)}, u32[]{:S(2)}) collective-permute-start(bf16[2,96,896]{2,1,0:T(8,128)(2,1)S(1)} %get-tuple-element.29.refs_4_), channel_id=1, source_target_pairs={{0,2},{1,3},{2,0},{3,1},{4,6},{5,7},{6,4},{7,5},{8,10},{9,11},{10,... | collective-permute-start | bytes 1032200 | tf_op jit(solution)/shard_map/ppermute | solution.py:346
  13.8 4.6 %collective-permute-done.2.refs_3_.refs_5_ = bf16[2,96,896]{2,1,0:T(8,128)(2,1)S(1)} collective-permute-done((bf16[2,96,896]{2,1,0:T(8,128)(2,1)S(1)}, bf16[2,96,896]{2,1,0:T(8,128)(2,1)S(1)}, u32[]{:S(2)}, u32[]{:S(2)}) %collective-permute-start.2) | collective-permute-done | bytes 344096 | tf_op jit(solution)/shard_map/ppermute | solution.py:346
  18.4 2.1 %collective-permute-done.1.refs_2_.refs_4_ = bf16[2,96,896]{2,1,0:T(8,128)(2,1)S(1)} collective-permute-done((bf16[2,96,896]{2,1,0:T(8,128)(2,1)S(1)}, bf16[2,96,896]{2,1,0:T(8,128)(2,1)S(1)}, u32[]{:S(2)}, u32[]{:S(2)}) %collective-permute-start.1) | collective-permute-done | bytes 344096 | tf_op jit(solution)/shard_map/ppermute | solution.py:346
  20.6 1.6 %collective-permute-start.5 = (bf16[1,96,896]{2,1,0:T(8,128)(2,1)S(1)}, bf16[1,96,896]{2,1,0:T(8,128)(2,1)S(1)}, u32[]{:S(2)}, u32[]{:S(2)}) collective-permute-start(bf16[1,96,896]{2,1,0:T(8,128)(2,1)S(1)} %get-tuple-element.31), channel_id=1, source_target_pairs={{0,2},{1,3},{2,0},{3,1},{4,6},{5,7},{6,4},{7,5},{8,10},{9,11},{10,... | collective-permute-start | bytes 516104 | tf_op jit(solution)/shard_map/ppermute | solution.py:346
  22.7 3.1 %collective-permute-done.7.refs_3_.refs_5_ = bf16[2,96,896]{2,1,0:T(8,128)(2,1)S(1)} collective-permute-done((bf16[2,96,896]{2,1,0:T(8,128)(2,1)S(1)}, bf16[2,96,896]{2,1,0:T(8,128)(2,1)S(1)}, u32[]{:S(2)}, u32[]{:S(2)}) %collective-permute-start.7) | collective-permute-done | bytes 344096 | tf_op jit(solution)/shard_map/ppermute | solution.py:346
  25.8 2.1 %collective-permute-done.6.refs_2_.refs_4_ = bf16[2,96,896]{2,1,0:T(8,128)(2,1)S(1)} collective-permute-done((bf16[2,96,896]{2,1,0:T(8,128)(2,1)S(1)}, bf16[2,96,896]{2,1,0:T(8,128)(2,1)S(1)}, u32[]{:S(2)}, u32[]{:S(2)}) %collective-permute-start.6) | collective-permute-done | bytes 344096 | tf_op jit(solution)/shard_map/ppermute | solution.py:346
  28.0 1.6 %collective-permute-start.9 = (bf16[1,96,896]{2,1,0:T(8,128)(2,1)S(1)}, bf16[1,96,896]{2,1,0:T(8,128)(2,1)S(1)}, u32[]{:S(2)}, u32[]{:S(2)}) collective-permute-start(bf16[1,96,896]{2,1,0:T(8,128)(2,1)S(1)} %get-tuple-element.35), channel_id=1, source_target_pairs={{0,2},{1,3},{2,0},{3,1},{4,6},{5,7},{6,4},{7,5},{8,10},{9,11},{10,... | collective-permute-start | bytes 516104 | tf_op jit(solution)/shard_map/ppermute | solution.py:346
  30.1 1.5 %collective-permute-done.5.refs_7_ = bf16[1,96,896]{2,1,0:T(8,128)(2,1)S(1)} collective-permute-done((bf16[1,96,896]{2,1,0:T(8,128)(2,1)S(1)}, bf16[1,96,896]{2,1,0:T(8,128)(2,1)S(1)}, u32[]{:S(2)}, u32[]{:S(2)}) %collective-permute-start.5) | collective-permute-done | bytes 172064 | tf_op jit(solution)/shard_map/ppermute | solution.py:346
  33.1 4.1 %collective-permute-start.11 = (bf16[96,1792]{1,0:T(8,128)(2,1)S(1)}, bf16[96,1792]{1,0:T(8,128)(2,1)S(1)}, u32[]{:S(2)}, u32[]{:S(2)}) collective-permute-start(bf16[96,1792]{1,0:T(8,128)(2,1)S(1)} %get-tuple-element.36.refs_8_.refs_0_), channel_id=1, source_target_pairs={{0,8},{9,17},{2,10},{11,19},{4,12},{13,21},{6,14},{15,23}} | collective-permute-start | bytes 1032200 | tf_op jit(solution)/shard_map/ppermute | solution.py:356
  39.5 2.5 %collective-permute-start.14 = (bf16[96,1792]{1,0:T(8,128)(2,1)S(1)}, bf16[96,1792]{1,0:T(8,128)(2,1)S(1)}, u32[]{:S(2)}, u32[]{:S(2)}) collective-permute-start(bf16[96,1792]{1,0:T(8,128)(2,1)S(1)} %get-tuple-element.38.refs_4_.refs_1_), channel_id=1, source_target_pairs={{0,8},{9,17},{2,10},{11,19},{4,12},{13,21},{6,14},{15,23}} | collective-permute-start | bytes 1032200 | tf_op jit(solution)/shard_map/ppermute | solution.py:356
  42.7 1.8 %keep.1.refs_4_ = f32[2520,128]{1,0:T(8,128)} custom-call(s32[1,5]{1,0:T(1,128)S(1)} %copy-done.1, f32[2520,128]{1,0:T(8,128)S(1)} %bitcast.10, f32[96,1792]{1,0:T(8,128)S(1)} %get-tuple-element.34.refs_2_, f32[96,1792]{1,0:T(8,128)S(1)} %get-tuple-element.37.refs_3_, bf16[96,1792]{1,0:T(8,128)(2,1)S(1)} %get-tuple-element.38.refs_4_.refs_1_), custom_call_target="tpu_custom_call" | custom-call | flops 1 | bytes 1 | tf_op jit(solution)/shard_map/keep/pallas_call | solution.py:52
  44.6 1.0 %collective-permute-done.11.refs_2_ = bf16[96,1792]{1,0:T(8,128)(2,1)S(1)} collective-permute-done((bf16[96,1792]{1,0:T(8,128)(2,1)S(1)}, bf16[96,1792]{1,0:T(8,128)(2,1)S(1)}, u32[]{:S(2)}, u32[]{:S(2)}) %collective-permute-start.11) | collective-permute-done | bytes 344096 | tf_op jit(solution)/shard_map/ppermute | solution.py:356
  46.5 5.7 %collective-permute-done.14.refs_3_ = bf16[96,1792]{1,0:T(8,128)(2,1)S(1)} collective-permute-done((bf16[96,1792]{1,0:T(8,128)(2,1)S(1)}, bf16[96,1792]{1,0:T(8,128)(2,1)S(1)}, u32[]{:S(2)}, u32[]{:S(2)}) %collective-permute-start.14) | collective-permute-done | bytes 344096 | tf_op jit(solution)/shard_map/ppermute | solution.py:356
  52.2 4.6 %chain.1 = (bf16[384,1792]{1,0:T(8,128)(2,1)S(1)}, bf16[4,192,384]{2,1,0:T(8,128)(2,1)S(1)}, f32[8,128]{1,0:T(8,128)S(1)}) custom-call(f32[384,384]{1,0:T(8,128)S(1)} %get-tuple-element.39.refs_0_, bf16[96,1792]{1,0:T(8,128)(2,1)S(1)} %get-tuple-element.38.refs_4_.refs_1_, bf16[96,1792]{1,0:T(8,128)(2,1)S(1)} %collective-permute-done.13.refs_2_, ...), custom_call_target="tpu_custom_call" | custom-call | flops 1 | bytes 1 | tf_op jit(solution)/shard_map/chain/pallas_call | solution.py:52
  56.9 1.0 %rows1.1.refs_4_ = bf16[96,3584]{1,0:T(8,128)(2,1)S(1)} custom-call(bf16[4,192,384]{2,1,0:T(8,128)(2,1)S(1)} %get-tuple-element.40.refs_0_, f32[8,128]{1,0:T(8,128)S(1)} %get-tuple-element.41.refs_1_, bf16[384,1792]{1,0:T(8,128)(2,1)S(1)} %get-tuple-element.42.refs_2_, bf16[384,1792]{1,0:T(8,128)(2,1)S(1)} %get-tuple-element.43.refs_3_), custom_call_target="tpu_custom_call" | custom-call | flops 1 | bytes 1 | tf_op jit(solution)/shard_map/rows1/pallas_call | solution.py:52
  58.5 1.0 %rows2.1.refs_4_ = bf16[96,3584]{1,0:T(8,128)(2,1)S(1)} custom-call(bf16[4,192,384]{2,1,0:T(8,128)(2,1)S(1)} %get-tuple-element.40.refs_0_, f32[8,128]{1,0:T(8,128)S(1)} %get-tuple-element.41.refs_1_, bf16[384,1792]{1,0:T(8,128)(2,1)S(1)} %get-tuple-element.42.refs_2_, bf16[384,1792]{1,0:T(8,128)(2,1)S(1)} %get-tuple-element.43.refs_3_, ...), custom_call_target="tpu_custom_call" | custom-call | flops 1 | bytes 1 | tf_op jit(solution)/shard_map/rows2/pallas_call | solution.py:52
  59.5 1.3 %collective-permute-start.17 = (bf16[96,3584]{1,0:T(8,128)(2,1)S(1)}, bf16[96,3584]{1,0:T(8,128)(2,1)S(1)}, u32[]{:S(2)}, u32[]{:S(2)}) collective-permute-start(bf16[96,3584]{1,0:T(8,128)(2,1)S(1)} %rows2.1.refs_4_), channel_id=1, source_target_pairs={{8,0},{17,9},{10,2},{19,11},{12,4},{21,13},{14,6},{23,15}} | collective-permute-start | bytes 2064392 | tf_op jit(solution)/shard_map/ppermute | solution.py:360
  62.5 14.8 %collective-permute-done.17.refs_0_.refs_5_ = bf16[96,3584]{1,0:T(8,128)(2,1)S(1)} collective-permute-done((bf16[96,3584]{1,0:T(8,128)(2,1)S(1)}, bf16[96,3584]{1,0:T(8,128)(2,1)S(1)}, u32[]{:S(2)}, u32[]{:S(2)}) %collective-permute-start.17) | collective-permute-done | bytes 688160 | tf_op jit(solution)/shard_map/ppermute | solution.py:360
  77.3 0.9 %last.1 = bf16[90,3584]{1,0:T(8,128)(2,1)} custom-call(bf16[4,192,384]{2,1,0:T(8,128)(2,1)S(1)} %get-tuple-element.40.refs_0_, f32[8,128]{1,0:T(8,128)S(1)} %get-tuple-element.41.refs_1_, bf16[384,1792]{1,0:T(8,128)(2,1)S(1)} %get-tuple-element.42.refs_2_, bf16[384,1792]{1,0:T(8,128)(2,1)S(1)} %get-tuple-element.43.refs_3_, ...), custom_call_target="tpu_custom_call" | custom-call | flops 1 | bytes 1 | tf_op jit(solution)/shard_map/last/pallas_call | solution.py:52
  (35 shorter events, 10.1 us)
Async XLA Ops:
  3.1 3.3 %collective-permute-start = (bf16[4,96,1792]{2,1,0:T(8,128)(2,1)S(1)}, bf16[4,96,1792]{2,1,0:T(8,128)(2,1)S(1)}, u32[]{:S(2)}, u32[]{:S(2)}) collective-permute-start(bf16[4,96,1792]{2,1,0:T(8,128)(2,1)S(1)} %get-tuple-element.24), channel_id=1, source_target_pairs={{0,1},{1,0},{2,3},{3,2},{4,5},{5,4},{6,7},{7,6},{8,9},{9,8},{10,11... | collective-permute-start | bytes 4128776 | tf_op jit(solution)/shard_map/ppermute | solution.py:346
  6.2 4.8 %collective-permute-start.3 = (bf16[4,96,1792]{2,1,0:T(8,128)(2,1)S(1)}, bf16[4,96,1792]{2,1,0:T(8,128)(2,1)S(1)}, u32[]{:S(2)}, u32[]{:S(2)}) collective-permute-start(bf16[4,96,1792]{2,1,0:T(8,128)(2,1)S(1)} %get-tuple-element.28), channel_id=1, source_target_pairs={{0,1},{1,0},{2,3},{3,2},{4,5},{5,4},{6,7},{7,6},{8,9},{9,8},{10,11... | collective-permute-start | bytes 4128776 | tf_op jit(solution)/shard_map/ppermute | solution.py:346
  6.6 11.8 %collective-permute-start.2 = (bf16[2,96,896]{2,1,0:T(8,128)(2,1)S(1)}, bf16[2,96,896]{2,1,0:T(8,128)(2,1)S(1)}, u32[]{:S(2)}, u32[]{:S(2)}) collective-permute-start(bf16[2,96,896]{2,1,0:T(8,128)(2,1)S(1)} %get-tuple-element.27), channel_id=1, source_target_pairs={{0,4},{1,5},{2,6},{3,7},{4,0},{5,1},{6,2},{7,3},{8,12},{9,13},{10,... | collective-permute-start | bytes 1032200 | tf_op jit(solution)/shard_map/ppermute | solution.py:346
  9.5 10.9 %collective-permute-start.1 = (bf16[2,96,896]{2,1,0:T(8,128)(2,1)S(1)}, bf16[2,96,896]{2,1,0:T(8,128)(2,1)S(1)}, u32[]{:S(2)}, u32[]{:S(2)}) collective-permute-start(bf16[2,96,896]{2,1,0:T(8,128)(2,1)S(1)} %get-tuple-element.26.refs_2_), channel_id=1, source_target_pairs={{0,2},{1,3},{2,0},{3,1},{4,6},{5,7},{6,4},{7,5},{8,10},{9,11},{10,... | collective-permute-start | bytes 1032200 | tf_op jit(solution)/shard_map/ppermute | solution.py:346
  11.2 14.6 %collective-permute-start.7 = (bf16[2,96,896]{2,1,0:T(8,128)(2,1)S(1)}, bf16[2,96,896]{2,1,0:T(8,128)(2,1)S(1)}, u32[]{:S(2)}, u32[]{:S(2)}) collective-permute-start(bf16[2,96,896]{2,1,0:T(8,128)(2,1)S(1)} %get-tuple-element.32), channel_id=1, source_target_pairs={{0,4},{1,5},{2,6},{3,7},{4,0},{5,1},{6,2},{7,3},{8,12},{9,13},{10,... | collective-permute-start | bytes 1032200 | tf_op jit(solution)/shard_map/ppermute | solution.py:346
  12.3 15.6 %collective-permute-start.6 = (bf16[2,96,896]{2,1,0:T(8,128)(2,1)S(1)}, bf16[2,96,896]{2,1,0:T(8,128)(2,1)S(1)}, u32[]{:S(2)}, u32[]{:S(2)}) collective-permute-start(bf16[2,96,896]{2,1,0:T(8,128)(2,1)S(1)} %get-tuple-element.29.refs_4_), channel_id=1, source_target_pairs={{0,2},{1,3},{2,0},{3,1},{4,6},{5,7},{6,4},{7,5},{8,10},{9,11},{10,... | collective-permute-start | bytes 1032200 | tf_op jit(solution)/shard_map/ppermute | solution.py:346
  20.6 10.9 %collective-permute-start.5 = (bf16[1,96,896]{2,1,0:T(8,128)(2,1)S(1)}, bf16[1,96,896]{2,1,0:T(8,128)(2,1)S(1)}, u32[]{:S(2)}, u32[]{:S(2)}) collective-permute-start(bf16[1,96,896]{2,1,0:T(8,128)(2,1)S(1)} %get-tuple-element.31), channel_id=1, source_target_pairs={{0,2},{1,3},{2,0},{3,1},{4,6},{5,7},{6,4},{7,5},{8,10},{9,11},{10,... | collective-permute-start | bytes 516104 | tf_op jit(solution)/shard_map/ppermute | solution.py:346
  22.2 9.4 %copy-start = (f32[1,90,3584]{2,0,1:T(1,128)S(1)}, f32[1,90,3584]{2,0,1:T(1,128)}, u32[]{:S(2)}) copy-start(f32[1,90,3584]{2,0,1:T(1,128)} %param.4) | copy-start | bytes 3870724
  22.2 9.4 %copy-start.1 = (s32[1,5]{1,0:T(1,128)S(1)}, s32[1,5]{1,0:T(1,128)}, u32[]{:S(2)}) copy-start(s32[1,5]{1,0:T(1,128)} %refs_0_.5) | copy-start | bytes 64
  22.2 9.4 %collective-permute-start.4 = (bf16[1,96,896]{2,1,0:T(8,128)(2,1)S(1)}, bf16[1,96,896]{2,1,0:T(8,128)(2,1)S(1)}, u32[]{:S(2)}, u32[]{:S(2)}) collective-permute-start(bf16[1,96,896]{2,1,0:T(8,128)(2,1)S(1)} %get-tuple-element.30.refs_4_), channel_id=1, source_target_pairs={{0,4},{1,5},{2,6},{3,7},{4,0},{5,1},{6,2},{7,3},{8,12},{9,13},{10,... | collective-permute-start | bytes 516104 | tf_op jit(solution)/shard_map/ppermute | solution.py:346
  28.0 9.9 %collective-permute-start.9 = (bf16[1,96,896]{2,1,0:T(8,128)(2,1)S(1)}, bf16[1,96,896]{2,1,0:T(8,128)(2,1)S(1)}, u32[]{:S(2)}, u32[]{:S(2)}) collective-permute-start(bf16[1,96,896]{2,1,0:T(8,128)(2,1)S(1)} %get-tuple-element.35), channel_id=1, source_target_pairs={{0,2},{1,3},{2,0},{3,1},{4,6},{5,7},{6,4},{7,5},{8,10},{9,11},{10,... | collective-permute-start | bytes 516104 | tf_op jit(solution)/shard_map/ppermute | solution.py:346
  29.6 8.4 %collective-permute-start.8 = (bf16[1,96,896]{2,1,0:T(8,128)(2,1)S(1)}, bf16[1,96,896]{2,1,0:T(8,128)(2,1)S(1)}, u32[]{:S(2)}, u32[]{:S(2)}) collective-permute-start(bf16[1,96,896]{2,1,0:T(8,128)(2,1)S(1)} %get-tuple-element.33.refs_8_), channel_id=1, source_target_pairs={{0,4},{1,5},{2,6},{3,7},{4,0},{5,1},{6,2},{7,3},{8,12},{9,13},{10,... | collective-permute-start | bytes 516104 | tf_op jit(solution)/shard_map/ppermute | solution.py:346
  32.4 9.6 %collective-permute-start.12 = (bf16[96,1792]{1,0:T(8,128)(2,1)S(1)}, bf16[96,1792]{1,0:T(8,128)(2,1)S(1)}, u32[]{:S(2)}, u32[]{:S(2)}) collective-permute-start(bf16[96,1792]{1,0:T(8,128)(2,1)S(1)} %get-tuple-element.36.refs_8_.refs_0_), channel_id=1, source_target_pairs={{16,8},{25,17},{18,10},{27,19},{20,12},{29,21},{22,14},{31,23}} | collective-permute-start | bytes 1032200 | tf_op jit(solution)/shard_map/ppermute | solution.py:356
  33.1 12.5 %collective-permute-start.11 = (bf16[96,1792]{1,0:T(8,128)(2,1)S(1)}, bf16[96,1792]{1,0:T(8,128)(2,1)S(1)}, u32[]{:S(2)}, u32[]{:S(2)}) collective-permute-start(bf16[96,1792]{1,0:T(8,128)(2,1)S(1)} %get-tuple-element.36.refs_8_.refs_0_), channel_id=1, source_target_pairs={{0,8},{9,17},{2,10},{11,19},{4,12},{13,21},{6,14},{15,23}} | collective-permute-start | bytes 1032200 | tf_op jit(solution)/shard_map/ppermute | solution.py:356
  37.2 8.4 %collective-permute-start.10 = (bf16[96,1792]{1,0:T(8,128)(2,1)S(1)}, bf16[96,1792]{1,0:T(8,128)(2,1)S(1)}, u32[]{:S(2)}, u32[]{:S(2)}) collective-permute-start(bf16[96,1792]{1,0:T(8,128)(2,1)S(1)} %get-tuple-element.36.refs_8_.refs_0_), channel_id=1, source_target_pairs={{24,8},{1,17},{26,10},{3,19},{28,12},{5,21},{30,14},{7,23}} | collective-permute-start | bytes 1032200 | tf_op jit(solution)/shard_map/ppermute | solution.py:356
  38.8 7.7 %collective-permute-start.15 = (bf16[96,1792]{1,0:T(8,128)(2,1)S(1)}, bf16[96,1792]{1,0:T(8,128)(2,1)S(1)}, u32[]{:S(2)}, u32[]{:S(2)}) collective-permute-start(bf16[96,1792]{1,0:T(8,128)(2,1)S(1)} %get-tuple-element.38.refs_4_.refs_1_), channel_id=1, source_target_pairs={{16,8},{25,17},{18,10},{27,19},{20,12},{29,21},{22,14},{31,23}} | collective-permute-start | bytes 1032200 | tf_op jit(solution)/shard_map/ppermute | solution.py:356
  39.5 12.7 %collective-permute-start.14 = (bf16[96,1792]{1,0:T(8,128)(2,1)S(1)}, bf16[96,1792]{1,0:T(8,128)(2,1)S(1)}, u32[]{:S(2)}, u32[]{:S(2)}) collective-permute-start(bf16[96,1792]{1,0:T(8,128)(2,1)S(1)} %get-tuple-element.38.refs_4_.refs_1_), channel_id=1, source_target_pairs={{0,8},{9,17},{2,10},{11,19},{4,12},{13,21},{6,14},{15,23}} | collective-permute-start | bytes 1032200 | tf_op jit(solution)/shard_map/ppermute | solution.py:356
  42.0 10.2 %collective-permute-start.13 = (bf16[96,1792]{1,0:T(8,128)(2,1)S(1)}, bf16[96,1792]{1,0:T(8,128)(2,1)S(1)}, u32[]{:S(2)}, u32[]{:S(2)}) collective-permute-start(bf16[96,1792]{1,0:T(8,128)(2,1)S(1)} %get-tuple-element.38.refs_4_.refs_1_), channel_id=1, source_target_pairs={{24,8},{1,17},{26,10},{3,19},{28,12},{5,21},{30,14},{7,23}} | collective-permute-start | bytes 1032200 | tf_op jit(solution)/shard_map/ppermute | solution.py:356
  57.8 4.6 %collective-permute-start.16 = (bf16[96,3584]{1,0:T(8,128)(2,1)S(1)}, bf16[96,3584]{1,0:T(8,128)(2,1)S(1)}, u32[]{:S(2)}, u32[]{:S(2)}) collective-permute-start(bf16[96,3584]{1,0:T(8,128)(2,1)S(1)} %rows1.1.refs_4_), channel_id=1, source_target_pairs={{8,24},{17,1},{10,26},{19,3},{12,28},{21,5},{14,30},{23,7}} | collective-permute-start | bytes 2064392 | tf_op jit(solution)/shard_map/ppermute | solution.py:360
  59.5 17.8 %collective-permute-start.17 = (bf16[96,3584]{1,0:T(8,128)(2,1)S(1)}, bf16[96,3584]{1,0:T(8,128)(2,1)S(1)}, u32[]{:S(2)}, u32[]{:S(2)}) collective-permute-start(bf16[96,3584]{1,0:T(8,128)(2,1)S(1)} %rows2.1.refs_4_), channel_id=1, source_target_pairs={{8,0},{17,9},{10,2},{19,11},{12,4},{21,13},{14,6},{23,15}} | collective-permute-start | bytes 2064392 | tf_op jit(solution)/shard_map/ppermute | solution.py:360
  61.8 15.6 %collective-permute-start.18 = (bf16[96,3584]{1,0:T(8,128)(2,1)S(1)}, bf16[96,3584]{1,0:T(8,128)(2,1)S(1)}, u32[]{:S(2)}, u32[]{:S(2)}) collective-permute-start(bf16[96,3584]{1,0:T(8,128)(2,1)S(1)} %rows3.1), channel_id=1, source_target_pairs={{8,16},{17,25},{10,18},{19,27},{12,20},{21,29},{14,22},{23,31}} | collective-permute-start | bytes 2064392 | tf_op jit(solution)/shard_map/ppermute | solution.py:360

commit v4 on v3

--- a/solution.py
+++ b/solution.py
@@ -9,8 +9,8 @@
 from jax.sharding import PartitionSpec as P
 
 ITERS = 3
-SHARES = (7, 7)
-STEPS = (('S', 0), ('S', 1), ('H', 0, 0), ('H', 1, 0), ('H', 0, 1), ('H', 1, 1), ('N', 0), ('N', 1))
+SHARES = (8, 6)
+STEPS = (('S', 0), ('S', 1), ('H', 0, 0), ('H', 0, 1), ('H', 1, 0), ('N', 0), ('H', 1, 1), ('N', 1))
 
 momentum_rate = 0.95
 coef_a = 3.4445
@@ -21,7 +21,7 @@
 VMEM_LIMIT = 24 * 1024 * 1024
 LANES = 128
 TILE = 256
-BESIDE = {'gate0': 1, 'gate1': 1, 'nest0': 8.7, 'nest1792': 8.7}
+BESIDE = {'gate1': 1, 'nest0': 16, 'gram0': 0.5, 'fold1_0': 4, 'split2048': 1, 'gate0': 1}
 bf16 = jnp.bfloat16
 f32 = jnp.float32
 
@@ -209,13 +209,26 @@
     return call(body, outs, [offsets, linear, *means], specs, after, hold=False, name="keep")[0]
 
 
+def symmetric(block, size):
+    if size <= TILE or size % LANES:
+        return block(slice(0, size), slice(0, size))
+    left = block(slice(0, size), slice(0, TILE))
+    corner = block(slice(TILE, size), slice(TILE, size))
+    top = jnp.concatenate([left[:TILE], left[TILE:].T], axis=1)
+    return jnp.concatenate([top, jnp.concatenate([left[TILE:], corner], axis=1)], axis=0)
+
+
 def gram_of(parts, stack_ref):
     rows = parts[0].shape[0]
     for i, part in enumerate(parts):
         stack_ref[i * rows : (i + 1) * rows, :] = part[...]
-    return lax.dot_general(
-        stack_ref[...], stack_ref[...], (((1,), (1,)), ((), ())), preferred_element_type=f32
-    )
+
+    def block(down, across):
+        return lax.dot_general(
+            stack_ref[down, :], stack_ref[across, :], (((1,), (1,)), ((), ())), preferred_element_type=f32
+        )
+
+    return symmetric(block, len(parts) * rows)
 
 
 def gram(parts, after, name):
@@ -250,23 +263,24 @@
         power = 1.0
         for iteration in range(ITERS):
             rounded = gram.astype(bf16)
-            square = dot(rounded, rounded)
+            square = symmetric(lambda down, across: dot(rounded[down], rounded[:, across]), size)
             poly = (coef_b * rounded.astype(f32) + coef_c * square).astype(bf16)
+            beside = jnp.concatenate([poly, poly], axis=1)
             if rest is None:
                 rest = poly.astype(f32)
+            elif iteration == 1:
+                rest = coef_a * rest + power * poly.astype(f32) + dot(poly, rest.astype(bf16))
             else:
-                rest_high, rest_low = two(rest)
-                rest = (
-                    coef_a * rest
-                    + power * poly.astype(f32)
-                    + (dot(poly, rest_high) + dot(poly, rest_low))
-                )
+                below = jnp.concatenate(two(rest), axis=0)
+                rest = coef_a * rest + power * poly.astype(f32) + dot(beside, below)
             power = power * coef_a
             if iteration < ITERS - 1:
-                gram_high, gram_low = two(gram)
-                left = coef_a * gram + (dot(poly, gram_high) + dot(poly, gram_low))
-                left_high, left_low = two(left)
-                gram = coef_a * left + (dot(left_high, poly) + dot(left_low, poly))
+                left = coef_a * gram + dot(beside, jnp.concatenate(two(gram), axis=0))
+                halves = jnp.concatenate(two(left), axis=1)
+                twice = jnp.concatenate([poly, poly], axis=0)
+                gram = symmetric(
+                    lambda down, across: coef_a * left[down, across] + dot(halves[down], twice[:, across]), size
+                )
         scale = scale * math.sqrt(full_width)
         high, low = two(rest * scale)
         for i in range(groups):
@@ -312,28 +326,30 @@
     return call(body, [jax.ShapeDtypeStruct((8, LANES), f32)], [], [], after, name=name)[0]
 
 
-def own_or_received(owners, factor, alpha, stacks, received, cap, after):
-    def body(factor_ref, alpha_ref, *refs):
+def own_or_received(owners, own, received, cap, after):
+    def body(own_ref, *refs):
         *inputs, out_ref = refs
         mine = lax.axis_index("fsdp") == owners + lax.rem(lax.axis_index("rep"), 2)
 
         @pl.when(mine)
         def _():
-            apply_rows(0, factor_ref, alpha_ref, inputs[: len(stacks)], out_ref)
+            for row in range(0, cap, 16):
+                to = slice(row, min(row + 16, cap))
+                out_ref[to, :] = own_ref[to, :]
 
         @pl.when(jnp.logical_not(mine))
         def _():
             for row in range(0, cap, 16):
                 to = slice(row, min(row + 16, cap))
-                added = None
-                for came in inputs[len(stacks) :]:
+                total = None
+                for came in inputs:
                     value = came[to, :]
-                    added = value if added is None else added + value
-                out_ref[to, :] = added
-
-    outs = [jax.ShapeDtypeStruct((cap, received[0].shape[1]), bf16)]
-    specs = in_vmem(2 + len(stacks) + len(received))
-    return call(body, outs, [factor, alpha, *stacks, *received], specs, after, hold=False, name="last")[0]
+                    total = value if total is None else total + value
+                out_ref[to, :] = total
+
+    outs = [jax.ShapeDtypeStruct((cap, own.shape[1]), bf16)]
+    specs = in_vmem(1 + len(received))
+    return call(body, outs, [own, *received], specs, after, hold=False, name="last")[0]
 
 
 def per_device(groups, replicas, gradients, momentum, offsets):
@@ -370,24 +386,42 @@
     orders = [bits[1:], bits[1:][::-1]]
     last = ()
 
-    def split_piece(first, wide):
+    def split_piece(first, wide, apart):
         nonlocal last
-        keep, send = split(flat, mats, cap, padded, first, wide, last)
-        last = (keep,)
         half = wide // 2
-        plans = [
-            {2 * i: [(first + side * half, half, [(t, i, side * half) for t in range(2)])] for i in range(mats // 2)}
-            for side in range(2)
-        ]
-        return [keep, swap(send, bits[0])], plans
-
-    def halve(level, terms, plans):
+        terms, plans = [], []
+        for at in (0, half) if apart else (0,):
+            keep, send = split(flat, mats, cap, padded, first + at, half if apart else wide, last)
+            last = (keep,)
+            terms += [keep, swap(send, bits[0])]
+        for side in range(2):
+            sources = (2 * side, 0) if apart else (0, side * half)
+            plans.append(
+                {
+                    2 * i: [(first + side * half, half, [(sources[0] + t, i, sources[1]) for t in range(2)])]
+                    for i in range(mats // 2)
+                }
+            )
+        return terms, plans
+
+    def halve(level, terms, plans, apart):
         nonlocal last
         moving = [[j for j in plan if j & order[level]] for plan, order in zip(plans, orders)]
         wanted = [[[(w, parts) for _, w, parts in plan[j]] for j in away] for plan, away in zip(plans, moving)]
         name = f"fold{level}_{plans[0][0][0][0]}"
-        sends = fold(terms, wanted, padded, last, name)
-        last = (sends[0],)
+        if apart:
+            sends = []
+            for side in range(2):
+                used = sorted({t for segments in wanted[side] for _, parts in segments for t, _, _ in parts})
+                own = [
+                    [(w, [(used.index(t), p, at) for t, p, at in parts]) for w, parts in segments]
+                    for segments in wanted[side]
+                ]
+                sends += fold([terms[t] for t in used], [own], padded, last, f"{name}_{side}")
+                last = (sends[-1],)
+        else:
+            sends = fold(terms, wanted, padded, last, name)
+            last = (sends[0],)
         for side, away in enumerate(moving):
             bit = orders[side][level]
             terms.append(swap(sends[side], bit))
@@ -413,7 +447,7 @@
 
     def halve_next(chunk):
         level = reached[chunk]
-        halve(level, *work[chunk])
+        halve(level, *work[chunk], False)
         arrived[chunk, level] = tuple(work[chunk][0][-2:])
         reached[chunk] += 1
 
@@ -421,7 +455,7 @@
         if more and isinstance(more[-1], tuple):
             last += arrived.get(more[-1], ())
         if kind == "S":
-            work[chunk] = split_piece(*chunks[chunk])
+            work[chunk] = split_piece(*chunks[chunk], False)
         elif kind == "H" and more[0] < levels:
             halve_next(chunk)
         elif kind == "N":
@@ -443,10 +477,12 @@
         result = rows_of(factor, alpha, stacks, k + 1, last)
         last = (result,)
         back.append(from_owner(result, k))
+    results = last
     last = ()
     for k, came in enumerate(back[:-1]):
         last = (gate((came, *last), f"gate{k}"),)
-    update = own_or_received((groups - 1) // 2, factor, alpha, stacks, back, cap, last)
+    own = rows_of(factor, alpha, stacks, 0, results)
+    update = own_or_received((groups - 1) // 2, own, back, cap, last)
     return (kept_state.reshape(1, cap, width), update[None])
 
 

time: 78.6 us -> 77 us (0.980)
  the two profiles are of different devices: /device:TPU:0 before, /device:TPU:16 now
where the time goes in v4:
time: 77 us; the launch traced here: 76.7 us
  waiting for transfers between devices  38 us (49%)
  starting transfers between devices  19.3 us (25%)
  Pallas kernels  18.6 us (24%)
  between operations  0.88 us (1%)
    ppermute x10, waiting for transfers between devices, swap(): return lax.ppermute(value, AXES, pairs)  19.6 us
    pallas_call x18, Pallas kernels, call(): pl.pallas_call(kernel, out_shape=tuple((pltpu.VMEM(o.shape, o.dtype) if h...  18.6 us
    ppermute x3, waiting for transfers between devices, from_owner(): return lax.ppermute(value, AXES, pairs)  18.1 us
    ppermute x10, starting transfers between devices, swap(): return lax.ppermute(value, AXES, pairs)  9 us
    ppermute x6, starting transfers between devices, to_owner(): return lax.ppermute(value, AXES, pairs)  7.61 us
    ppermute x3, starting transfers between devices, from_owner(): return lax.ppermute(value, AXES, pairs)  2.7 us
  transfers between devices with their start and end apart: 19, of which 9 were waited for; matrix products, arithmetic and copies ran while one was open for 0% of the time, Pallas kernels for 13%

profile of v4, /device:TPU:16, one launch (start us, length us, event | category | flops | bytes accessed | tf_op | source)
XLA Modules:
  0.0 76.7 jit_solution(12306776164204479671)
XLA Ops:
  0.6 2.6 %split0.1 = (bf16[4,96,2048]{2,1,0:T(8,128)(2,1)S(1)}, bf16[4,96,2048]{2,1,0:T(8,128)(2,1)S(1)}) custom-call(bf16[720,3584]{1,0:T(8,128)(2,1)} %bitcast.11), custom_call_target="tpu_custom_call" | custom-call | flops 1 | bytes 1 | tf_op jit(solution)/shard_map/split0/pallas_call | solution.py:52
  3.3 2.3 %split2048.1 = (bf16[4,96,1536]{2,1,0:T(8,128)(2,1)S(1)}, bf16[4,96,1536]{2,1,0:T(8,128)(2,1)S(1)}) custom-call(bf16[720,3584]{1,0:T(8,128)(2,1)} %bitcast.12, bf16[4,96,2048]{2,1,0:T(8,128)(2,1)S(1)} %get-tuple-element.23.refs_1_.refs_0_.refs_2_), custom_call_target="tpu_custom_call" | custom-call | flops 1150000000 | bytes 1 | tf_op jit(solution)/shard_map/split2048/pallas_call | solution.py:52
  6.9 1.6 %collective-permute-start.2 = (bf16[2,96,1024]{2,1,0:T(8,128)(2,1)S(1)}, bf16[2,96,1024]{2,1,0:T(8,128)(2,1)S(1)}, u32[]{:S(2)}, u32[]{:S(2)}) collective-permute-start(bf16[2,96,1024]{2,1,0:T(8,128)(2,1)S(1)} %get-tuple-element.27), channel_id=1, source_target_pairs={{0,4},{1,5},{2,6},{3,7},{4,0},{5,1},{6,2},{7,3},{8,12},{9,13},{10,... | collective-permute-start | bytes 1179656 | tf_op jit(solution)/shard_map/ppermute | solution.py:362
  8.5 1.5 %collective-permute-start.1 = (bf16[2,96,1024]{2,1,0:T(8,128)(2,1)S(1)}, bf16[2,96,1024]{2,1,0:T(8,128)(2,1)S(1)}, u32[]{:S(2)}, u32[]{:S(2)}) collective-permute-start(bf16[2,96,1024]{2,1,0:T(8,128)(2,1)S(1)} %get-tuple-element.26.refs_4_), channel_id=1, source_target_pairs={{0,2},{1,3},{2,0},{3,1},{4,6},{5,7},{6,4},{7,5},{8,10},{9,11},{10,... | collective-permute-start | bytes 1179656 | tf_op jit(solution)/shard_map/ppermute | solution.py:362
  10.0 8.1 %collective-permute-done.2.refs_3_.refs_5_ = bf16[2,96,1024]{2,1,0:T(8,128)(2,1)S(1)} collective-permute-done((bf16[2,96,1024]{2,1,0:T(8,128)(2,1)S(1)}, bf16[2,96,1024]{2,1,0:T(8,128)(2,1)S(1)}, u32[]{:S(2)}, u32[]{:S(2)}) %collective-permute-start.2) | collective-permute-done | bytes 393248 | tf_op jit(solution)/shard_map/ppermute | solution.py:362
  18.1 1.2 %collective-permute-done.1.refs_2_.refs_4_ = bf16[2,96,1024]{2,1,0:T(8,128)(2,1)S(1)} collective-permute-done((bf16[2,96,1024]{2,1,0:T(8,128)(2,1)S(1)}, bf16[2,96,1024]{2,1,0:T(8,128)(2,1)S(1)}, u32[]{:S(2)}, u32[]{:S(2)}) %collective-permute-start.1) | collective-permute-done | bytes 393248 | tf_op jit(solution)/shard_map/ppermute | solution.py:362
  19.5 1.6 %collective-permute-start.4 = (bf16[1,96,1024]{2,1,0:T(8,128)(2,1)S(1)}, bf16[1,96,1024]{2,1,0:T(8,128)(2,1)S(1)}, u32[]{:S(2)}, u32[]{:S(2)}) collective-permute-start(bf16[1,96,1024]{2,1,0:T(8,128)(2,1)S(1)} %get-tuple-element.29), channel_id=1, source_target_pairs={{0,2},{1,3},{2,0},{3,1},{4,6},{5,7},{6,4},{7,5},{8,10},{9,11},{10,... | collective-permute-start | bytes 589832 | tf_op jit(solution)/shard_map/ppermute | solution.py:362
  21.7 1.6 %collective-permute-start.7 = (bf16[2,96,768]{2,1,0:T(8,128)(2,1)S(1)}, bf16[2,96,768]{2,1,0:T(8,128)(2,1)S(1)}, u32[]{:S(2)}, u32[]{:S(2)}) collective-permute-start(bf16[2,96,768]{2,1,0:T(8,128)(2,1)S(1)} %get-tuple-element.33), channel_id=1, source_target_pairs={{0,4},{1,5},{2,6},{3,7},{4,0},{5,1},{6,2},{7,3},{8,12},{9,13},{10,... | collective-permute-start | bytes 884744 | tf_op jit(solution)/shard_map/ppermute | solution.py:362
  23.8 2.9 %collective-permute-done.4.refs_7_ = bf16[1,96,1024]{2,1,0:T(8,128)(2,1)S(1)} collective-permute-done((bf16[1,96,1024]{2,1,0:T(8,128)(2,1)S(1)}, bf16[1,96,1024]{2,1,0:T(8,128)(2,1)S(1)}, u32[]{:S(2)}, u32[]{:S(2)}) %collective-permute-start.4) | collective-permute-done | bytes 196640 | tf_op jit(solution)/shard_map/ppermute | solution.py:362
  26.7 2.2 %collective-permute-done.3.refs_6_ = bf16[1,96,1024]{2,1,0:T(8,128)(2,1)S(1)} collective-permute-done((bf16[1,96,1024]{2,1,0:T(8,128)(2,1)S(1)}, bf16[1,96,1024]{2,1,0:T(8,128)(2,1)S(1)}, u32[]{:S(2)}, u32[]{:S(2)}) %collective-permute-start.3) | collective-permute-done | bytes 196640 | tf_op jit(solution)/shard_map/ppermute | solution.py:362
  28.9 0.9 %nest0.1 = (bf16[96,2048]{1,0:T(8,128)(2,1)S(1)}, f32[96,2048]{1,0:T(8,128)S(1)}) custom-call(s32[1,5]{1,0:T(1,128)S(1)} %copy-done.1, f32[2520,128]{1,0:T(8,128)S(1)} %bitcast.8, bf16[4,96,2048]{2,1,0:T(8,128)(2,1)S(1)} %get-tuple-element.23.refs_1_.refs_0_.refs_2_, bf16[4,96,2048]{2,1,0:T(8,128)(2,1)S(1)} %collective-permute-done.refs_1_.refs_3_, ...), custom_call_target="tpu_custom_call" | custom-call | flops 18400000000 | bytes 1 | tf_op jit(solution)/shard_map/nest0/pallas_call | solution.py:52
  29.8 2.4 %collective-permute-start.12 = (bf16[96,2048]{1,0:T(8,128)(2,1)S(1)}, bf16[96,2048]{1,0:T(8,128)(2,1)S(1)}, u32[]{:S(2)}, u32[]{:S(2)}) collective-permute-start(bf16[96,2048]{1,0:T(8,128)(2,1)S(1)} %get-tuple-element.34.refs_4_.refs_0_), channel_id=1, source_target_pairs={{16,8},{25,17},{18,10},{27,19},{20,12},{29,21},{22,14},{31,23}} | collective-permute-start | bytes 1179656 | tf_op jit(solution)/shard_map/ppermute | solution.py:372
  34.8 4.1 %collective-permute-done.9.refs_7_ = bf16[1,96,768]{2,1,0:T(8,128)(2,1)S(1)} collective-permute-done((bf16[1,96,768]{2,1,0:T(8,128)(2,1)S(1)}, bf16[1,96,768]{2,1,0:T(8,128)(2,1)S(1)}, u32[]{:S(2)}, u32[]{:S(2)}) %collective-permute-start.9) | collective-permute-done | bytes 147488 | tf_op jit(solution)/shard_map/ppermute | solution.py:362
  39.5 0.8 %nest2048.1 = (bf16[96,1536]{1,0:T(8,128)(2,1)S(1)}, f32[96,1536]{1,0:T(8,128)S(1)}) custom-call(s32[1,5]{1,0:T(1,128)S(1)} %copy-done.1, f32[2520,128]{1,0:T(8,128)S(1)} %bitcast.9, bf16[4,96,1536]{2,1,0:T(8,128)(2,1)S(1)} %get-tuple-element.25.refs_2_.refs_0_, bf16[4,96,1536]{2,1,0:T(8,128)(2,1)S(1)} %collective-permute-done.5.refs_1_.refs_3_, ...), custom_call_target="tpu_custom_call" | custom-call | flops 1 | bytes 1 | tf_op jit(solution)/shard_map/nest2048/pallas_call | solution.py:52
  40.3 2.5 %collective-permute-start.15 = (bf16[96,1536]{1,0:T(8,128)(2,1)S(1)}, bf16[96,1536]{1,0:T(8,128)(2,1)S(1)}, u32[]{:S(2)}, u32[]{:S(2)}) collective-permute-start(bf16[96,1536]{1,0:T(8,128)(2,1)S(1)} %get-tuple-element.38.refs_4_.refs_1_), channel_id=1, source_target_pairs={{16,8},{25,17},{18,10},{27,19},{20,12},{29,21},{22,14},{31,23}} | collective-permute-start | bytes 884744 | tf_op jit(solution)/shard_map/ppermute | solution.py:372
  44.2 1.8 %keep.1.refs_4_ = f32[2520,128]{1,0:T(8,128)} custom-call(s32[1,5]{1,0:T(1,128)S(1)} %copy-done.1, f32[2520,128]{1,0:T(8,128)S(1)} %bitcast.10, f32[96,2048]{1,0:T(8,128)S(1)} %get-tuple-element.32.refs_2_, f32[96,1536]{1,0:T(8,128)S(1)} %get-tuple-element.37.refs_3_, bf16[96,1536]{1,0:T(8,128)(2,1)S(1)} %get-tuple-element.38.refs_4_.refs_1_), custom_call_target="tpu_custom_call" | custom-call | flops 1 | bytes 1 | tf_op jit(solution)/shard_map/keep/pallas_call | solution.py:52
  47.0 4.0 %chain.1 = (bf16[384,1536]{1,0:T(8,128)(2,1)S(1)}, bf16[4,192,384]{2,1,0:T(8,128)(2,1)S(1)}, f32[8,128]{1,0:T(8,128)S(1)}) custom-call(f32[384,384]{1,0:T(8,128)S(1)} %get-tuple-element.39.refs_0_, bf16[96,1536]{1,0:T(8,128)(2,1)S(1)} %get-tuple-element.38.refs_4_.refs_1_, bf16[96,1536]{1,0:T(8,128)(2,1)S(1)} %collective-permute-done.13.refs_2_, ...), custom_call_target="tpu_custom_call" | custom-call | flops 1 | bytes 1 | tf_op jit(solution)/shard_map/chain/pallas_call | solution.py:52
  51.1 0.9 %rows1.1.refs_4_ = bf16[96,3584]{1,0:T(8,128)(2,1)S(1)} custom-call(bf16[4,192,384]{2,1,0:T(8,128)(2,1)S(1)} %get-tuple-element.40.refs_0_, f32[8,128]{1,0:T(8,128)S(1)} %get-tuple-element.41.refs_1_, bf16[384,2048]{1,0:T(8,128)(2,1)S(1)} %get-tuple-element.42.refs_2_, bf16[384,1536]{1,0:T(8,128)(2,1)S(1)} %get-tuple-element.43.refs_3_), custom_call_target="tpu_custom_call" | custom-call | flops 1 | bytes 1 | tf_op jit(solution)/shard_map/rows1/pallas_call | solution.py:52
  52.7 0.9 %rows2.1.refs_4_ = bf16[96,3584]{1,0:T(8,128)(2,1)S(1)} custom-call(bf16[4,192,384]{2,1,0:T(8,128)(2,1)S(1)} %get-tuple-element.40.refs_0_, f32[8,128]{1,0:T(8,128)S(1)} %get-tuple-element.41.refs_1_, bf16[384,2048]{1,0:T(8,128)(2,1)S(1)} %get-tuple-element.42.refs_2_, bf16[384,1536]{1,0:T(8,128)(2,1)S(1)} %get-tuple-element.43.refs_3_, ...), custom_call_target="tpu_custom_call" | custom-call | flops 1 | bytes 1 | tf_op jit(solution)/shard_map/rows2/pallas_call | solution.py:52
  54.4 0.9 %rows3.1.refs_4_ = bf16[96,3584]{1,0:T(8,128)(2,1)S(1)} custom-call(bf16[4,192,384]{2,1,0:T(8,128)(2,1)S(1)} %get-tuple-element.40.refs_0_, f32[8,128]{1,0:T(8,128)S(1)} %get-tuple-element.41.refs_1_, bf16[384,2048]{1,0:T(8,128)(2,1)S(1)} %get-tuple-element.42.refs_2_, bf16[384,1536]{1,0:T(8,128)(2,1)S(1)} %get-tuple-element.43.refs_3_, ...), custom_call_target="tpu_custom_call" | custom-call | flops 1 | bytes 1 | tf_op jit(solution)/shard_map/rows3/pallas_call | solution.py:52
  55.3 1.3 %collective-permute-start.18 = (bf16[96,3584]{1,0:T(8,128)(2,1)S(1)}, bf16[96,3584]{1,0:T(8,128)(2,1)S(1)}, u32[]{:S(2)}, u32[]{:S(2)}) collective-permute-start(bf16[96,3584]{1,0:T(8,128)(2,1)S(1)} %rows3.1.refs_4_), channel_id=1, source_target_pairs={{8,16},{17,25},{10,18},{19,27},{12,20},{21,29},{14,22},{23,31}} | collective-permute-start | bytes 2064392 | tf_op jit(solution)/shard_map/ppermute | solution.py:376
  56.6 0.9 %rows0.1.refs_0_ = bf16[96,3584]{1,0:T(8,128)(2,1)S(1)} custom-call(bf16[4,192,384]{2,1,0:T(8,128)(2,1)S(1)} %get-tuple-element.40.refs_0_, f32[8,128]{1,0:T(8,128)S(1)} %get-tuple-element.41.refs_1_, bf16[384,2048]{1,0:T(8,128)(2,1)S(1)} %get-tuple-element.42.refs_2_, bf16[384,1536]{1,0:T(8,128)(2,1)S(1)} %get-tuple-element.43.refs_3_, ...), custom_call_target="tpu_custom_call" | custom-call | flops 1 | bytes 1 | tf_op jit(solution)/shard_map/rows0/pallas_call | solution.py:52
  57.6 18.1 %collective-permute-done.18.refs_3_ = bf16[96,3584]{1,0:T(8,128)(2,1)S(1)} collective-permute-done((bf16[96,3584]{1,0:T(8,128)(2,1)S(1)}, bf16[96,3584]{1,0:T(8,128)(2,1)S(1)}, u32[]{:S(2)}, u32[]{:S(2)}) %collective-permute-start.18) | collective-permute-done | bytes 688160 | tf_op jit(solution)/shard_map/ppermute | solution.py:376
  75.8 0.9 %last.1 = bf16[90,3584]{1,0:T(8,128)(2,1)} custom-call(bf16[96,3584]{1,0:T(8,128)(2,1)S(1)} %rows0.1.refs_0_, bf16[96,3584]{1,0:T(8,128)(2,1)S(1)} %collective-permute-done.16.refs_0_.refs_1_, bf16[96,3584]{1,0:T(8,128)(2,1)S(1)} %collective-permute-done.17.refs_0_.refs_2_, bf16[96,3584]{1,0:T(8,128)(2,1)S(1)} %collective-permute-done.18.refs_3_, ...), custom_call_target="tpu_custom_call" | custom-call | flops 1 | bytes 1 | tf_op jit(solution)/shard_map/last/pallas_call | solution.py:52
  (36 shorter events, 9.6 us)
Async XLA Ops:
  3.2 3.5 %collective-permute-start = (bf16[4,96,2048]{2,1,0:T(8,128)(2,1)S(1)}, bf16[4,96,2048]{2,1,0:T(8,128)(2,1)S(1)}, u32[]{:S(2)}, u32[]{:S(2)}) collective-permute-start(bf16[4,96,2048]{2,1,0:T(8,128)(2,1)S(1)} %get-tuple-element.24), channel_id=1, source_target_pairs={{0,1},{1,0},{2,3},{3,2},{4,5},{5,4},{6,7},{7,6},{8,9},{9,8},{10,11... | collective-permute-start | bytes 4718600 | tf_op jit(solution)/shard_map/ppermute | solution.py:362
  5.6 16.0 %collective-permute-start.5 = (bf16[4,96,1536]{2,1,0:T(8,128)(2,1)S(1)}, bf16[4,96,1536]{2,1,0:T(8,128)(2,1)S(1)}, u32[]{:S(2)}, u32[]{:S(2)}) collective-permute-start(bf16[4,96,1536]{2,1,0:T(8,128)(2,1)S(1)} %get-tuple-element.30), channel_id=1, source_target_pairs={{0,1},{1,0},{2,3},{3,2},{4,5},{5,4},{6,7},{7,6},{8,9},{9,8},{10,11... | collective-permute-start | bytes 3538952 | tf_op jit(solution)/shard_map/ppermute | solution.py:362
  6.9 11.2 %collective-permute-start.2 = (bf16[2,96,1024]{2,1,0:T(8,128)(2,1)S(1)}, bf16[2,96,1024]{2,1,0:T(8,128)(2,1)S(1)}, u32[]{:S(2)}, u32[]{:S(2)}) collective-permute-start(bf16[2,96,1024]{2,1,0:T(8,128)(2,1)S(1)} %get-tuple-element.27), channel_id=1, source_target_pairs={{0,4},{1,5},{2,6},{3,7},{4,0},{5,1},{6,2},{7,3},{8,12},{9,13},{10,... | collective-permute-start | bytes 1179656 | tf_op jit(solution)/shard_map/ppermute | solution.py:362
  8.5 10.9 %collective-permute-start.1 = (bf16[2,96,1024]{2,1,0:T(8,128)(2,1)S(1)}, bf16[2,96,1024]{2,1,0:T(8,128)(2,1)S(1)}, u32[]{:S(2)}, u32[]{:S(2)}) collective-permute-start(bf16[2,96,1024]{2,1,0:T(8,128)(2,1)S(1)} %get-tuple-element.26.refs_4_), channel_id=1, source_target_pairs={{0,2},{1,3},{2,0},{3,1},{4,6},{5,7},{6,4},{7,5},{8,10},{9,11},{10,... | collective-permute-start | bytes 1179656 | tf_op jit(solution)/shard_map/ppermute | solution.py:362
  19.5 9.4 %copy-start = (f32[1,90,3584]{2,0,1:T(1,128)S(1)}, f32[1,90,3584]{2,0,1:T(1,128)}, u32[]{:S(2)}) copy-start(f32[1,90,3584]{2,0,1:T(1,128)} %param.4) | copy-start | bytes 3870724
  19.5 9.4 %copy-start.1 = (s32[1,5]{1,0:T(1,128)S(1)}, s32[1,5]{1,0:T(1,128)}, u32[]{:S(2)}) copy-start(s32[1,5]{1,0:T(1,128)} %refs_0_.5) | copy-start | bytes 64
  19.5 7.2 %collective-permute-start.4 = (bf16[1,96,1024]{2,1,0:T(8,128)(2,1)S(1)}, bf16[1,96,1024]{2,1,0:T(8,128)(2,1)S(1)}, u32[]{:S(2)}, u32[]{:S(2)}) collective-permute-start(bf16[1,96,1024]{2,1,0:T(8,128)(2,1)S(1)} %get-tuple-element.29), channel_id=1, source_target_pairs={{0,2},{1,3},{2,0},{3,1},{4,6},{5,7},{6,4},{7,5},{8,10},{9,11},{10,... | collective-permute-start | bytes 589832 | tf_op jit(solution)/shard_map/ppermute | solution.py:362
  21.1 7.8 %collective-permute-start.3 = (bf16[1,96,1024]{2,1,0:T(8,128)(2,1)S(1)}, bf16[1,96,1024]{2,1,0:T(8,128)(2,1)S(1)}, u32[]{:S(2)}, u32[]{:S(2)}) collective-permute-start(bf16[1,96,1024]{2,1,0:T(8,128)(2,1)S(1)} %get-tuple-element.28.refs_2_), channel_id=1, source_target_pairs={{0,4},{1,5},{2,6},{3,7},{4,0},{5,1},{6,2},{7,3},{8,12},{9,13},{10,... | collective-permute-start | bytes 589832 | tf_op jit(solution)/shard_map/ppermute | solution.py:362
  21.7 11.9 %collective-permute-start.7 = (bf16[2,96,768]{2,1,0:T(8,128)(2,1)S(1)}, bf16[2,96,768]{2,1,0:T(8,128)(2,1)S(1)}, u32[]{:S(2)}, u32[]{:S(2)}) collective-permute-start(bf16[2,96,768]{2,1,0:T(8,128)(2,1)S(1)} %get-tuple-element.33), channel_id=1, source_target_pairs={{0,4},{1,5},{2,6},{3,7},{4,0},{5,1},{6,2},{7,3},{8,12},{9,13},{10,... | collective-permute-start | bytes 884744 | tf_op jit(solution)/shard_map/ppermute | solution.py:362
  23.3 10.3 %collective-permute-start.6 = (bf16[2,96,768]{2,1,0:T(8,128)(2,1)S(1)}, bf16[2,96,768]{2,1,0:T(8,128)(2,1)S(1)}, u32[]{:S(2)}, u32[]{:S(2)}) collective-permute-start(bf16[2,96,768]{2,1,0:T(8,128)(2,1)S(1)} %get-tuple-element.31.refs_8_), channel_id=1, source_target_pairs={{0,2},{1,3},{2,0},{3,1},{4,6},{5,7},{6,4},{7,5},{8,10},{9,11},{10,... | collective-permute-start | bytes 884744 | tf_op jit(solution)/shard_map/ppermute | solution.py:362
  29.8 13.7 %collective-permute-start.12 = (bf16[96,2048]{1,0:T(8,128)(2,1)S(1)}, bf16[96,2048]{1,0:T(8,128)(2,1)S(1)}, u32[]{:S(2)}, u32[]{:S(2)}) collective-permute-start(bf16[96,2048]{1,0:T(8,128)(2,1)S(1)} %get-tuple-element.34.refs_4_.refs_0_), channel_id=1, source_target_pairs={{16,8},{25,17},{18,10},{27,19},{20,12},{29,21},{22,14},{31,23}} | collective-permute-start | bytes 1179656 | tf_op jit(solution)/shard_map/ppermute | solution.py:372
  32.2 13.8 %collective-permute-start.11 = (bf16[96,2048]{1,0:T(8,128)(2,1)S(1)}, bf16[96,2048]{1,0:T(8,128)(2,1)S(1)}, u32[]{:S(2)}, u32[]{:S(2)}) collective-permute-start(bf16[96,2048]{1,0:T(8,128)(2,1)S(1)} %get-tuple-element.34.refs_4_.refs_0_), channel_id=1, source_target_pairs={{0,8},{9,17},{2,10},{11,19},{4,12},{13,21},{6,14},{15,23}} | collective-permute-start | bytes 1179656 | tf_op jit(solution)/shard_map/ppermute | solution.py:372
  32.9 13.1 %collective-permute-start.10 = (bf16[96,2048]{1,0:T(8,128)(2,1)S(1)}, bf16[96,2048]{1,0:T(8,128)(2,1)S(1)}, u32[]{:S(2)}, u32[]{:S(2)}) collective-permute-start(bf16[96,2048]{1,0:T(8,128)(2,1)S(1)} %get-tuple-element.34.refs_4_.refs_0_), channel_id=1, source_target_pairs={{24,8},{1,17},{26,10},{3,19},{28,12},{5,21},{30,14},{7,23}} | collective-permute-start | bytes 1179656 | tf_op jit(solution)/shard_map/ppermute | solution.py:372
  33.7 5.2 %collective-permute-start.9 = (bf16[1,96,768]{2,1,0:T(8,128)(2,1)S(1)}, bf16[1,96,768]{2,1,0:T(8,128)(2,1)S(1)}, u32[]{:S(2)}, u32[]{:S(2)}) collective-permute-start(bf16[1,96,768]{2,1,0:T(8,128)(2,1)S(1)} %get-tuple-element.36), channel_id=1, source_target_pairs={{0,2},{1,3},{2,0},{3,1},{4,6},{5,7},{6,4},{7,5},{8,10},{9,11},{10,... | collective-permute-start | bytes 442376 | tf_op jit(solution)/shard_map/ppermute | solution.py:362
  34.3 5.1 %collective-permute-start.8 = (bf16[1,96,768]{2,1,0:T(8,128)(2,1)S(1)}, bf16[1,96,768]{2,1,0:T(8,128)(2,1)S(1)}, u32[]{:S(2)}, u32[]{:S(2)}) collective-permute-start(bf16[1,96,768]{2,1,0:T(8,128)(2,1)S(1)} %get-tuple-element.35.refs_8_), channel_id=1, source_target_pairs={{0,4},{1,5},{2,6},{3,7},{4,0},{5,1},{6,2},{7,3},{8,12},{9,13},{10,... | collective-permute-start | bytes 442376 | tf_op jit(solution)/shard_map/ppermute | solution.py:362
  40.3 6.7 %collective-permute-start.15 = (bf16[96,1536]{1,0:T(8,128)(2,1)S(1)}, bf16[96,1536]{1,0:T(8,128)(2,1)S(1)}, u32[]{:S(2)}, u32[]{:S(2)}) collective-permute-start(bf16[96,1536]{1,0:T(8,128)(2,1)S(1)} %get-tuple-element.38.refs_4_.refs_1_), channel_id=1, source_target_pairs={{16,8},{25,17},{18,10},{27,19},{20,12},{29,21},{22,14},{31,23}} | collective-permute-start | bytes 884744 | tf_op jit(solution)/shard_map/ppermute | solution.py:372
  42.8 4.2 %collective-permute-start.14 = (bf16[96,1536]{1,0:T(8,128)(2,1)S(1)}, bf16[96,1536]{1,0:T(8,128)(2,1)S(1)}, u32[]{:S(2)}, u32[]{:S(2)}) collective-permute-start(bf16[96,1536]{1,0:T(8,128)(2,1)S(1)} %get-tuple-element.38.refs_4_.refs_1_), channel_id=1, source_target_pairs={{0,8},{9,17},{2,10},{11,19},{4,12},{13,21},{6,14},{15,23}} | collective-permute-start | bytes 884744 | tf_op jit(solution)/shard_map/ppermute | solution.py:372
  43.5 3.5 %collective-permute-start.13 = (bf16[96,1536]{1,0:T(8,128)(2,1)S(1)}, bf16[96,1536]{1,0:T(8,128)(2,1)S(1)}, u32[]{:S(2)}, u32[]{:S(2)}) collective-permute-start(bf16[96,1536]{1,0:T(8,128)(2,1)S(1)} %get-tuple-element.38.refs_4_.refs_1_), channel_id=1, source_target_pairs={{24,8},{1,17},{26,10},{3,19},{28,12},{5,21},{30,14},{7,23}} | collective-permute-start | bytes 884744 | tf_op jit(solution)/shard_map/ppermute | solution.py:372
  52.0 5.6 %collective-permute-start.16 = (bf16[96,3584]{1,0:T(8,128)(2,1)S(1)}, bf16[96,3584]{1,0:T(8,128)(2,1)S(1)}, u32[]{:S(2)}, u32[]{:S(2)}) collective-permute-start(bf16[96,3584]{1,0:T(8,128)(2,1)S(1)} %rows1.1.refs_4_), channel_id=1, source_target_pairs={{8,24},{17,1},{10,26},{19,3},{12,28},{21,5},{14,30},{23,7}} | collective-permute-start | bytes 2064392 | tf_op jit(solution)/shard_map/ppermute | solution.py:376
  53.7 3.9 %collective-permute-start.17 = (bf16[96,3584]{1,0:T(8,128)(2,1)S(1)}, bf16[96,3584]{1,0:T(8,128)(2,1)S(1)}, u32[]{:S(2)}, u32[]{:S(2)}) collective-permute-start(bf16[96,3584]{1,0:T(8,128)(2,1)S(1)} %rows2.1.refs_4_), channel_id=1, source_target_pairs={{8,0},{17,9},{10,2},{19,11},{12,4},{21,13},{14,6},{23,15}} | collective-permute-start | bytes 2064392 | tf_op jit(solution)/shard_map/ppermute | solution.py:376
  55.3 20.4 %collective-permute-start.18 = (bf16[96,3584]{1,0:T(8,128)(2,1)S(1)}, bf16[96,3584]{1,0:T(8,128)(2,1)S(1)}, u32[]{:S(2)}, u32[]{:S(2)}) collective-permute-start(bf16[96,3584]{1,0:T(8,128)(2,1)S(1)} %rows3.1.refs_4_), channel_id=1, source_target_pairs={{8,16},{17,25},{10,18},{19,27},{12,20},{21,29},{14,22},{23,31}} | collective-permute-start | bytes 2064392 | tf_op jit(solution)/shard_map/ppermute | solution.py:376

commit v5 on v4

--- a/solution.py
+++ b/solution.py
@@ -9,8 +9,8 @@
 from jax.sharding import PartitionSpec as P
 
 ITERS = 3
-SHARES = (8, 6)
-STEPS = (('S', 0), ('S', 1), ('H', 0, 0), ('H', 0, 1), ('H', 1, 0), ('N', 0), ('H', 1, 1), ('N', 1))
+SHARES = (7, 7)
+STEPS = (('S', 0), ('S', 1), ('H', 0, 0), ('H', 1, 0), ('H', 0, 1), ('H', 1, 1), ('N', 0), ('N', 1))
 
 momentum_rate = 0.95
 coef_a = 3.4445
@@ -21,7 +21,7 @@
 VMEM_LIMIT = 24 * 1024 * 1024
 LANES = 128
 TILE = 256
-BESIDE = {'gate1': 1, 'nest0': 16, 'gram0': 0.5, 'fold1_0': 4, 'split2048': 1, 'gate0': 1}
+BESIDE = {'gate0': 1, 'gate1': 1, 'nest0': 8.7, 'nest1792': 8.7}
 bf16 = jnp.bfloat16
 f32 = jnp.float32
 
@@ -82,7 +82,15 @@
         in_row = lax.broadcasted_iota(jnp.int32, (size, size), 1)
         place = out_row // rows
         within = out_row - place * rows
-        j = jnp.where(place < half, 2 * place, 2 * (place - half) + 1)
+        kept = place < half
+        order = jnp.where(kept, place, place - half)
+        reverse = jnp.zeros_like(order)
+        high = half.bit_length() - 1
+        for bit in range(high):
+            reverse = reverse + ((order >> bit) & 1) * (1 << (high - 1 - bit))
+        odd = lax.rem(me, 2)
+        turned = jnp.where(kept, odd, 1 - odd) == 1
+        j = 2 * jnp.where(turned, reverse, order) + jnp.where(kept, 0, 1)
         matrix = jnp.bitwise_xor(j, me)
         chosen = {}
         for block, start in enumerate(starts):
@@ -299,8 +307,10 @@
 def apply_rows(index, factor_ref, alpha_ref, stacks, out_ref):
     rows = factor_ref.shape[1] // 2
     height = out_ref.shape[0]
-    left = factor_ref[index]
-    own = slice(index * rows, (index + 1) * rows)
+    even, odd = index
+    block = jnp.where(lax.rem(lax.axis_index("rep"), 2) == 0, even, odd)
+    left = factor_ref[block]
+    own = pl.ds(pl.multiple_of(block * rows, rows), rows)
     first = 0
     for stack_ref in stacks:
         for at in range(0, stack_ref.shape[1], TILE):
@@ -316,7 +326,7 @@
         apply_rows(index, factor_ref, alpha_ref, refs[:-1], refs[-1])
 
     outs = [jax.ShapeDtypeStruct((factor.shape[1] // 2, sum(s.shape[1] for s in stacks)), bf16)]
-    return call(body, outs, [factor, alpha, *stacks], in_vmem(2 + len(stacks)), after, name=f"rows{index}")[0]
+    return call(body, outs, [factor, alpha, *stacks], in_vmem(2 + len(stacks)), after, name=f"rows{index[0]}")[0]
 
 
 def gate(after, name):
@@ -358,7 +368,12 @@
     bits = [1 << i for i in range(replicas.bit_length() - 1)]
 
     def swap(value, bit):
-        pairs = [(f * replicas + r, f * replicas + (r ^ bit)) for f in range(groups) for r in range(replicas)]
+        def partner(r):
+            if r % 2 and bit > 1:
+                return r ^ bits[1:][::-1][bits.index(bit) - 1]
+            return r ^ bit
+
+        pairs = [(f * replicas + r, f * replicas + partner(r)) for f in range(groups) for r in range(replicas)]
         return lax.ppermute(value, AXES, pairs)
 
     def owner(r):
@@ -372,8 +387,14 @@
         return lax.ppermute(value, AXES, pairs)
 
     def from_owner(value, k):
-        pairs = [(owner(r) * replicas + r, others(r)[k] * replicas + r) for r in range(replicas)]
+        pairs = [(owner(r) * replicas + r, returns(r)[k] * replicas + r) for r in range(replicas)]
         return lax.ppermute(value, AXES, pairs)
+
+    def returns(r):
+        return sorted(others(r), key=lambda f: f > 0)
+
+    def place(r, k):
+        return others(r).index(returns(r)[k]) + 1
 
     flat = jnp.transpose(gradients[0], (1, 0, 2)).reshape(cap * mats, width)
     linear = momentum[0].reshape(cap * (width // LANES), LANES)
@@ -474,14 +495,14 @@
     back = []
     last = ()
     for k in range(groups - 1):
-        result = rows_of(factor, alpha, stacks, k + 1, last)
+        result = rows_of(factor, alpha, stacks, (place(0, k), place(1, k)), last)
         last = (result,)
         back.append(from_owner(result, k))
     results = last
     last = ()
     for k, came in enumerate(back[:-1]):
         last = (gate((came, *last), f"gate{k}"),)
-    own = rows_of(factor, alpha, stacks, 0, results)
+    own = rows_of(factor, alpha, stacks, (0, 0), results)
     update = own_or_received((groups - 1) // 2, own, back, cap, last)
     return (kept_state.reshape(1, cap, width), update[None])
 

time: 77 us -> 77.6 us (level)
  the two profiles are of different devices: /device:TPU:16 before, /device:TPU:0 now
where the time goes in v5:
time: 77.6 us; the launch traced here: 76.9 us
  waiting for transfers between devices  32.4 us (42%)
  starting transfers between devices  24.7 us (32%)
  Pallas kernels  18.9 us (24%)
  between operations  0.84 us (1%)
    pallas_call x18, Pallas kernels, call(): pl.pallas_call(kernel, out_shape=tuple((pltpu.VMEM(o.shape, o.dtype) if h...  18.9 us
    ppermute x3, waiting for transfers between devices, from_owner(): return lax.ppermute(value, AXES, pairs)  14.6 us
    ppermute x10, starting transfers between devices, swap(): return lax.ppermute(value, AXES, pairs)  12.6 us
    ppermute x10, waiting for transfers between devices, swap(): return lax.ppermute(value, AXES, pairs)  11.2 us
    ppermute x6, starting transfers between devices, to_owner(): return lax.ppermute(value, AXES, pairs)  9.38 us
    ppermute x6, waiting for transfers between devices, to_owner(): return lax.ppermute(value, AXES, pairs)  6.63 us
    ppermute x3, starting transfers between devices, from_owner(): return lax.ppermute(value, AXES, pairs)  2.7 us
  transfers between devices with their start and end apart: 19, of which 7 were waited for; matrix products, arithmetic and copies ran while one was open for 0% of the time, Pallas kernels for 13%

profile of v5, /device:TPU:0, one launch (start us, length us, event | category | flops | bytes accessed | tf_op | source)
XLA Modules:
  0.0 76.9 jit_solution(9666289870891810781)
XLA Ops:
  0.6 2.5 %split0.1 = (bf16[4,96,1792]{2,1,0:T(8,128)(2,1)S(1)}, bf16[4,96,1792]{2,1,0:T(8,128)(2,1)S(1)}) custom-call(bf16[720,3584]{1,0:T(8,128)(2,1)} %bitcast.11), custom_call_target="tpu_custom_call" | custom-call | flops 1 | bytes 1 | tf_op jit(solution)/shard_map/split0/pallas_call | solution.py:52
  3.7 2.5 %split1792.1 = (bf16[4,96,1792]{2,1,0:T(8,128)(2,1)S(1)}, bf16[4,96,1792]{2,1,0:T(8,128)(2,1)S(1)}) custom-call(bf16[720,3584]{1,0:T(8,128)(2,1)} %bitcast.12, bf16[4,96,1792]{2,1,0:T(8,128)(2,1)S(1)} %get-tuple-element.23.refs_1_.refs_0_.refs_2_), custom_call_target="tpu_custom_call" | custom-call | flops 1 | bytes 1 | tf_op jit(solution)/shard_map/split1792/pallas_call | solution.py:52
  6.6 3.0 %collective-permute-start.2 = (bf16[2,96,896]{2,1,0:T(8,128)(2,1)S(1)}, bf16[2,96,896]{2,1,0:T(8,128)(2,1)S(1)}, u32[]{:S(2)}, u32[]{:S(2)}) collective-permute-start(bf16[2,96,896]{2,1,0:T(8,128)(2,1)S(1)} %get-tuple-element.27), channel_id=1, source_target_pairs={{0,4},{1,3},{2,6},{3,1},{4,0},{5,7},{6,2},{7,5},{8,12},{9,11},{10,... | collective-permute-start | bytes 1032200 | tf_op jit(solution)/shard_map/ppermute | solution.py:377
  9.5 1.5 %collective-permute-start.1 = (bf16[2,96,896]{2,1,0:T(8,128)(2,1)S(1)}, bf16[2,96,896]{2,1,0:T(8,128)(2,1)S(1)}, u32[]{:S(2)}, u32[]{:S(2)}) collective-permute-start(bf16[2,96,896]{2,1,0:T(8,128)(2,1)S(1)} %get-tuple-element.26.refs_2_), channel_id=1, source_target_pairs={{0,2},{1,5},{2,0},{3,7},{4,6},{5,1},{6,4},{7,3},{8,10},{9,13},{10,... | collective-permute-start | bytes 1032200 | tf_op jit(solution)/shard_map/ppermute | solution.py:377
  11.2 1.0 %collective-permute-start.7 = (bf16[2,96,896]{2,1,0:T(8,128)(2,1)S(1)}, bf16[2,96,896]{2,1,0:T(8,128)(2,1)S(1)}, u32[]{:S(2)}, u32[]{:S(2)}) collective-permute-start(bf16[2,96,896]{2,1,0:T(8,128)(2,1)S(1)} %get-tuple-element.32), channel_id=1, source_target_pairs={{0,4},{1,3},{2,6},{3,1},{4,0},{5,7},{6,2},{7,5},{8,12},{9,11},{10,... | collective-permute-start | bytes 1032200 | tf_op jit(solution)/shard_map/ppermute | solution.py:377
  12.2 1.5 %collective-permute-start.6 = (bf16[2,96,896]{2,1,0:T(8,128)(2,1)S(1)}, bf16[2,96,896]{2,1,0:T(8,128)(2,1)S(1)}, u32[]{:S(2)}, u32[]{:S(2)}) collective-permute-start(bf16[2,96,896]{2,1,0:T(8,128)(2,1)S(1)} %get-tuple-element.29.refs_4_), channel_id=1, source_target_pairs={{0,2},{1,5},{2,0},{3,7},{4,6},{5,1},{6,4},{7,3},{8,10},{9,13},{10,... | collective-permute-start | bytes 1032200 | tf_op jit(solution)/shard_map/ppermute | solution.py:377
  13.7 4.0 %collective-permute-done.2.refs_3_.refs_5_ = bf16[2,96,896]{2,1,0:T(8,128)(2,1)S(1)} collective-permute-done((bf16[2,96,896]{2,1,0:T(8,128)(2,1)S(1)}, bf16[2,96,896]{2,1,0:T(8,128)(2,1)S(1)}, u32[]{:S(2)}, u32[]{:S(2)}) %collective-permute-start.2) | collective-permute-done | bytes 344096 | tf_op jit(solution)/shard_map/ppermute | solution.py:377
  17.7 2.8 %collective-permute-done.1.refs_2_.refs_4_ = bf16[2,96,896]{2,1,0:T(8,128)(2,1)S(1)} collective-permute-done((bf16[2,96,896]{2,1,0:T(8,128)(2,1)S(1)}, bf16[2,96,896]{2,1,0:T(8,128)(2,1)S(1)}, u32[]{:S(2)}, u32[]{:S(2)}) %collective-permute-start.1) | collective-permute-done | bytes 344096 | tf_op jit(solution)/shard_map/ppermute | solution.py:377
  20.7 1.6 %collective-permute-start.5 = (bf16[1,96,896]{2,1,0:T(8,128)(2,1)S(1)}, bf16[1,96,896]{2,1,0:T(8,128)(2,1)S(1)}, u32[]{:S(2)}, u32[]{:S(2)}) collective-permute-start(bf16[1,96,896]{2,1,0:T(8,128)(2,1)S(1)} %get-tuple-element.31), channel_id=1, source_target_pairs={{0,2},{1,5},{2,0},{3,7},{4,6},{5,1},{6,4},{7,3},{8,10},{9,13},{10,... | collective-permute-start | bytes 516104 | tf_op jit(solution)/shard_map/ppermute | solution.py:377
  22.7 2.3 %collective-permute-done.7.refs_3_.refs_5_ = bf16[2,96,896]{2,1,0:T(8,128)(2,1)S(1)} collective-permute-done((bf16[2,96,896]{2,1,0:T(8,128)(2,1)S(1)}, bf16[2,96,896]{2,1,0:T(8,128)(2,1)S(1)}, u32[]{:S(2)}, u32[]{:S(2)}) %collective-permute-start.7) | collective-permute-done | bytes 344096 | tf_op jit(solution)/shard_map/ppermute | solution.py:377
  25.1 2.0 %collective-permute-done.6.refs_2_.refs_4_ = bf16[2,96,896]{2,1,0:T(8,128)(2,1)S(1)} collective-permute-done((bf16[2,96,896]{2,1,0:T(8,128)(2,1)S(1)}, bf16[2,96,896]{2,1,0:T(8,128)(2,1)S(1)}, u32[]{:S(2)}, u32[]{:S(2)}) %collective-permute-start.6) | collective-permute-done | bytes 344096 | tf_op jit(solution)/shard_map/ppermute | solution.py:377
  27.2 1.9 %collective-permute-start.9 = (bf16[1,96,896]{2,1,0:T(8,128)(2,1)S(1)}, bf16[1,96,896]{2,1,0:T(8,128)(2,1)S(1)}, u32[]{:S(2)}, u32[]{:S(2)}) collective-permute-start(bf16[1,96,896]{2,1,0:T(8,128)(2,1)S(1)} %get-tuple-element.35), channel_id=1, source_target_pairs={{0,2},{1,5},{2,0},{3,7},{4,6},{5,1},{6,4},{7,3},{8,10},{9,13},{10,... | collective-permute-start | bytes 516104 | tf_op jit(solution)/shard_map/ppermute | solution.py:377
  29.0 1.1 %collective-permute-start.8 = (bf16[1,96,896]{2,1,0:T(8,128)(2,1)S(1)}, bf16[1,96,896]{2,1,0:T(8,128)(2,1)S(1)}, u32[]{:S(2)}, u32[]{:S(2)}) collective-permute-start(bf16[1,96,896]{2,1,0:T(8,128)(2,1)S(1)} %get-tuple-element.33.refs_8_), channel_id=1, source_target_pairs={{0,4},{1,3},{2,6},{3,1},{4,0},{5,7},{6,2},{7,5},{8,12},{9,11},{10,... | collective-permute-start | bytes 516104 | tf_op jit(solution)/shard_map/ppermute | solution.py:377
  31.7 4.1 %collective-permute-start.11 = (bf16[96,1792]{1,0:T(8,128)(2,1)S(1)}, bf16[96,1792]{1,0:T(8,128)(2,1)S(1)}, u32[]{:S(2)}, u32[]{:S(2)}) collective-permute-start(bf16[96,1792]{1,0:T(8,128)(2,1)S(1)} %get-tuple-element.36.refs_8_.refs_0_), channel_id=1, source_target_pairs={{0,8},{9,17},{2,10},{11,19},{4,12},{13,21},{6,14},{15,23}} | collective-permute-start | bytes 1032200 | tf_op jit(solution)/shard_map/ppermute | solution.py:387
  38.1 2.5 %collective-permute-start.14 = (bf16[96,1792]{1,0:T(8,128)(2,1)S(1)}, bf16[96,1792]{1,0:T(8,128)(2,1)S(1)}, u32[]{:S(2)}, u32[]{:S(2)}) collective-permute-start(bf16[96,1792]{1,0:T(8,128)(2,1)S(1)} %get-tuple-element.38.refs_4_.refs_1_), channel_id=1, source_target_pairs={{0,8},{9,17},{2,10},{11,19},{4,12},{13,21},{6,14},{15,23}} | collective-permute-start | bytes 1032200 | tf_op jit(solution)/shard_map/ppermute | solution.py:387
  41.3 1.8 %keep.1.refs_4_ = f32[2520,128]{1,0:T(8,128)} custom-call(s32[1,5]{1,0:T(1,128)S(1)} %copy-done.1, f32[2520,128]{1,0:T(8,128)S(1)} %bitcast.10, f32[96,1792]{1,0:T(8,128)S(1)} %get-tuple-element.34.refs_2_, f32[96,1792]{1,0:T(8,128)S(1)} %get-tuple-element.37.refs_3_, bf16[96,1792]{1,0:T(8,128)(2,1)S(1)} %get-tuple-element.38.refs_4_.refs_1_), custom_call_target="tpu_custom_call" | custom-call | flops 1 | bytes 1 | tf_op jit(solution)/shard_map/keep/pallas_call | solution.py:52
  44.0 6.6 %collective-permute-done.14.refs_3_ = bf16[96,1792]{1,0:T(8,128)(2,1)S(1)} collective-permute-done((bf16[96,1792]{1,0:T(8,128)(2,1)S(1)}, bf16[96,1792]{1,0:T(8,128)(2,1)S(1)}, u32[]{:S(2)}, u32[]{:S(2)}) %collective-permute-start.14) | collective-permute-done | bytes 344096 | tf_op jit(solution)/shard_map/ppermute | solution.py:387
  50.6 4.2 %chain.1 = (bf16[384,1792]{1,0:T(8,128)(2,1)S(1)}, bf16[4,192,384]{2,1,0:T(8,128)(2,1)S(1)}, f32[8,128]{1,0:T(8,128)S(1)}) custom-call(f32[384,384]{1,0:T(8,128)S(1)} %get-tuple-element.39.refs_0_, bf16[96,1792]{1,0:T(8,128)(2,1)S(1)} %get-tuple-element.38.refs_4_.refs_1_, bf16[96,1792]{1,0:T(8,128)(2,1)S(1)} %collective-permute-done.13.refs_2_, ...), custom_call_target="tpu_custom_call" | custom-call | flops 1 | bytes 1 | tf_op jit(solution)/shard_map/chain/pallas_call | solution.py:52
  54.7 1.0 %rows2.1.refs_4_ = bf16[96,3584]{1,0:T(8,128)(2,1)S(1)} custom-call(bf16[4,192,384]{2,1,0:T(8,128)(2,1)S(1)} %get-tuple-element.40.refs_0_, f32[8,128]{1,0:T(8,128)S(1)} %get-tuple-element.41.refs_1_, bf16[384,1792]{1,0:T(8,128)(2,1)S(1)} %get-tuple-element.42.refs_2_, bf16[384,1792]{1,0:T(8,128)(2,1)S(1)} %get-tuple-element.43.refs_3_), custom_call_target="tpu_custom_call" | custom-call | flops 1 | bytes 1 | tf_op jit(solution)/shard_map/rows2/pallas_call | solution.py:52
  55.7 1.3 %collective-permute-start.16 = (bf16[96,3584]{1,0:T(8,128)(2,1)S(1)}, bf16[96,3584]{1,0:T(8,128)(2,1)S(1)}, u32[]{:S(2)}, u32[]{:S(2)}) collective-permute-start(bf16[96,3584]{1,0:T(8,128)(2,1)S(1)} %rows2.1.refs_4_), channel_id=1, source_target_pairs={{8,0},{17,1},{10,2},{19,3},{12,4},{21,5},{14,6},{23,7}} | collective-permute-start | bytes 2064392 | tf_op jit(solution)/shard_map/ppermute | solution.py:391
  57.0 1.0 %rows1.1.refs_4_ = bf16[96,3584]{1,0:T(8,128)(2,1)S(1)} custom-call(bf16[4,192,384]{2,1,0:T(8,128)(2,1)S(1)} %get-tuple-element.40.refs_0_, f32[8,128]{1,0:T(8,128)S(1)} %get-tuple-element.41.refs_1_, bf16[384,1792]{1,0:T(8,128)(2,1)S(1)} %get-tuple-element.42.refs_2_, bf16[384,1792]{1,0:T(8,128)(2,1)S(1)} %get-tuple-element.43.refs_3_, ...), custom_call_target="tpu_custom_call" | custom-call | flops 1 | bytes 1 | tf_op jit(solution)/shard_map/rows1/pallas_call | solution.py:52
  60.4 1.0 %rows0.1.refs_0_ = bf16[96,3584]{1,0:T(8,128)(2,1)S(1)} custom-call(bf16[4,192,384]{2,1,0:T(8,128)(2,1)S(1)} %get-tuple-element.40.refs_0_, f32[8,128]{1,0:T(8,128)S(1)} %get-tuple-element.41.refs_1_, bf16[384,1792]{1,0:T(8,128)(2,1)S(1)} %get-tuple-element.42.refs_2_, bf16[384,1792]{1,0:T(8,128)(2,1)S(1)} %get-tuple-element.43.refs_3_, ...), custom_call_target="tpu_custom_call" | custom-call | flops 1 | bytes 1 | tf_op jit(solution)/shard_map/rows0/pallas_call | solution.py:52
  61.4 14.6 %collective-permute-done.16.refs_0_.refs_1_ = bf16[96,3584]{1,0:T(8,128)(2,1)S(1)} collective-permute-done((bf16[96,3584]{1,0:T(8,128)(2,1)S(1)}, bf16[96,3584]{1,0:T(8,128)(2,1)S(1)}, u32[]{:S(2)}, u32[]{:S(2)}) %collective-permute-start.16) | collective-permute-done | bytes 688160 | tf_op jit(solution)/shard_map/ppermute | solution.py:391
  75.9 1.0 %last.1 = bf16[90,3584]{1,0:T(8,128)(2,1)} custom-call(bf16[96,3584]{1,0:T(8,128)(2,1)S(1)} %rows0.1.refs_0_, bf16[96,3584]{1,0:T(8,128)(2,1)S(1)} %collective-permute-done.16.refs_0_.refs_1_, bf16[96,3584]{1,0:T(8,128)(2,1)S(1)} %collective-permute-done.17.refs_0_.refs_2_, bf16[96,3584]{1,0:T(8,128)(2,1)S(1)} %collective-permute-done.18.refs_3_, ...), custom_call_target="tpu_custom_call" | custom-call | flops 1 | bytes 1 | tf_op jit(solution)/shard_map/last/pallas_call | solution.py:52
  (36 shorter events, 9.5 us)
Async XLA Ops:
  3.1 3.3 %collective-permute-start = (bf16[4,96,1792]{2,1,0:T(8,128)(2,1)S(1)}, bf16[4,96,1792]{2,1,0:T(8,128)(2,1)S(1)}, u32[]{:S(2)}, u32[]{:S(2)}) collective-permute-start(bf16[4,96,1792]{2,1,0:T(8,128)(2,1)S(1)} %get-tuple-element.24), channel_id=1, source_target_pairs={{0,1},{1,0},{2,3},{3,2},{4,5},{5,4},{6,7},{7,6},{8,9},{9,8},{10,11... | collective-permute-start | bytes 4128776 | tf_op jit(solution)/shard_map/ppermute | solution.py:377
  6.2 4.9 %collective-permute-start.3 = (bf16[4,96,1792]{2,1,0:T(8,128)(2,1)S(1)}, bf16[4,96,1792]{2,1,0:T(8,128)(2,1)S(1)}, u32[]{:S(2)}, u32[]{:S(2)}) collective-permute-start(bf16[4,96,1792]{2,1,0:T(8,128)(2,1)S(1)} %get-tuple-element.28), channel_id=1, source_target_pairs={{0,1},{1,0},{2,3},{3,2},{4,5},{5,4},{6,7},{7,6},{8,9},{9,8},{10,11... | collective-permute-start | bytes 4128776 | tf_op jit(solution)/shard_map/ppermute | solution.py:377
  6.6 11.1 %collective-permute-start.2 = (bf16[2,96,896]{2,1,0:T(8,128)(2,1)S(1)}, bf16[2,96,896]{2,1,0:T(8,128)(2,1)S(1)}, u32[]{:S(2)}, u32[]{:S(2)}) collective-permute-start(bf16[2,96,896]{2,1,0:T(8,128)(2,1)S(1)} %get-tuple-element.27), channel_id=1, source_target_pairs={{0,4},{1,3},{2,6},{3,1},{4,0},{5,7},{6,2},{7,5},{8,12},{9,11},{10,... | collective-permute-start | bytes 1032200 | tf_op jit(solution)/shard_map/ppermute | solution.py:377
  9.5 11.0 %collective-permute-start.1 = (bf16[2,96,896]{2,1,0:T(8,128)(2,1)S(1)}, bf16[2,96,896]{2,1,0:T(8,128)(2,1)S(1)}, u32[]{:S(2)}, u32[]{:S(2)}) collective-permute-start(bf16[2,96,896]{2,1,0:T(8,128)(2,1)S(1)} %get-tuple-element.26.refs_2_), channel_id=1, source_target_pairs={{0,2},{1,5},{2,0},{3,7},{4,6},{5,1},{6,4},{7,3},{8,10},{9,13},{10,... | collective-permute-start | bytes 1032200 | tf_op jit(solution)/shard_map/ppermute | solution.py:377
  11.2 13.8 %collective-permute-start.7 = (bf16[2,96,896]{2,1,0:T(8,128)(2,1)S(1)}, bf16[2,96,896]{2,1,0:T(8,128)(2,1)S(1)}, u32[]{:S(2)}, u32[]{:S(2)}) collective-permute-start(bf16[2,96,896]{2,1,0:T(8,128)(2,1)S(1)} %get-tuple-element.32), channel_id=1, source_target_pairs={{0,4},{1,3},{2,6},{3,1},{4,0},{5,7},{6,2},{7,5},{8,12},{9,11},{10,... | collective-permute-start | bytes 1032200 | tf_op jit(solution)/shard_map/ppermute | solution.py:377
  12.2 14.8 %collective-permute-start.6 = (bf16[2,96,896]{2,1,0:T(8,128)(2,1)S(1)}, bf16[2,96,896]{2,1,0:T(8,128)(2,1)S(1)}, u32[]{:S(2)}, u32[]{:S(2)}) collective-permute-start(bf16[2,96,896]{2,1,0:T(8,128)(2,1)S(1)} %get-tuple-element.29.refs_4_), channel_id=1, source_target_pairs={{0,2},{1,5},{2,0},{3,7},{4,6},{5,1},{6,4},{7,3},{8,10},{9,13},{10,... | collective-permute-start | bytes 1032200 | tf_op jit(solution)/shard_map/ppermute | solution.py:377
  20.7 9.4 %collective-permute-start.5 = (bf16[1,96,896]{2,1,0:T(8,128)(2,1)S(1)}, bf16[1,96,896]{2,1,0:T(8,128)(2,1)S(1)}, u32[]{:S(2)}, u32[]{:S(2)}) collective-permute-start(bf16[1,96,896]{2,1,0:T(8,128)(2,1)S(1)} %get-tuple-element.31), channel_id=1, source_target_pairs={{0,2},{1,5},{2,0},{3,7},{4,6},{5,1},{6,4},{7,3},{8,10},{9,13},{10,... | collective-permute-start | bytes 516104 | tf_op jit(solution)/shard_map/ppermute | solution.py:377
  22.3 7.8 %copy-start = (f32[1,90,3584]{2,0,1:T(1,128)S(1)}, f32[1,90,3584]{2,0,1:T(1,128)}, u32[]{:S(2)}) copy-start(f32[1,90,3584]{2,0,1:T(1,128)} %param.4) | copy-start | bytes 3870724
  22.3 7.8 %copy-start.1 = (s32[1,5]{1,0:T(1,128)S(1)}, s32[1,5]{1,0:T(1,128)}, u32[]{:S(2)}) copy-start(s32[1,5]{1,0:T(1,128)} %refs_0_.5) | copy-start | bytes 64
  22.3 7.8 %collective-permute-start.4 = (bf16[1,96,896]{2,1,0:T(8,128)(2,1)S(1)}, bf16[1,96,896]{2,1,0:T(8,128)(2,1)S(1)}, u32[]{:S(2)}, u32[]{:S(2)}) collective-permute-start(bf16[1,96,896]{2,1,0:T(8,128)(2,1)S(1)} %get-tuple-element.30.refs_4_), channel_id=1, source_target_pairs={{0,4},{1,3},{2,6},{3,1},{4,0},{5,7},{6,2},{7,5},{8,12},{9,11},{10,... | collective-permute-start | bytes 516104 | tf_op jit(solution)/shard_map/ppermute | solution.py:377
  27.2 9.3 %collective-permute-start.9 = (bf16[1,96,896]{2,1,0:T(8,128)(2,1)S(1)}, bf16[1,96,896]{2,1,0:T(8,128)(2,1)S(1)}, u32[]{:S(2)}, u32[]{:S(2)}) collective-permute-start(bf16[1,96,896]{2,1,0:T(8,128)(2,1)S(1)} %get-tuple-element.35), channel_id=1, source_target_pairs={{0,2},{1,5},{2,0},{3,7},{4,6},{5,1},{6,4},{7,3},{8,10},{9,13},{10,... | collective-permute-start | bytes 516104 | tf_op jit(solution)/shard_map/ppermute | solution.py:377
  29.0 7.5 %collective-permute-start.8 = (bf16[1,96,896]{2,1,0:T(8,128)(2,1)S(1)}, bf16[1,96,896]{2,1,0:T(8,128)(2,1)S(1)}, u32[]{:S(2)}, u32[]{:S(2)}) collective-permute-start(bf16[1,96,896]{2,1,0:T(8,128)(2,1)S(1)} %get-tuple-element.33.refs_8_), channel_id=1, source_target_pairs={{0,4},{1,3},{2,6},{3,1},{4,0},{5,7},{6,2},{7,5},{8,12},{9,11},{10,... | collective-permute-start | bytes 516104 | tf_op jit(solution)/shard_map/ppermute | solution.py:377
  31.0 9.6 %collective-permute-start.12 = (bf16[96,1792]{1,0:T(8,128)(2,1)S(1)}, bf16[96,1792]{1,0:T(8,128)(2,1)S(1)}, u32[]{:S(2)}, u32[]{:S(2)}) collective-permute-start(bf16[96,1792]{1,0:T(8,128)(2,1)S(1)} %get-tuple-element.36.refs_8_.refs_0_), channel_id=1, source_target_pairs={{16,8},{25,17},{18,10},{27,19},{20,12},{29,21},{22,14},{31,23}} | collective-permute-start | bytes 1032200 | tf_op jit(solution)/shard_map/ppermute | solution.py:387
  31.7 11.5 %collective-permute-start.11 = (bf16[96,1792]{1,0:T(8,128)(2,1)S(1)}, bf16[96,1792]{1,0:T(8,128)(2,1)S(1)}, u32[]{:S(2)}, u32[]{:S(2)}) collective-permute-start(bf16[96,1792]{1,0:T(8,128)(2,1)S(1)} %get-tuple-element.36.refs_8_.refs_0_), channel_id=1, source_target_pairs={{0,8},{9,17},{2,10},{11,19},{4,12},{13,21},{6,14},{15,23}} | collective-permute-start | bytes 1032200 | tf_op jit(solution)/shard_map/ppermute | solution.py:387
  35.8 7.4 %collective-permute-start.10 = (bf16[96,1792]{1,0:T(8,128)(2,1)S(1)}, bf16[96,1792]{1,0:T(8,128)(2,1)S(1)}, u32[]{:S(2)}, u32[]{:S(2)}) collective-permute-start(bf16[96,1792]{1,0:T(8,128)(2,1)S(1)} %get-tuple-element.36.refs_8_.refs_0_), channel_id=1, source_target_pairs={{24,8},{1,17},{26,10},{3,19},{28,12},{5,21},{30,14},{7,23}} | collective-permute-start | bytes 1032200 | tf_op jit(solution)/shard_map/ppermute | solution.py:387
  37.4 6.5 %collective-permute-start.15 = (bf16[96,1792]{1,0:T(8,128)(2,1)S(1)}, bf16[96,1792]{1,0:T(8,128)(2,1)S(1)}, u32[]{:S(2)}, u32[]{:S(2)}) collective-permute-start(bf16[96,1792]{1,0:T(8,128)(2,1)S(1)} %get-tuple-element.38.refs_4_.refs_1_), channel_id=1, source_target_pairs={{16,8},{25,17},{18,10},{27,19},{20,12},{29,21},{22,14},{31,23}} | collective-permute-start | bytes 1032200 | tf_op jit(solution)/shard_map/ppermute | solution.py:387
  38.1 12.5 %collective-permute-start.14 = (bf16[96,1792]{1,0:T(8,128)(2,1)S(1)}, bf16[96,1792]{1,0:T(8,128)(2,1)S(1)}, u32[]{:S(2)}, u32[]{:S(2)}) collective-permute-start(bf16[96,1792]{1,0:T(8,128)(2,1)S(1)} %get-tuple-element.38.refs_4_.refs_1_), channel_id=1, source_target_pairs={{0,8},{9,17},{2,10},{11,19},{4,12},{13,21},{6,14},{15,23}} | collective-permute-start | bytes 1032200 | tf_op jit(solution)/shard_map/ppermute | solution.py:387
  40.6 9.9 %collective-permute-start.13 = (bf16[96,1792]{1,0:T(8,128)(2,1)S(1)}, bf16[96,1792]{1,0:T(8,128)(2,1)S(1)}, u32[]{:S(2)}, u32[]{:S(2)}) collective-permute-start(bf16[96,1792]{1,0:T(8,128)(2,1)S(1)} %get-tuple-element.38.refs_4_.refs_1_), channel_id=1, source_target_pairs={{24,8},{1,17},{26,10},{3,19},{28,12},{5,21},{30,14},{7,23}} | collective-permute-start | bytes 1032200 | tf_op jit(solution)/shard_map/ppermute | solution.py:387
  55.7 20.2 %collective-permute-start.16 = (bf16[96,3584]{1,0:T(8,128)(2,1)S(1)}, bf16[96,3584]{1,0:T(8,128)(2,1)S(1)}, u32[]{:S(2)}, u32[]{:S(2)}) collective-permute-start(bf16[96,3584]{1,0:T(8,128)(2,1)S(1)} %rows2.1.refs_4_), channel_id=1, source_target_pairs={{8,0},{17,1},{10,2},{19,3},{12,4},{21,5},{14,6},{23,7}} | collective-permute-start | bytes 2064392 | tf_op jit(solution)/shard_map/ppermute | solution.py:391
  58.0 17.9 %collective-permute-start.17 = (bf16[96,3584]{1,0:T(8,128)(2,1)S(1)}, bf16[96,3584]{1,0:T(8,128)(2,1)S(1)}, u32[]{:S(2)}, u32[]{:S(2)}) collective-permute-start(bf16[96,3584]{1,0:T(8,128)(2,1)S(1)} %rows1.1.refs_4_), channel_id=1, source_target_pairs={{8,24},{17,9},{10,26},{19,11},{12,28},{21,13},{14,30},{23,15}} | collective-permute-start | bytes 2064392 | tf_op jit(solution)/shard_map/ppermute | solution.py:391
  59.7 16.3 %collective-permute-start.18 = (bf16[96,3584]{1,0:T(8,128)(2,1)S(1)}, bf16[96,3584]{1,0:T(8,128)(2,1)S(1)}, u32[]{:S(2)}, u32[]{:S(2)}) collective-permute-start(bf16[96,3584]{1,0:T(8,128)(2,1)S(1)} %rows3.1.refs_4_), channel_id=1, source_target_pairs={{8,16},{17,25},{10,18},{19,27},{12,20},{21,29},{14,22},{23,31}} | collective-permute-start | bytes 2064392 | tf_op jit(solution)/shard_map/ppermute | solution.py:391
